TPU v7x, 512 devices: a whole 4x4x16 slice. The times are simulated.
512 devices in a mesh: samp: 64 (over y, z_lo, core), feat: 8 (over z_hi, x).
Axes of the slice: x: 4, y: 4, z: 16 (z_hi: 2, z_lo: 8; z = z_hi * 8 + z_lo), core: 2. Of those that a mesh axis runs over, the one named last changes fastest.
Arguments:
- grads: bfloat16 [32768, 4096], P('samp', 'feat'), may hold values from -60 to 60
- weights: float32 [32768], P('samp'), may hold values from 0.05 to 6
- targets: float32 [4096, 64], P('feat'), may hold values from -6 to 6
Outputs:
- scores: float32 [32768, 64], P(('samp', 'feat'))
- solution: float32 [4096, 64], P('feat')
- residual: float32 [4096, 64], P('feat')
All inputs are finite; a program needn't handle non-finite values.
Results may differ from a plain program's by a relative error of at most 0.014.
Values may be sent and summed in bfloat16 or wider, within the bound.
No kernel may reach another device: no remote copies, remote signals or barrier semaphores. Data moves between devices by JAX's collectives and lax.ppermute only.
A program may use at most 64 MiB of HBM per device.

v0:
```python
import math

import jax
import jax.numpy as jnp
from jax import lax
from jax.sharding import PartitionSpec as P

ITERS = 2


damping_term = 0.1


def copy_for_each(x, axis):
    devices = lax.axis_size(axis)
    return lax.all_to_all(jnp.broadcast_to(x[None], (devices, *x.shape)), axis, 0, 0, tiled=True)


def of_everyone(x, axis):
    return copy_for_each(x, axis).astype(jnp.float32).sum(axis=0)


def rows_for(lines, devices):
    spare = -len(lines) % devices
    return jnp.pad(lines, [(0, spare)] + [(0, 0)] * (lines.ndim - 1))


def laid_out(pieces, dim):
    lengths = list(pieces.shape[1:])
    lengths[dim] *= pieces.shape[0]
    return jnp.moveaxis(pieces, 0, dim).reshape(lengths)


def gathered_copies(x, axis, dim):
    pieces = copy_for_each(x, axis)
    return laid_out(pieces, dim)


def split_up(x, dim, devices):
    lengths = x.shape
    pieces = x.reshape(*lengths[:dim], devices, lengths[dim] // devices, *lengths[dim + 1 :])
    return jnp.moveaxis(pieces, dim, 0)


def sent_and_summed(x, axis, dim):
    pieces = split_up(x, dim, lax.axis_size(axis))
    arrived = lax.all_to_all(pieces, axis, split_axis=0, concat_axis=0, tiled=True)
    return arrived.astype(jnp.float32).sum(axis=0)


def nested_sum(x, axes):
    lines = x.reshape(-1, x.shape[-1])
    padded = rows_for(lines, lax.axis_size(axes))
    whole = gathered_copies(sent_and_summed(padded, axes, 0).astype(jnp.bfloat16), axes, 0)
    return lax.slice_in_dim(whole, 0, len(lines)).reshape(x.shape).astype(jnp.float32)


def over_copies(x, axis):
    everything = copy_for_each(x, axis)
    return jnp.sum(everything, axis=0)


def per_device(grads, weights, targets):
    rows_dev, feat_cols = grads.shape
    n_samp = lax.axis_size("samp")
    n_feat = lax.axis_size("feat")
    total = rows_dev * n_samp
    full_width = feat_cols * n_feat
    share = rows_dev // n_feat
    offset = lax.axis_index("feat") * share
    scaled = weights / total

    def column_norms(resid):
        squares = jnp.sum(resid * resid, axis=0)
        parts = (squares,)
        return (over_copies(parts[0], "feat"),)

    solution = jnp.zeros_like(targets)
    resid = targets
    direction = targets
    accum = jnp.zeros((share, targets.shape[1]), jnp.float32)
    norm_now = column_norms(resid)[0]
    for step in range(ITERS):
        packed = direction.astype(jnp.bfloat16)
        local_rows = jnp.dot(grads, packed, preferred_element_type=jnp.float32)
        sample_rows = of_everyone(local_rows.astype(jnp.bfloat16), "feat").astype(jnp.float32)
        weighted = (sample_rows * scaled[:, None]).astype(jnp.bfloat16)
        partial_image = lax.dot_general(
            grads, weighted, (((0,), (0,)), ((), ())), preferred_element_type=jnp.float32
        )
        own_rows = lax.dynamic_slice_in_dim(sample_rows, offset, share, 0)
        own_weights = lax.dynamic_slice_in_dim(scaled, offset, share, 0)
        apply_own_rows = own_rows
        apply_own_weights = own_weights
        image = nested_sum(partial_image.astype(jnp.bfloat16), "samp") + damping_term * direction
        own_rows, own_weights, image = (apply_own_rows, apply_own_weights, image)
        curvature = over_copies(jnp.sum(direction * image, axis=0), "feat")
        alpha = norm_now / curvature
        solution = solution + alpha * direction
        resid = resid - alpha * image
        accum = accum + alpha * own_rows
        if step + 1 < ITERS:
            sums = column_norms(resid)
            norm_next = sums[0]
            ratio = norm_next / norm_now
            direction = resid + ratio * direction
            norm_now = norm_next
    scores = accum / math.sqrt(full_width)
    return (scores, solution, resid)


def solution(mesh):
    return jax.shard_map(
        per_device,
        mesh=mesh,
        in_specs=(P("samp", "feat"), P("samp"), P("feat", None)),
        out_specs=(P(("samp", "feat"), None), P("feat", None), P("feat", None)),
        check_vma=False,
    )
```

profile of v0, /device:TPU:1, one launch (start us, length us, event | category | flops | bytes accessed | tf_op | source)
XLA Modules:
  0.0 243.5 jit_solution(2003193492615021404)
XLA Ops:
  0.6 0.0 copy-start
  0.6 1.0 copy-done
  1.7 1.2 convolution_convert_fusion.3
  2.9 0.8 broadcast_in_dim.17
  3.7 0.0 copy-start.2
  3.7 18.2 %all-to-all-start.1 = ((bf16[8,512,64]{1,2,0:T(8,128)(2,1)}), bf16[8,512,64]{1,2,0:T(8,128)(2,1)S(1)}, u32[]{:S(2)}, u32[]{:S(2)}) async-start(bf16[8,512,64]{1,2,0:T(8,128)(2,1)} %broadcast_in_dim.17), calls=%async_computation.1 | async-start | bytes 1048576 | tf_op jit(solution)/shard_map/all_to_all | solution.py:16
  21.9 0.0 copy-done.2
  21.9 17.1 %all-to-all-done.1 = bf16[8,512,64]{1,2,0:T(8,128)(2,1)S(1)} async-done(((bf16[8,512,64]{1,2,0:T(8,128)(2,1)}), bf16[8,512,64]{1,2,0:T(8,128)(2,1)S(1)}, u32[]{:S(2)}, u32[]{:S(2)}) %all-to-all-start.1) | async-done | bytes 524320 | tf_op jit(solution)/shard_map/all_to_all | solution.py:16
  39.0 0.1 convert_reduce_fusion.1
  39.1 0.2 fusion.1
  39.3 0.1 copy.49
  39.4 0.2 reshape.66
  39.6 39.2 %all_to_all.54 = bf16[64,2,256]{2,1,0:T(2,128)(2,1)S(1)} all-to-all(bf16[64,2,256]{2,1,0:T(2,128)(2,1)S(1)} %reshape.66), channel_id=1, replica_groups=mesh['samp'=64,'feat'=8] {'samp'}, dimensions={0} | all-to-all | bytes 131072 | tf_op jit(solution)/shard_map/all_to_all | solution.py:47
  78.8 0.1 reshape.67
  78.9 0.1 reduce_sum.117
  79.0 0.0 copy-start.1
  79.0 0.8 reshape.68
  79.8 5.0 %all-to-all-start.3 = ((bf16[64,2,256]{2,1,0:T(2,128)(2,1)}), bf16[64,2,256]{2,1,0:T(2,128)(2,1)S(1)}, u32[]{:S(2)}, u32[]{:S(2)}) async-start(bf16[64,2,256]{2,1,0:T(2,128)(2,1)} %reshape.68), calls=%async_computation.3 | async-start | bytes 131072 | tf_op jit(solution)/shard_map/all_to_all | solution.py:16
  84.9 0.0 copy-done.1
  84.9 0.1 copy.51
  85.0 0.1 multiply_reduce_fusion.3
  85.1 12.6 %all-to-all-done.3 = bf16[64,2,256]{2,1,0:T(2,128)(2,1)S(1)} async-done(((bf16[64,2,256]{2,1,0:T(2,128)(2,1)}), bf16[64,2,256]{2,1,0:T(2,128)(2,1)S(1)}, u32[]{:S(2)}, u32[]{:S(2)}) %all-to-all-start.3) | async-done | bytes 65568 | tf_op jit(solution)/shard_map/all_to_all | solution.py:16
  97.7 0.6 broadcast_in_dim.16
  98.3 3.3 %all-to-all-start = ((f32[8,1,64]{2,1,0:T(1,128)}), f32[8,1,64]{2,1,0:T(1,128)S(1)}, u32[]{:S(2)}, u32[]{:S(2)}) async-start(f32[8,1,64]{2,1,0:T(1,128)} %broadcast_in_dim.16), calls=%async_computation | async-start | bytes 8192 | tf_op jit(solution)/shard_map/all_to_all | solution.py:16
  101.6 0.1 reshape.69
  101.8 0.1 multiply_reduce_fusion.2
  101.8 13.3 %all-to-all-done = f32[8,1,64]{2,1,0:T(1,128)S(1)} async-done(((f32[8,1,64]{2,1,0:T(1,128)}), f32[8,1,64]{2,1,0:T(1,128)S(1)}, u32[]{:S(2)}, u32[]{:S(2)}) %all-to-all-start) | async-done | bytes 2080 | tf_op jit(solution)/shard_map/all_to_all | solution.py:16
  115.2 0.6 broadcast_in_dim.19
  115.8 3.3 %all-to-all-start.4 = ((f32[8,1,64]{2,1,0:T(1,128)}), f32[8,1,64]{2,1,0:T(1,128)S(1)}, u32[]{:S(2)}, u32[]{:S(2)}) async-start(f32[8,1,64]{2,1,0:T(1,128)} %broadcast_in_dim.19), calls=%async_computation.4 | async-start | bytes 8192 | tf_op jit(solution)/shard_map/all_to_all | solution.py:16
  119.1 13.6 %all-to-all-done.4 = f32[8,1,64]{2,1,0:T(1,128)S(1)} async-done(((f32[8,1,64]{2,1,0:T(1,128)}), f32[8,1,64]{2,1,0:T(1,128)S(1)}, u32[]{:S(2)}, u32[]{:S(2)}) %all-to-all-start.4) | async-done | bytes 2080 | tf_op jit(solution)/shard_map/all_to_all | solution.py:16
  132.7 0.1 multiply_reduce_fusion.1
  132.8 16.1 %all_to_all.55 = f32[8,1,64]{2,1,0:T(1,128)S(1)} all-to-all(f32[8,1,64]{2,1,0:T(1,128)S(1)} %broadcast_in_dim.20), channel_id=1, replica_groups=mesh['samp'=64,'feat'=8] {'feat'}, dimensions={0} | all-to-all | bytes 4096 | tf_op jit(solution)/shard_map/all_to_all | solution.py:16
  148.9 0.3 fusion
  149.3 19.1 %all_to_all.56 = bf16[8,512,64]{1,2,0:T(8,128)(2,1)S(1)} all-to-all(bf16[8,512,64]{1,2,0:T(8,128)(2,1)S(1)} %broadcast_in_dim.21), channel_id=1, replica_groups=mesh['samp'=64,'feat'=8] {'feat'}, dimensions={0} | all-to-all | bytes 1048576 | tf_op jit(solution)/shard_map/all_to_all | solution.py:16
  168.3 0.1 convert_reduce_fusion
  168.4 0.2 fusion.2
  168.6 0.1 copy.56
  168.7 0.2 reshape.70
  168.9 36.3 %all_to_all.57 = bf16[64,2,256]{2,1,0:T(2,128)(2,1)S(1)} all-to-all(bf16[64,2,256]{2,1,0:T(2,128)(2,1)S(1)} %reshape.70), channel_id=1, replica_groups=mesh['samp'=64,'feat'=8] {'samp'}, dimensions={0} | all-to-all | bytes 131072 | tf_op jit(solution)/shard_map/all_to_all | solution.py:47
  205.1 0.1 reshape.71
  205.3 0.1 reduce_sum.123
  205.4 0.2 reshape.72
  205.5 17.7 %all_to_all.58 = bf16[64,2,256]{2,1,0:T(2,128)(2,1)S(1)} all-to-all(bf16[64,2,256]{2,1,0:T(2,128)(2,1)S(1)} %reshape.72), channel_id=1, replica_groups=mesh['samp'=64,'feat'=8] {'samp'}, dimensions={0} | all-to-all | bytes 131072 | tf_op jit(solution)/shard_map/all_to_all | solution.py:16
  223.2 0.1 reshape.73
  223.3 0.1 multiply_reduce_fusion
  223.5 0.6 broadcast_in_dim.23
  224.1 3.3 %all-to-all-start.9 = ((f32[8,1,64]{2,1,0:T(1,128)}), f32[8,1,64]{2,1,0:T(1,128)S(1)}, u32[]{:S(2)}, u32[]{:S(2)}) async-start(f32[8,1,64]{2,1,0:T(1,128)} %broadcast_in_dim.23), calls=%async_computation.9 | async-start | bytes 8192 | tf_op jit(solution)/shard_map/all_to_all | solution.py:16
  227.4 13.6 %all-to-all-done.9 = f32[8,1,64]{2,1,0:T(1,128)S(1)} async-done(((f32[8,1,64]{2,1,0:T(1,128)}), f32[8,1,64]{2,1,0:T(1,128)S(1)}, u32[]{:S(2)}, u32[]{:S(2)}) %all-to-all-start.9) | async-done | bytes 2080 | tf_op jit(solution)/shard_map/all_to_all | solution.py:16
  241.0 0.1 multiply_subtract_fusion
  241.1 0.8 copy.60
  241.9 0.8 copy.61
  242.7 0.1 add_multiply_fusion
  242.8 0.7 copy.59
  (12 shorter events, 0.2 us)
Async XLA Ops:
  0.6 1.0 copy-start
  3.7 18.2 %copy-start.2 = (f32[512]{0:T(512)S(1)}, f32[512]{0:T(512)}, u32[]{:S(2)}) copy-start(f32[512]{0:T(512)} %param.4) | copy-start | bytes 6148
  3.7 35.3 %all-to-all-start.1 = ((bf16[8,512,64]{1,2,0:T(8,128)(2,1)}), bf16[8,512,64]{1,2,0:T(8,128)(2,1)S(1)}, u32[]{:S(2)}, u32[]{:S(2)}) async-start(bf16[8,512,64]{1,2,0:T(8,128)(2,1)} %broadcast_in_dim.17), calls=%async_computation.1 | async-start | bytes 1048576 | tf_op jit(solution)/shard_map/all_to_all | solution.py:16
  79.0 5.8 %copy-start.1 = (f32[512,64]{0,1:T(8,128)S(1)}, f32[512,64]{0,1:T(8,128)}, u32[]{:S(2)}) copy-start(f32[512,64]{0,1:T(8,128)} %param.5) | copy-start | bytes 393220
  79.8 17.9 %all-to-all-start.3 = ((bf16[64,2,256]{2,1,0:T(2,128)(2,1)}), bf16[64,2,256]{2,1,0:T(2,128)(2,1)S(1)}, u32[]{:S(2)}, u32[]{:S(2)}) async-start(bf16[64,2,256]{2,1,0:T(2,128)(2,1)} %reshape.68), calls=%async_computation.3 | async-start | bytes 131072 | tf_op jit(solution)/shard_map/all_to_all | solution.py:16
  98.3 16.9 %all-to-all-start = ((f32[8,1,64]{2,1,0:T(1,128)}), f32[8,1,64]{2,1,0:T(1,128)S(1)}, u32[]{:S(2)}, u32[]{:S(2)}) async-start(f32[8,1,64]{2,1,0:T(1,128)} %broadcast_in_dim.16), calls=%async_computation | async-start | bytes 8192 | tf_op jit(solution)/shard_map/all_to_all | solution.py:16
  115.8 16.9 %all-to-all-start.4 = ((f32[8,1,64]{2,1,0:T(1,128)}), f32[8,1,64]{2,1,0:T(1,128)S(1)}, u32[]{:S(2)}, u32[]{:S(2)}) async-start(f32[8,1,64]{2,1,0:T(1,128)} %broadcast_in_dim.19), calls=%async_computation.4 | async-start | bytes 8192 | tf_op jit(solution)/shard_map/all_to_all | solution.py:16
  224.1 16.9 %all-to-all-start.9 = ((f32[8,1,64]{2,1,0:T(1,128)}), f32[8,1,64]{2,1,0:T(1,128)S(1)}, u32[]{:S(2)}, u32[]{:S(2)}) async-start(f32[8,1,64]{2,1,0:T(1,128)} %broadcast_in_dim.23), calls=%async_computation.9 | async-start | bytes 8192 | tf_op jit(solution)/shard_map/all_to_all | solution.py:16
where the time goes:
time: 244 us; the launch traced here: 243 us
  blocking collectives  128 us (52%)
  waiting for transfers between devices  70.1 us (29%)
  starting transfers between devices  33.2 us (14%)
  local copies, waits for them, and re-layouts  8.18 us (3%)
    all_to_all x2, blocking collectives, sent_and_summed(): lax.all_to_all(pieces, axis, split_axis=0, concat_axis=0, tiled=True)  75.5 us
    all_to_all x5, waiting for transfers between devices, copy_for_each(): lax.all_to_all(jnp.broadcast_to(x[None], (devices, *x.shape)), axis, 0, 0...  70.1 us
    all_to_all x3, blocking collectives, copy_for_each(): lax.all_to_all(jnp.broadcast_to(x[None], (devices, *x.shape)), axis, 0, 0...  52.8 us
    all_to_all x5, starting transfers between devices, copy_for_each(): lax.all_to_all(jnp.broadcast_to(x[None], (devices, *x.shape)), axis, 0, 0...  33.2 us
    unnamed x18, local copies, waits for them, and re-layouts  5.23 us
  transfers between devices with their start and end apart: 5, of which 5 were waited for; matrix products, arithmetic and copies ran while one was open for 0% of the time, Pallas kernels for 0%

commit v1 on v0

v1 whole, which is shorter than its diff:
```python
import math

import jax
import jax.numpy as jnp
from jax import lax
from jax.sharding import PartitionSpec as P

ITERS = 2
DAMPING = 0.1
PLANES, LAYERS, CORES = 4, 8, 2
HALVES, COLUMNS = 2, 4
NEAR = PLANES * CORES
TAIL = 128

X_GROUPS = [[h * COLUMNS + i for i in range(COLUMNS)] for h in range(HALVES)]
SWAP = [(i, (i + COLUMNS) % (HALVES * COLUMNS)) for i in range(HALVES * COLUMNS)]
NEAR_GROUPS = [
    [(y * LAYERS + z) * CORES + c for y in range(PLANES) for c in range(CORES)]
    for z in range(LAYERS)
]
FAR_GROUPS = [
    [(y * LAYERS + z) * CORES + c for z in range(LAYERS)]
    for y in range(PLANES)
    for c in range(CORES)
]


def rounded(x):
    return lax.reduce_precision(x, 8, 7)


def packed(body, scalars):
    high = rounded(scalars)
    middle = rounded(scalars - high)
    low = scalars - high - middle
    tail = jnp.concatenate([high, middle, low], axis=1)
    tail = jnp.pad(tail, [(0, 0), (0, TAIL - tail.shape[1])])
    return jnp.concatenate([body.astype(jnp.bfloat16), tail.astype(jnp.bfloat16)], axis=1)


def unpacked(x, k):
    x = x.astype(jnp.float32)
    body, tail = x[:, :-TAIL], x[:, -TAIL:]
    return body, tail[:, :k] + tail[:, k : 2 * k] + tail[:, 2 * k : 3 * k]


def exchanged(pieces, axis, groups):
    return lax.all_to_all(pieces, axis, 0, 0, tiled=True, axis_index_groups=groups)


def copies(x, n):
    return jnp.broadcast_to(x[None], (n, *x.shape))


def feature_sum(rows, scalars):
    k = scalars.shape[1]
    arrived = exchanged(copies(packed(rows, scalars), COLUMNS), "feat", X_GROUPS)
    body, scal = unpacked(arrived.astype(jnp.float32).sum(axis=0), k)
    mine = packed(body, scal)
    other = lax.ppermute(mine, "feat", SWAP)
    return unpacked(mine.astype(jnp.float32) + other.astype(jnp.float32), k)


def sample_sum(image, scalars):
    k = scalars.shape[1]
    lines = packed(image, scalars)
    pieces = lines.reshape(NEAR, lines.shape[0] // NEAR, lines.shape[1])
    arrived = exchanged(pieces, "samp", NEAR_GROUPS)
    body, scal = unpacked(arrived.astype(jnp.float32).sum(axis=0), k)
    arrived = exchanged(copies(packed(body, scal), LAYERS), "samp", FAR_GROUPS)
    return unpacked(arrived.astype(jnp.float32).sum(axis=0), k)


def gathered(body, scalars):
    k = scalars.shape[1]
    whole = exchanged(copies(packed(body, scalars), NEAR), "samp", NEAR_GROUPS)
    return unpacked(whole.reshape(-1, whole.shape[-1]), k)


def dot(a, b, dims):
    return lax.dot_general(
        a.astype(jnp.bfloat16), b, (dims, ((), ())), preferred_element_type=jnp.float32
    )


def col(x):
    return jnp.sum(x, axis=1, keepdims=True)


def per_device(grads, weights, targets):
    n_samp, n_feat = lax.axis_size("samp"), lax.axis_size("feat")
    total = grads.shape[0] * n_samp
    share = grads.shape[0] // n_feat
    scaled = (weights / total)[None, :]
    me = lax.axis_index("samp")
    near = me // (LAYERS * CORES) * CORES + me % CORES
    lines = targets.shape[1] // NEAR

    def own(x):
        return lax.dynamic_slice_in_dim(x, near * lines, lines, 0)

    base = targets.T
    base_own = own(base)

    rows0, norm0 = feature_sum(dot(base, grads, ((1,), (1,))), col(base * base))
    weighted = rows0 * scaled
    image, curve = sample_sum(dot(weighted, grads, ((1,), (0,))), col(weighted * rows0))
    alpha = own(norm0) / (curve + DAMPING * own(norm0))
    resid_own = base_own - alpha * (image + DAMPING * base_own)
    resid, alpha0 = gathered(resid_own, alpha)

    sums = jnp.concatenate([col(resid * resid), col(resid * base)], axis=1)
    rows1, sums = feature_sum(dot(resid, grads, ((1,), (1,))), sums)
    norm1, cross = sums[:, :1], sums[:, 1:]
    beta = norm1 / norm0
    rows1 = rows1 + beta * rows0
    weighted = rows1 * scaled
    image, curve = sample_sum(dot(weighted, grads, ((1,), (0,))), col(weighted * rows1))
    square = norm1 + 2.0 * beta * cross + beta * beta * norm0
    alpha = own(norm1) / (curve + DAMPING * own(square))
    line_own = resid_own + own(beta) * base_own
    resid_own = resid_own - alpha * (image + DAMPING * line_own)
    last, alpha1 = gathered(resid_own, alpha)

    direction = resid + beta * base
    answer = alpha0 * base + alpha1 * direction
    scores = (alpha0 * rows0 + alpha1 * rows1) / math.sqrt(grads.shape[1] * n_feat)
    scores = lax.dynamic_slice_in_dim(scores.T, lax.axis_index("feat") * share, share, 0)
    return scores, answer.T, last.T


def solution(mesh):
    return jax.shard_map(
        per_device,
        mesh=mesh,
        in_specs=(P("samp", "feat"), P("samp"), P("feat", None)),
        out_specs=(P(("samp", "feat"), None), P("feat", None), P("feat", None)),
        check_vma=False,
    )
```

time: 244 us -> 142 us (0.58)
  blocking collectives: 128 us -> 54.5 us
  waiting for transfers between devices: 70.1 us -> 31.8 us
  starting transfers between devices: 33.2 us -> 44 us
  local copies, waits for them, and re-layouts: 8.18 us -> 4.02 us
  other arithmetic: 1.04 us -> 4.64 us
    all_to_all x5, blocking collectives: 128 us -> 54.5 us  [exchanged(): lax.all_to_all(pieces, axis, 0, 0, tiled=True, axis_index_groups=groups)]
    all_to_all x5 -> x3, waiting for transfers between devices: 70.1 us -> 24.4 us  [exchanged(): lax.all_to_all(pieces, axis, 0, 0, tiled=True, axis_index_groups=groups)]
    ppermute x0 -> x2, starting transfers between devices: none -> 25.2 us  [feature_sum(): other = lax.ppermute(mine, 'feat', SWAP)]
    all_to_all x5 -> x3, starting transfers between devices: 33.2 us -> 18.8 us  [exchanged(): lax.all_to_all(pieces, axis, 0, 0, tiled=True, axis_index_groups=groups)]
    ppermute x0 -> x2, waiting for transfers between devices: none -> 7.35 us  [feature_sum(): other = lax.ppermute(mine, 'feat', SWAP)]
    unnamed x18 -> x15, local copies, waits for them, and re-layouts: 5.23 us -> 1.36 us
where the time goes in v1:
time: 142 us; the launch traced here: 141 us
  blocking collectives  54.5 us (38%)
  starting transfers between devices  44 us (31%)
  waiting for transfers between devices  31.8 us (22%)
  other arithmetic  4.64 us (3%)
  local copies, waits for them, and re-layouts  4.02 us (3%)
    all_to_all x5, blocking collectives, exchanged(): lax.all_to_all(pieces, axis, 0, 0, tiled=True, axis_index_groups=groups)  54.5 us
    ppermute x2, starting transfers between devices, feature_sum(): other = lax.ppermute(mine, 'feat', SWAP)  25.2 us
    all_to_all x3, waiting for transfers between devices, exchanged(): lax.all_to_all(pieces, axis, 0, 0, tiled=True, axis_index_groups=groups)  24.4 us
    all_to_all x3, starting transfers between devices, exchanged(): lax.all_to_all(pieces, axis, 0, 0, tiled=True, axis_index_groups=groups)  18.8 us
    ppermute x2, waiting for transfers between devices, feature_sum(): other = lax.ppermute(mine, 'feat', SWAP)  7.35 us
  transfers between devices with their start and end apart: 5, of which 5 were waited for; matrix products, arithmetic and copies ran while one was open for 0% of the time, Pallas kernels for 0%

profile of v1, /device:TPU:1, one launch (start us, length us, event | category | flops | bytes accessed | tf_op | source)
XLA Modules:
  0.0 141.0 jit_solution(8136785073017480225)
XLA Ops:
  0.6 0.0 copy-start
  0.6 0.0 copy-start.1
  0.7 1.1 fusion.8
  1.8 0.1 copy.50
  1.9 0.0 copy-done
  1.9 0.0 copy-done.1
  1.9 0.3 fusion.84
  2.2 10.5 %all_to_all.40 = bf16[4,64,640]{2,1,0:T(8,128)(2,1)S(1)} all-to-all(bf16[4,64,640]{2,1,0:T(8,128)(2,1)S(1)} %broadcast_in_dim.16), channel_id=1, replica_groups={{0,1,2,3},{4,5,6,7},{8,9,10,11},{12,13,14,15},{16,17,18,19},{20,21,22,2..., dimensions={0} | all-to-all | bytes 655360 | tf_op jit(solution)/shard_map/all_to_all | solution.py:48
  12.8 0.1 fusion.83
  12.9 0.1 copy.63
  13.0 0.1 copy.64
  13.0 0.1 copy.65
  13.2 0.1 copy.69
  13.3 0.0 copy-start.2
  13.3 15.7 %collective-permute-start = (bf16[64,640]{1,0:T(8,128)(2,1)S(1)}, bf16[64,640]{1,0:T(8,128)(2,1)S(1)}, u32[]{:S(2)}, u32[]{:S(2)}) collective-permute-start(bf16[64,640]{1,0:T(8,128)(2,1)S(1)} %fusion.15), channel_id=1, source_target_pairs={{0,4},{1,5},{2,6},{3,7},{4,0},{5,1},{6,2},{7,3},{8,12},{9,13},{10,... | collective-permute-start | bytes 245768 | tf_op jit(solution)/shard_map/ppermute | solution.py:60
  29.0 0.0 copy-done.2
  29.1 2.0 %collective-permute-done = bf16[64,640]{1,0:T(8,128)(2,1)S(1)} collective-permute-done((bf16[64,640]{1,0:T(8,128)(2,1)S(1)}, bf16[64,640]{1,0:T(8,128)(2,1)S(1)}, u32[]{:S(2)}, u32[]{:S(2)}) %collective-permute-start) | collective-permute-done | bytes 81952 | tf_op jit(solution)/shard_map/ppermute | solution.py:60
  31.1 0.1 fusion.81
  31.2 0.2 convolution_convert_fusion.2
  31.4 0.1 copy.55
  31.6 13.7 %all_to_all.41 = bf16[8,8,640]{2,1,0:T(8,128)(2,1)S(1)} all-to-all(bf16[8,8,640]{2,1,0:T(8,128)(2,1)S(1)} %fusion.17), channel_id=1, replica_groups={{0,8,128,136,256,264,384,392},{16,24,144,152,272,280,400,408},{32,40,16..., dimensions={0} | all-to-all | bytes 163840 | tf_op jit(solution)/shard_map/all_to_all | solution.py:48
  45.2 0.1 reduce-precision_convert_fusion.7
  45.3 0.1 fusion.60
  45.4 0.6 broadcast_in_dim.17
  46.1 9.6 %all-to-all-start.2 = ((bf16[8,8,640]{2,1,0:T(8,128)(2,1)}), bf16[8,8,640]{2,1,0:T(8,128)(2,1)S(1)}, u32[]{:S(2)}, u32[]{:S(2)}) async-start(bf16[8,8,640]{2,1,0:T(8,128)(2,1)} %broadcast_in_dim.17), calls=%async_computation.2 | async-start | bytes 163840 | tf_op jit(solution)/shard_map/all_to_all | solution.py:48
  55.7 0.1 slice_add_fusion.7
  55.8 9.8 %all-to-all-done.2 = bf16[8,8,640]{2,1,0:T(8,128)(2,1)S(1)} async-done(((bf16[8,8,640]{2,1,0:T(8,128)(2,1)}), bf16[8,8,640]{2,1,0:T(8,128)(2,1)S(1)}, u32[]{:S(2)}, u32[]{:S(2)}) %all-to-all-start.2) | async-done | bytes 81952 | tf_op jit(solution)/shard_map/all_to_all | solution.py:48
  65.6 0.2 fusion.79
  65.8 0.1 fusion.73
  65.9 0.1 fusion.62
  66.0 9.5 %all_to_all.42 = bf16[8,8,640]{2,1,0:T(8,128)(2,1)S(1)} all-to-all(bf16[8,8,640]{2,1,0:T(8,128)(2,1)S(1)} %broadcast_in_dim.18), channel_id=1, replica_groups={{0,8,128,136,256,264,384,392},{16,24,144,152,272,280,400,408},{32,40,16..., dimensions={0} | all-to-all | bytes 163840 | tf_op jit(solution)/shard_map/all_to_all | solution.py:48
  75.5 0.3 convolution_convert_fusion.1
  75.8 0.1 multiply_reduce_fusion
  76.0 0.1 copy.56
  76.1 9.0 %all_to_all.43 = bf16[4,64,640]{2,1,0:T(8,128)(2,1)S(1)} all-to-all(bf16[4,64,640]{2,1,0:T(8,128)(2,1)S(1)} %broadcast_in_dim.21), channel_id=1, replica_groups={{0,1,2,3},{4,5,6,7},{8,9,10,11},{12,13,14,15},{16,17,18,19},{20,21,22,2..., dimensions={0} | all-to-all | bytes 655360 | tf_op jit(solution)/shard_map/all_to_all | solution.py:48
  85.2 0.1 fusion.82
  85.3 0.1 copy.66
  85.3 0.1 copy.67
  85.4 0.1 copy.68
  85.5 0.1 copy.70
  85.7 9.5 %collective-permute-start.1 = (bf16[64,640]{1,0:T(8,128)(2,1)S(1)}, bf16[64,640]{1,0:T(8,128)(2,1)S(1)}, u32[]{:S(2)}, u32[]{:S(2)}) collective-permute-start(bf16[64,640]{1,0:T(8,128)(2,1)S(1)} %fusion.19), channel_id=1, source_target_pairs={{0,4},{1,5},{2,6},{3,7},{4,0},{5,1},{6,2},{7,3},{8,12},{9,13},{10,... | collective-permute-start | bytes 245768 | tf_op jit(solution)/shard_map/ppermute | solution.py:60
  95.2 5.4 %collective-permute-done.1 = bf16[64,640]{1,0:T(8,128)(2,1)S(1)} collective-permute-done((bf16[64,640]{1,0:T(8,128)(2,1)S(1)}, bf16[64,640]{1,0:T(8,128)(2,1)S(1)}, u32[]{:S(2)}, u32[]{:S(2)}) %collective-permute-start.1) | collective-permute-done | bytes 81952 | tf_op jit(solution)/shard_map/ppermute | solution.py:60
  100.6 0.1 slice_add_fusion.3
  100.7 0.2 fusion.78
  100.9 0.2 fusion.7
  101.1 0.2 convolution_convert_fusion
  101.3 0.1 copy.61
  101.4 11.8 %all_to_all.44 = bf16[8,8,640]{2,1,0:T(8,128)(2,1)S(1)} all-to-all(bf16[8,8,640]{2,1,0:T(8,128)(2,1)S(1)} %fusion.21), channel_id=1, replica_groups={{0,8,128,136,256,264,384,392},{16,24,144,152,272,280,400,408},{32,40,16..., dimensions={0} | all-to-all | bytes 163840 | tf_op jit(solution)/shard_map/all_to_all | solution.py:48
  113.3 0.1 reduce-precision_convert_fusion.3
  113.4 0.1 fusion.64
  113.5 0.6 broadcast_in_dim.22
  114.1 3.7 %all-to-all-start.6 = ((bf16[8,8,640]{2,1,0:T(8,128)(2,1)}), bf16[8,8,640]{2,1,0:T(8,128)(2,1)S(1)}, u32[]{:S(2)}, u32[]{:S(2)}) async-start(bf16[8,8,640]{2,1,0:T(8,128)(2,1)} %broadcast_in_dim.22), calls=%async_computation.6 | async-start | bytes 163840 | tf_op jit(solution)/shard_map/all_to_all | solution.py:48
  117.8 9.9 %all-to-all-done.6 = bf16[8,8,640]{2,1,0:T(8,128)(2,1)S(1)} async-done(((bf16[8,8,640]{2,1,0:T(8,128)(2,1)}), bf16[8,8,640]{2,1,0:T(8,128)(2,1)S(1)}, u32[]{:S(2)}, u32[]{:S(2)}) %all-to-all-start.6) | async-done | bytes 81952 | tf_op jit(solution)/shard_map/all_to_all | solution.py:48
  127.7 0.2 fusion.76
  128.0 0.1 fusion.31
  128.0 0.1 fusion.66
  128.1 0.6 broadcast_in_dim.23
  128.8 5.5 %all-to-all-start.7 = ((bf16[8,8,640]{2,1,0:T(8,128)(2,1)}), bf16[8,8,640]{2,1,0:T(8,128)(2,1)S(1)}, u32[]{:S(2)}, u32[]{:S(2)}) async-start(bf16[8,8,640]{2,1,0:T(8,128)(2,1)} %broadcast_in_dim.23), calls=%async_computation.7 | async-start | bytes 163840 | tf_op jit(solution)/shard_map/all_to_all | solution.py:48
  134.3 0.2 fusion.28
  134.4 4.8 %all-to-all-done.7 = bf16[8,8,640]{2,1,0:T(8,128)(2,1)S(1)} async-done(((bf16[8,8,640]{2,1,0:T(8,128)(2,1)}), bf16[8,8,640]{2,1,0:T(8,128)(2,1)S(1)}, u32[]{:S(2)}, u32[]{:S(2)}) %all-to-all-start.7) | async-done | bytes 81952 | tf_op jit(solution)/shard_map/all_to_all | solution.py:48
  139.2 0.2 fusion.27
  139.4 0.8 slice_bitcast_fusion
  140.2 0.1 fusion.26
  140.3 0.7 copy.62
  (46 shorter events, 0.6 us)
Async XLA Ops:
  0.6 1.3 copy-start
  0.6 1.2 copy-start.1
  13.3 15.8 %copy-start.2 = (f32[512]{0:T(512)S(1)}, f32[512]{0:T(512)}, u32[]{:S(2)}) copy-start(f32[512]{0:T(512)} %param.4) | copy-start | bytes 6148
  13.3 17.7 %collective-permute-start = (bf16[64,640]{1,0:T(8,128)(2,1)S(1)}, bf16[64,640]{1,0:T(8,128)(2,1)S(1)}, u32[]{:S(2)}, u32[]{:S(2)}) collective-permute-start(bf16[64,640]{1,0:T(8,128)(2,1)S(1)} %fusion.15), channel_id=1, source_target_pairs={{0,4},{1,5},{2,6},{3,7},{4,0},{5,1},{6,2},{7,3},{8,12},{9,13},{10,... | collective-permute-start | bytes 245768 | tf_op jit(solution)/shard_map/ppermute | solution.py:60
  46.1 19.5 %all-to-all-start.2 = ((bf16[8,8,640]{2,1,0:T(8,128)(2,1)}), bf16[8,8,640]{2,1,0:T(8,128)(2,1)S(1)}, u32[]{:S(2)}, u32[]{:S(2)}) async-start(bf16[8,8,640]{2,1,0:T(8,128)(2,1)} %broadcast_in_dim.17), calls=%async_computation.2 | async-start | bytes 163840 | tf_op jit(solution)/shard_map/all_to_all | solution.py:48
  85.7 14.9 %collective-permute-start.1 = (bf16[64,640]{1,0:T(8,128)(2,1)S(1)}, bf16[64,640]{1,0:T(8,128)(2,1)S(1)}, u32[]{:S(2)}, u32[]{:S(2)}) collective-permute-start(bf16[64,640]{1,0:T(8,128)(2,1)S(1)} %fusion.19), channel_id=1, source_target_pairs={{0,4},{1,5},{2,6},{3,7},{4,0},{5,1},{6,2},{7,3},{8,12},{9,13},{10,... | collective-permute-start | bytes 245768 | tf_op jit(solution)/shard_map/ppermute | solution.py:60
  114.1 13.6 %all-to-all-start.6 = ((bf16[8,8,640]{2,1,0:T(8,128)(2,1)}), bf16[8,8,640]{2,1,0:T(8,128)(2,1)S(1)}, u32[]{:S(2)}, u32[]{:S(2)}) async-start(bf16[8,8,640]{2,1,0:T(8,128)(2,1)} %broadcast_in_dim.22), calls=%async_computation.6 | async-start | bytes 163840 | tf_op jit(solution)/shard_map/all_to_all | solution.py:48
  128.8 10.4 %all-to-all-start.7 = ((bf16[8,8,640]{2,1,0:T(8,128)(2,1)}), bf16[8,8,640]{2,1,0:T(8,128)(2,1)S(1)}, u32[]{:S(2)}, u32[]{:S(2)}) async-start(bf16[8,8,640]{2,1,0:T(8,128)(2,1)} %broadcast_in_dim.23), calls=%async_computation.7 | async-start | bytes 163840 | tf_op jit(solution)/shard_map/all_to_all | solution.py:48

commit v2 on v1

v2 whole, which is shorter than its diff:
```python
import functools
import math

import jax
import jax.numpy as jnp
from jax import lax
from jax.experimental import pallas as pl
from jax.experimental.pallas import tpu as pltpu
from jax.sharding import PartitionSpec as P

DAMPING = 0.1
PLANES, LAYERS, CORES = 4, 8, 2
HALVES, COLUMNS = 2, 4
NEAR = PLANES * CORES
TAIL = 128

X_GROUPS = [[h * COLUMNS + i for i in range(COLUMNS)] for h in range(HALVES)]
SWAP = [(i, (i + COLUMNS) % (HALVES * COLUMNS)) for i in range(HALVES * COLUMNS)]
NEAR_GROUPS = [
    [(y * LAYERS + z) * CORES + c for y in range(PLANES) for c in range(CORES)]
    for z in range(LAYERS)
]
FAR_GROUPS = [
    [(y * LAYERS + z) * CORES + c for z in range(LAYERS)]
    for y in range(PLANES)
    for c in range(CORES)
]
F32, BF16 = jnp.float32, jnp.bfloat16


def rounded(x):
    return x.astype(BF16).astype(F32)


def tail_of(*scalars):
    n = scalars[0].shape[0]
    lane = lax.broadcasted_iota(jnp.int32, (n, TAIL), 1)
    tail = jnp.zeros((n, TAIL), F32)
    for i, x in enumerate(scalars):
        x = jnp.broadcast_to(x, (n, TAIL))
        for term in range(3):
            part = rounded(x)
            tail = jnp.where(lane == 3 * i + term, part, tail)
            x = x - part
    return tail


def scalar_in(tail, i):
    lane = lax.broadcasted_iota(jnp.int32, tail.shape, 1)
    return jnp.sum(jnp.where(lane // 3 == i, tail, 0.0), axis=1, keepdims=True)


def wide(x):
    return jnp.broadcast_to(x, (x.shape[0], TAIL))


def dot(a, b, dims):
    return lax.dot_general(a.astype(BF16), b, (dims, ((), ())), preferred_element_type=F32)


def col(x):
    return jnp.sum(x, axis=1, keepdims=True)


def summed(ref):
    x = ref[0].astype(F32)
    for i in range(1, ref.shape[0]):
        x = x + ref[i].astype(F32)
    return x


def put_copies(ref, body, tail):
    m = body.shape[1]
    body, tail = body.astype(BF16), tail.astype(BF16)
    for i in range(ref.shape[0]):
        ref[i, :, :m] = body
        ref[i, :, m:] = tail


def put_pieces(ref, body, tail):
    n, lines, m = ref.shape[0], ref.shape[1], body.shape[1]
    for i in range(n):
        ref[i, :, :m] = body[i * lines : (i + 1) * lines].astype(BF16)
        ref[i, :, m:] = tail[i * lines : (i + 1) * lines].astype(BF16)


def own_lines(ref):
    me = lax.axis_index("samp")
    near = me // (LAYERS * CORES) * CORES + lax.rem(me, CORES)
    lines = ref.shape[0] // NEAR
    return ref[pl.ds(pl.multiple_of(near * lines, lines), lines), :]


def first_rows(grads, base, out):
    b = base[...]
    put_copies(out, dot(b, grads[...], ((1,), (1,))), tail_of(col(b * b)))


def x_total(count, arrived, out):
    m = arrived.shape[2] - TAIL
    total = summed(arrived)
    tail = total[:, m:]
    out[:, :m] = total[:, :m].astype(BF16)
    out[:, m:] = tail_of(*[scalar_in(tail, i) for i in range(count)]).astype(BF16)


def first_image(grads, weights, mine, other, rows, norm, out):
    m = rows.shape[1]
    total = mine[...].astype(F32) + other[...].astype(F32)
    r = total[:, :m]
    rows[...] = r
    norm[...] = wide(scalar_in(total[:, m:], 0))
    weighted = r * weights[...]
    image = dot(weighted, grads[...], ((1,), (0,)))
    put_pieces(out, image, tail_of(col(weighted * r)))


def near_total(arrived, out):
    m = arrived.shape[2] - TAIL
    total = summed(arrived)
    put_copies(out, total[:, :m], tail_of(scalar_in(total[:, m:], 0)))


def first_step(base, norm, arrived, resid, out):
    m = base.shape[1]
    total = summed(arrived)
    b, nn = own_lines(base), own_lines(norm)[:, :1]
    alpha = nn / (scalar_in(total[:, m:], 0) + DAMPING * nn)
    r = b - alpha * (total[:, :m] + DAMPING * b)
    resid[...] = r
    put_copies(out, r, tail_of(alpha))


def lay_out(ref, arrived):
    lines = arrived.shape[1]
    for i in range(arrived.shape[0]):
        ref[i * lines : (i + 1) * lines, :] = arrived[i].astype(F32)


def next_rows(grads, base, arrived, resid, alpha, out, whole):
    m = base.shape[1]
    lay_out(whole, arrived)
    r = whole[:, :m]
    resid[...] = r
    alpha[...] = wide(scalar_in(whole[:, m:], 0))
    put_copies(
        out,
        dot(r, grads[...], ((1,), (1,))),
        tail_of(col(r * r), col(r * base[...])),
    )


def next_image(grads, weights, mine, other, rows0, norm0, rows, norm, square, beta, out):
    m = rows.shape[1]
    total = mine[...].astype(F32) + other[...].astype(F32)
    tail = total[:, m:]
    n0, n1, cross = norm0[:, :1], scalar_in(tail, 0), scalar_in(tail, 1)
    bt = n1 / n0
    r = total[:, :m] + bt * rows0[...]
    rows[...] = r
    norm[...] = wide(n1)
    beta[...] = wide(bt)
    square[...] = wide(n1 + 2.0 * bt * cross + bt * bt * n0)
    weighted = r * weights[...]
    image = dot(weighted, grads[...], ((1,), (0,)))
    put_pieces(out, image, tail_of(col(weighted * r)))


def last_step(base, resid, norm, square, beta, arrived, out):
    m = base.shape[1]
    total = summed(arrived)
    line = resid[...] + own_lines(beta)[:, :1] * own_lines(base)
    alpha = own_lines(norm)[:, :1] / (
        scalar_in(total[:, m:], 0) + DAMPING * own_lines(square)[:, :1]
    )
    r = resid[...] - alpha * (total[:, :m] + DAMPING * line)
    put_copies(out, r, tail_of(alpha))


def outputs(scale, base, resid, beta, alpha0, rows0, rows1, arrived, scores, answer, last, whole):
    m = base.shape[1]
    lay_out(whole, arrived)
    last[...] = whole[:, :m]
    a0, a1 = alpha0[:, :1], scalar_in(whole[:, m:], 0)
    b = base[...]
    answer[...] = a0 * b + a1 * (resid[...] + beta[:, :1] * b)
    every = (a0 * rows0[...] + a1 * rows1[...]) * scale
    share = scores.shape[1]
    feat = lax.axis_index("feat")
    mine = every[:, :share]
    for i in range(1, every.shape[1] // share):
        mine = jnp.where(feat == i, every[:, i * share : (i + 1) * share], mine)
    scores[...] = mine


def call(kernel, outs, *args, scratch=()):
    whole = pl.BlockSpec(memory_space=pltpu.VMEM)
    return pl.pallas_call(
        kernel,
        out_shape=[jax.ShapeDtypeStruct(s, t) for s, t in outs],
        in_specs=[whole] * len(args),
        out_specs=[whole] * len(outs),
        scratch_shapes=list(scratch),
        compiler_params=pltpu.CompilerParams(vmem_limit_bytes=8 * 2**20),
    )(*args)


def exchanged(pieces, axis, groups):
    return lax.all_to_all(pieces, axis, 0, 0, tiled=True, axis_index_groups=groups)


def per_device(grads, weights, targets):
    n_samp, n_feat = lax.axis_size("samp"), lax.axis_size("feat")
    samples = grads.shape[0]
    share = samples // n_feat
    scaled = (weights / (samples * n_samp))[None, :]
    base = targets.T
    dirs, m = base.shape
    lines = dirs // NEAR
    long = m + TAIL
    block, tile = ((dirs, m), F32), ((dirs, TAIL), F32)
    part = ((lines, m), F32)
    to_x = ((COLUMNS, dirs, long), BF16)
    to_half = ((dirs, long), BF16)
    to_near = ((NEAR, lines, long), BF16)
    to_far = ((LAYERS, lines, long), BF16)
    assembled = [pltpu.VMEM((dirs, long), F32)]

    (out,) = call(first_rows, [to_x], grads, base)
    (mine,) = call(functools.partial(x_total, 1), [to_half], exchanged(out, "feat", X_GROUPS))
    other = lax.ppermute(mine, "feat", SWAP)
    rows0, norm0, out = call(
        first_image, [((dirs, samples), F32), tile, to_near], grads, scaled, mine, other
    )
    (out,) = call(near_total, [to_far], exchanged(out, "samp", NEAR_GROUPS))
    resid_own, out = call(
        first_step, [part, to_near], base, norm0, exchanged(out, "samp", FAR_GROUPS)
    )
    resid, alpha0, out = call(
        next_rows,
        [block, tile, to_x],
        grads,
        base,
        exchanged(out, "samp", NEAR_GROUPS),
        scratch=assembled,
    )
    (mine,) = call(functools.partial(x_total, 2), [to_half], exchanged(out, "feat", X_GROUPS))
    other = lax.ppermute(mine, "feat", SWAP)
    rows1, norm1, square, beta, out = call(
        next_image,
        [((dirs, samples), F32), tile, tile, tile, to_near],
        grads,
        scaled,
        mine,
        other,
        rows0,
        norm0,
    )
    (out,) = call(near_total, [to_far], exchanged(out, "samp", NEAR_GROUPS))
    (out,) = call(
        last_step,
        [to_near],
        base,
        resid_own,
        norm1,
        square,
        beta,
        exchanged(out, "samp", FAR_GROUPS),
    )
    scores, answer, last = call(
        functools.partial(outputs, 1.0 / math.sqrt(m * n_feat)),
        [((dirs, share), F32), block, block],
        base,
        resid,
        beta,
        alpha0,
        rows0,
        rows1,
        exchanged(out, "samp", NEAR_GROUPS),
        scratch=assembled,
    )
    return scores.T, answer.T, last.T


def solution(mesh):
    return jax.shard_map(
        per_device,
        mesh=mesh,
        in_specs=(P("samp", "feat"), P("samp"), P("feat", None)),
        out_specs=(P(("samp", "feat"), None), P("feat", None), P("feat", None)),
        check_vma=False,
    )
```

time: 142 us -> 137 us (0.965)
  blocking collectives: 54.5 us -> 96.9 us
  waiting for transfers between devices: 31.8 us -> 7.35 us
  starting transfers between devices: 44 us -> 25.2 us
  other arithmetic: 4.64 us -> 0.01 us
  Pallas kernels: 0 us -> 3.18 us
    all_to_all x5 -> x8, blocking collectives: 54.5 us -> 96.9 us  [exchanged(): lax.all_to_all(pieces, axis, 0, 0, tiled=True, axis_index_groups=groups)]
    all_to_all x3 -> x0, waiting for transfers between devices: 24.4 us -> none  [exchanged(): lax.all_to_all(pieces, axis, 0, 0, tiled=True, axis_index_groups=groups)]
    all_to_all x3 -> x0, starting transfers between devices: 18.8 us -> none  [exchanged(): lax.all_to_all(pieces, axis, 0, 0, tiled=True, axis_index_groups=groups)]
    pallas_call x0 -> x11, Pallas kernels: none -> 3.18 us  [call(): pl.pallas_call(kernel, out_shape=[jax.ShapeDtypeStruct(s, t) for s, t in...]
    broadcast_in_dim x6 -> x0, local copies, waits for them, and re-layouts: 2.01 us -> none  [copies(): return jnp.broadcast_to(x[None], (n, *x.shape))]
    reduce_sum x9 -> x0, other arithmetic: 1.54 us -> none  [the longest x3 1.39 us: col(): return jnp.sum(x, axis=1, keepdims=True)]
  transfers between devices with their start and end apart: 5 -> 2, of which waited for: 5 -> 2; matrix products, arithmetic and copies ran while one was open for 0% -> 0% of each run, Pallas kernels for 0% -> 0%
where the time goes in v2:
time: 137 us; the launch traced here: 136 us
  blocking collectives  96.9 us (71%)
  starting transfers between devices  25.2 us (18%)
  waiting for transfers between devices  7.35 us (5%)
  Pallas kernels  3.18 us (2%)
  local copies, waits for them, and re-layouts  2.65 us (2%)
    all_to_all x8, blocking collectives, exchanged(): lax.all_to_all(pieces, axis, 0, 0, tiled=True, axis_index_groups=groups)  96.9 us
    ppermute x2, starting transfers between devices, per_device(): other = lax.ppermute(mine, 'feat', SWAP)  25.2 us
    ppermute x2, waiting for transfers between devices, per_device(): other = lax.ppermute(mine, 'feat', SWAP)  7.35 us
    pallas_call x11, Pallas kernels, call(): pl.pallas_call(kernel, out_shape=[jax.ShapeDtypeStruct(s, t) for s, t in...  3.18 us
  transfers between devices with their start and end apart: 2, of which 2 were waited for; matrix products, arithmetic and copies ran while one was open for 0% of the time, Pallas kernels for 0%

profile of v2, /device:TPU:1, one launch (start us, length us, event | category | flops | bytes accessed | tf_op | source)
XLA Modules:
  0.0 136.0 jit_solution(14050858420203762659)
XLA Ops:
  0.6 0.0 copy-start
  0.6 1.0 copy-done
  1.7 0.0 copy-start.2
  1.7 0.9 copy-done.2
  2.6 0.3 shard_map.58
  2.9 0.0 copy-start.1
  2.9 10.7 %all_to_all.40.arrived = bf16[4,64,640]{2,1,0:T(8,128)(2,1)S(1)} all-to-all(bf16[4,64,640]{2,1,0:T(8,128)(2,1)S(1)} %shard_map.58), channel_id=1, replica_groups={{0,1,2,3},{4,5,6,7},{8,9,10,11},{12,13,14,15},{16,17,18,19},{20,21,22,2..., dimensions={0} | all-to-all | bytes 655360 | tf_op jit(solution)/shard_map/all_to_all | solution.py:209
  13.5 0.0 copy-start.4
  13.5 0.1 shard_map.59.mine
  13.6 15.7 %collective-permute-start = (bf16[64,640]{1,0:T(8,128)(2,1)S(1)}, bf16[64,640]{1,0:T(8,128)(2,1)S(1)}, u32[]{:S(2)}, u32[]{:S(2)}) collective-permute-start(bf16[64,640]{1,0:T(8,128)(2,1)S(1)} %shard_map.59.mine), channel_id=1, source_target_pairs={{0,4},{1,5},{2,6},{3,7},{4,0},{5,1},{6,2},{7,3},{8,12},{9,13},{10,... | collective-permute-start | bytes 245768 | tf_op jit(solution)/shard_map/ppermute | solution.py:231
  29.4 0.0 copy-done.4
  29.4 2.0 %collective-permute-done.other = bf16[64,640]{1,0:T(8,128)(2,1)S(1)} collective-permute-done((bf16[64,640]{1,0:T(8,128)(2,1)S(1)}, bf16[64,640]{1,0:T(8,128)(2,1)S(1)}, u32[]{:S(2)}, u32[]{:S(2)}) %collective-permute-start) | collective-permute-done | bytes 81952 | tf_op jit(solution)/shard_map/ppermute | solution.py:231
  31.4 0.0 copy-done.1
  31.4 0.2 shard_map.60
  31.6 13.7 %all_to_all.41.arrived = bf16[8,8,640]{2,1,0:T(8,128)(2,1)S(1)} all-to-all(bf16[8,8,640]{2,1,0:T(8,128)(2,1)S(1)} %get-tuple-element.20), channel_id=1, replica_groups={{0,8,128,136,256,264,384,392},{16,24,144,152,272,280,400,408},{32,40,16..., dimensions={0} | all-to-all | bytes 163840 | tf_op jit(solution)/shard_map/all_to_all | solution.py:209
  45.2 0.0 copy-start.3
  45.2 0.1 shard_map.61
  45.3 19.3 %all_to_all.42.arrived = bf16[8,8,640]{2,1,0:T(8,128)(2,1)S(1)} all-to-all(bf16[8,8,640]{2,1,0:T(8,128)(2,1)S(1)} %shard_map.61), channel_id=1, replica_groups={{0,16,32,48,64,80,96,112},{8,24,40,56,72,88,104,120},{128,144,160,176,1..., dimensions={0} | all-to-all | bytes 163840 | tf_op jit(solution)/shard_map/all_to_all | solution.py:209
  64.6 0.0 copy-done.3
  64.6 0.2 shard_map.62
  64.8 9.5 %all_to_all.43.arrived = bf16[8,8,640]{2,1,0:T(8,128)(2,1)S(1)} all-to-all(bf16[8,8,640]{2,1,0:T(8,128)(2,1)S(1)} %get-tuple-element.21), channel_id=1, replica_groups={{0,8,128,136,256,264,384,392},{16,24,144,152,272,280,400,408},{32,40,16..., dimensions={0} | all-to-all | bytes 163840 | tf_op jit(solution)/shard_map/all_to_all | solution.py:209
  74.3 0.3 shard_map.63
  74.6 9.0 %all_to_all.44.arrived = bf16[4,64,640]{2,1,0:T(8,128)(2,1)S(1)} all-to-all(bf16[4,64,640]{2,1,0:T(8,128)(2,1)S(1)} %get-tuple-element.23), channel_id=1, replica_groups={{0,1,2,3},{4,5,6,7},{8,9,10,11},{12,13,14,15},{16,17,18,19},{20,21,22,2..., dimensions={0} | all-to-all | bytes 655360 | tf_op jit(solution)/shard_map/all_to_all | solution.py:209
  83.6 0.1 shard_map.64.mine
  83.8 9.5 %collective-permute-start.1 = (bf16[64,640]{1,0:T(8,128)(2,1)S(1)}, bf16[64,640]{1,0:T(8,128)(2,1)S(1)}, u32[]{:S(2)}, u32[]{:S(2)}) collective-permute-start(bf16[64,640]{1,0:T(8,128)(2,1)S(1)} %shard_map.64.mine), channel_id=1, source_target_pairs={{0,4},{1,5},{2,6},{3,7},{4,0},{5,1},{6,2},{7,3},{8,12},{9,13},{10,... | collective-permute-start | bytes 245768 | tf_op jit(solution)/shard_map/ppermute | solution.py:248
  93.3 5.4 %collective-permute-done.1.other = bf16[64,640]{1,0:T(8,128)(2,1)S(1)} collective-permute-done((bf16[64,640]{1,0:T(8,128)(2,1)S(1)}, bf16[64,640]{1,0:T(8,128)(2,1)S(1)}, u32[]{:S(2)}, u32[]{:S(2)}) %collective-permute-start.1) | collective-permute-done | bytes 81952 | tf_op jit(solution)/shard_map/ppermute | solution.py:248
  98.6 0.4 shard_map.65
  99.0 11.8 %all_to_all.45.arrived = bf16[8,8,640]{2,1,0:T(8,128)(2,1)S(1)} all-to-all(bf16[8,8,640]{2,1,0:T(8,128)(2,1)S(1)} %get-tuple-element.31), channel_id=1, replica_groups={{0,8,128,136,256,264,384,392},{16,24,144,152,272,280,400,408},{32,40,16..., dimensions={0} | all-to-all | bytes 163840 | tf_op jit(solution)/shard_map/all_to_all | solution.py:209
  110.8 0.1 shard_map.66
  110.9 13.4 %all_to_all.46.arrived = bf16[8,8,640]{2,1,0:T(8,128)(2,1)S(1)} all-to-all(bf16[8,8,640]{2,1,0:T(8,128)(2,1)S(1)} %shard_map.66), channel_id=1, replica_groups={{0,16,32,48,64,80,96,112},{8,24,40,56,72,88,104,120},{128,144,160,176,1..., dimensions={0} | all-to-all | bytes 163840 | tf_op jit(solution)/shard_map/all_to_all | solution.py:209
  124.3 0.2 shard_map.67
  124.5 9.5 %all_to_all.47.arrived = bf16[8,8,640]{2,1,0:T(8,128)(2,1)S(1)} all-to-all(bf16[8,8,640]{2,1,0:T(8,128)(2,1)S(1)} %shard_map.67), channel_id=1, replica_groups={{0,8,128,136,256,264,384,392},{16,24,144,152,272,280,400,408},{32,40,16..., dimensions={0} | all-to-all | bytes 163840 | tf_op jit(solution)/shard_map/all_to_all | solution.py:209
  134.0 1.3 shard_map.68
  135.3 0.7 copy.6
  (1 shorter events, 0.0 us)
Async XLA Ops:
  0.6 1.0 copy-start
  1.7 0.9 copy-start.2
  2.9 28.5 %copy-start.1 = (bf16[512,512]{1,0:T(8,128)(2,1)S(1)}, bf16[512,512]{1,0:T(8,128)(2,1)}, u32[]{:S(2)}) copy-start(bf16[512,512]{1,0:T(8,128)(2,1)} %grads.7) | copy-start | bytes 1572868
  13.5 15.8 %copy-start.4 = (f32[512]{0:T(512)S(1)}, f32[512]{0:T(512)}, u32[]{:S(2)}) copy-start(f32[512]{0:T(512)} %param.4) | copy-start | bytes 6148
  13.6 17.7 %collective-permute-start = (bf16[64,640]{1,0:T(8,128)(2,1)S(1)}, bf16[64,640]{1,0:T(8,128)(2,1)S(1)}, u32[]{:S(2)}, u32[]{:S(2)}) collective-permute-start(bf16[64,640]{1,0:T(8,128)(2,1)S(1)} %shard_map.59.mine), channel_id=1, source_target_pairs={{0,4},{1,5},{2,6},{3,7},{4,0},{5,1},{6,2},{7,3},{8,12},{9,13},{10,... | collective-permute-start | bytes 245768 | tf_op jit(solution)/shard_map/ppermute | solution.py:231
  45.2 19.4 %copy-start.3 = (f32[512,64]{0,1:T(8,128)S(1)}, f32[512,64]{0,1:T(8,128)}, u32[]{:S(2)}) copy-start(f32[512,64]{0,1:T(8,128)} %param.5) | copy-start | bytes 393220
  83.8 14.9 %collective-permute-start.1 = (bf16[64,640]{1,0:T(8,128)(2,1)S(1)}, bf16[64,640]{1,0:T(8,128)(2,1)S(1)}, u32[]{:S(2)}, u32[]{:S(2)}) collective-permute-start(bf16[64,640]{1,0:T(8,128)(2,1)S(1)} %shard_map.64.mine), channel_id=1, source_target_pairs={{0,4},{1,5},{2,6},{3,7},{4,0},{5,1},{6,2},{7,3},{8,12},{9,13},{10,... | collective-permute-start | bytes 245768 | tf_op jit(solution)/shard_map/ppermute | solution.py:248

commit v3 on v2

v3 whole, which is shorter than its diff:
```python
import functools
import math

import jax
import jax.numpy as jnp
from jax import lax
from jax.experimental import pallas as pl
from jax.experimental.pallas import tpu as pltpu
from jax.sharding import PartitionSpec as P

DAMPING = 0.1
PLANES, LAYERS, CORES = 4, 8, 2
HALVES, COLUMNS = 2, 4
NEAR = PLANES * CORES
LINES, LANES = 8, 128
CHUNKS = 4

X_GROUPS = [[h * COLUMNS + i for i in range(COLUMNS)] for h in range(HALVES)]
SWAP = [(i, (i + COLUMNS) % (HALVES * COLUMNS)) for i in range(HALVES * COLUMNS)]
NEAR_GROUPS = [
    [(y * LAYERS + z) * CORES + c for y in range(PLANES) for c in range(CORES)]
    for z in range(LAYERS)
]
FAR_GROUPS = [
    [(y * LAYERS + z) * CORES + c for z in range(LAYERS)]
    for y in range(PLANES)
    for c in range(CORES)
]
F32, BF16 = jnp.float32, jnp.bfloat16


def dot(a, b, dims):
    return lax.dot_general(a.astype(BF16), b, (dims, ((), ())), preferred_element_type=F32)


def col(x):
    return jnp.sum(x, axis=1, keepdims=True)


def iota(shape, axis):
    return lax.broadcasted_iota(jnp.int32, shape, axis)


def as_row(column):
    shape = (column.shape[0], LANES)
    eye = iota(shape, 0) == iota(shape, 1)
    return jnp.sum(jnp.where(eye, jnp.broadcast_to(column, shape), 0.0), axis=0, keepdims=True)


def as_column(row, n, first=0):
    shape = (n, LANES)
    eye = iota(shape, 0) + first == iota(shape, 1)
    return col(jnp.where(eye, jnp.broadcast_to(row, shape), 0.0))


def tail_of(*rows):
    shape = (LINES, LANES)
    tail = jnp.zeros(shape, F32)
    for i, x in enumerate(rows):
        x = jnp.broadcast_to(x, shape)
        for term in range(3):
            part = x.astype(BF16).astype(F32)
            tail = jnp.where(iota(shape, 0) == 3 * i + term, part, tail)
            x = x - part
    return tail


def row_in(tail, i):
    line = iota(tail.shape, 0)
    chosen = (line >= 3 * i) & (line < 3 * i + 3)
    return jnp.sum(jnp.where(chosen, tail, 0.0), axis=0, keepdims=True)


def tiles_of(body):
    return [
        body[i : i + LINES, j : j + LANES]
        for i in range(0, body.shape[0], LINES)
        for j in range(0, body.shape[1], LANES)
    ]


def body_of(tiles, width):
    across = width // LANES
    lines = [
        jnp.concatenate(tiles[i : i + across], axis=1) for i in range(0, len(tiles), across)
    ]
    return jnp.concatenate(lines, axis=0) if len(lines) > 1 else lines[0]


def put(ref, tiles):
    for i, tile in enumerate(tiles):
        ref[i] = tile.astype(BF16)


def put_copies(ref, tiles):
    for i in range(ref.shape[0]):
        put(ref.at[i], tiles)


def tiles_in(ref):
    return [ref[i].astype(F32) for i in range(ref.shape[0])]


def summed(ref):
    totals = tiles_in(ref.at[0])
    for i in range(1, ref.shape[0]):
        totals = [a + b for a, b in zip(totals, tiles_in(ref.at[i]))]
    return totals


def own_first():
    me = lax.axis_index("samp")
    near = me // (LAYERS * CORES) * CORES + lax.rem(me, CORES)
    return near * LINES


def own_lines(ref):
    return ref[pl.ds(pl.multiple_of(own_first(), LINES), LINES), :]


def put_pieces(out, image, curve):
    tiles, tail = tiles_of(image), tail_of(as_row(curve))
    across = len(tiles) // out.shape[0]
    for i in range(out.shape[0]):
        put(out.at[i], tiles[i * across : (i + 1) * across] + [tail])


def first_rows(grads, base, out, held, line, sems):
    high = held.shape[1]
    loads = [pltpu.make_async_copy(base, line, sems.at[CHUNKS])] + [
        pltpu.make_async_copy(grads.at[pl.ds(i * high, high), :], held.at[i], sems.at[i])
        for i in range(CHUNKS)
    ]
    for load in loads:
        load.start()
    loads[0].wait()
    b = line[...]
    tail = tail_of(as_row(col(b * b)))
    packed = b.astype(BF16)
    parts = []
    for i in range(CHUNKS):
        loads[i + 1].wait()
        parts.append(dot(packed, held[i], ((1,), (1,))))
    put_copies(out, tiles_of(jnp.concatenate(parts, axis=1)) + [tail])


def x_total(count, arrived, out):
    tiles = summed(arrived)
    tail = tail_of(*[row_in(tiles[-1], i) for i in range(count)])
    put(out, tiles[:-1] + [tail])


def first_image(grads, weights, mine, other, rows, norm, out):
    tiles = [a + b for a, b in zip(tiles_in(mine), tiles_in(other))]
    r = body_of(tiles[:-1], rows.shape[1])
    rows[...] = r
    norm[...] = row_in(tiles[-1], 0)
    weighted = r * weights[...]
    put_pieces(out, dot(weighted, grads[...], ((1,), (0,))), col(weighted * r))


def near_total(arrived, out):
    tiles = summed(arrived)
    put_copies(out, tiles[:-1] + [tail_of(row_in(tiles[-1], 0))])


def first_step(base, norm, arrived, resid, alpha, out):
    tiles = summed(arrived)
    n = norm[...]
    a = n / (row_in(tiles[-1], 0) + DAMPING * n)
    alpha[...] = a
    b = own_lines(base)
    image = body_of(tiles[:-1], base.shape[1])
    r = b - as_column(a, LINES, own_first()) * (image + DAMPING * b)
    resid[...] = r
    put_copies(out, tiles_of(r))


def laid_out(arrived, width):
    return body_of([t for i in range(arrived.shape[0]) for t in tiles_in(arrived.at[i])], width)


def next_rows(grads, base, arrived, resid, out):
    b = base[...]
    r = laid_out(arrived, b.shape[1])
    resid[...] = r
    tail = tail_of(as_row(col(r * r)), as_row(col(r * b)))
    put_copies(out, tiles_of(dot(r, grads[...], ((1,), (1,)))) + [tail])


def next_image(grads, weights, mine, other, rows0, norm0, rows, norm, square, beta, out):
    tiles = [a + b for a, b in zip(tiles_in(mine), tiles_in(other))]
    n0, n1, cross = norm0[...], row_in(tiles[-1], 0), row_in(tiles[-1], 1)
    bt = n1 / n0
    norm[...] = n1
    beta[...] = bt
    square[...] = n1 + 2.0 * bt * cross + bt * bt * n0
    old = rows0[...]
    r = body_of(tiles[:-1], old.shape[1]) + as_column(bt, old.shape[0]) * old
    rows[...] = r
    weighted = r * weights[...]
    put_pieces(out, dot(weighted, grads[...], ((1,), (0,))), col(weighted * r))


def last_step(base, resid, norm, square, beta, arrived, alpha, out):
    tiles = summed(arrived)
    a = norm[...] / (row_in(tiles[-1], 0) + DAMPING * square[...])
    alpha[...] = a
    first = own_first()
    line = resid[...] + as_column(beta[...], LINES, first) * own_lines(base)
    image = body_of(tiles[:-1], base.shape[1])
    r = resid[...] - as_column(a, LINES, first) * (image + DAMPING * line)
    put_copies(out, tiles_of(r))


def outputs(
    scale, base, resid, beta, alpha0, alpha1, rows0, rows1, arrived, scores, answer, last, *scratch
):
    score_held, answer_held, last_held, sems = scratch
    last_held[...] = laid_out(arrived, base.shape[1])
    stores = [
        pltpu.make_async_copy(held, out, sems.at[i])
        for i, (held, out) in enumerate(
            ((last_held, last), (answer_held, answer), (score_held, scores))
        )
    ]
    stores[0].start()
    b = base[...]
    dirs = b.shape[0]
    a0, a1 = as_column(alpha0[...], dirs), as_column(alpha1[...], dirs)
    answer_held[...] = a0 * b + a1 * (resid[...] + as_column(beta[...], dirs) * b)
    stores[1].start()
    every = (a0 * rows0[...] + a1 * rows1[...]) * scale
    share = scores.shape[0]
    feat = lax.axis_index("feat")
    mine = every[:, :share]
    for i in range(1, every.shape[1] // share):
        mine = jnp.where(feat == i, every[:, i * share : (i + 1) * share], mine)
    score_held[...] = mine.T
    stores[2].start()
    for store in stores:
        store.wait()


VMEM = pl.BlockSpec(memory_space=pltpu.VMEM)
HBM = pl.BlockSpec(memory_space=pltpu.HBM)


def call(kernel, outs, *args, inputs=VMEM, results=VMEM, scratch=()):
    return pl.pallas_call(
        kernel,
        out_shape=[jax.ShapeDtypeStruct(s, t) for s, t in outs],
        in_specs=[inputs] * len(args),
        out_specs=[results] * len(outs),
        scratch_shapes=list(scratch),
        compiler_params=pltpu.CompilerParams(vmem_limit_bytes=8 * 2**20),
    )(*args)


def exchanged(pieces, axis, groups):
    return lax.all_to_all(pieces, axis, 0, 0, tiled=True, axis_index_groups=groups)


def per_device(grads, weights, targets):
    n_samp, n_feat = lax.axis_size("samp"), lax.axis_size("feat")
    samples = grads.shape[0]
    share = samples // n_feat
    scaled = (weights / (samples * n_samp))[None, :]
    base = targets.T
    dirs, m = base.shape
    across = m // LANES
    row_tiles = dirs // LINES * (samples // LANES) + 1
    block, row, part = ((dirs, m), F32), ((1, LANES), F32), ((LINES, m), F32)
    block_rows = ((dirs, samples), F32)
    to_x = ((COLUMNS, row_tiles, LINES, LANES), BF16)
    to_half = ((row_tiles, LINES, LANES), BF16)
    to_near = ((NEAR, across + 1, LINES, LANES), BF16)
    to_far = ((LAYERS, across + 1, LINES, LANES), BF16)
    to_all = ((NEAR, across, LINES, LANES), BF16)

    (out,) = call(
        first_rows,
        [to_x],
        pltpu.with_memory_space_constraint(grads, pltpu.HBM),
        pltpu.with_memory_space_constraint(base, pltpu.HBM),
        inputs=HBM,
        scratch=[
            pltpu.VMEM((CHUNKS, samples // CHUNKS, m), BF16),
            pltpu.VMEM((dirs, m), F32),
            pltpu.SemaphoreType.DMA((CHUNKS + 1,)),
        ],
    )
    (mine,) = call(functools.partial(x_total, 1), [to_half], exchanged(out, "feat", X_GROUPS))
    other = lax.ppermute(mine, "feat", SWAP)
    rows0, norm0, out = call(
        first_image, [block_rows, row, to_near], grads, scaled, mine, other
    )
    (out,) = call(near_total, [to_far], exchanged(out, "samp", NEAR_GROUPS))
    resid_own, alpha0, out = call(
        first_step, [part, row, to_all], base, norm0, exchanged(out, "samp", FAR_GROUPS)
    )
    resid, out = call(
        next_rows, [block, to_x], grads, base, exchanged(out, "samp", NEAR_GROUPS)
    )
    (mine,) = call(functools.partial(x_total, 2), [to_half], exchanged(out, "feat", X_GROUPS))
    other = lax.ppermute(mine, "feat", SWAP)
    rows1, norm1, square, beta, out = call(
        next_image,
        [block_rows, row, row, row, to_near],
        grads,
        scaled,
        mine,
        other,
        rows0,
        norm0,
    )
    (out,) = call(near_total, [to_far], exchanged(out, "samp", NEAR_GROUPS))
    alpha1, out = call(
        last_step,
        [row, to_all],
        base,
        resid_own,
        norm1,
        square,
        beta,
        exchanged(out, "samp", FAR_GROUPS),
    )
    scores, answer, last = call(
        functools.partial(outputs, 1.0 / math.sqrt(m * n_feat)),
        [((share, dirs), F32), block, block],
        base,
        resid,
        beta,
        alpha0,
        alpha1,
        rows0,
        rows1,
        exchanged(out, "samp", NEAR_GROUPS),
        results=HBM,
        scratch=[
            pltpu.VMEM((share, dirs), F32),
            pltpu.VMEM((dirs, m), F32),
            pltpu.VMEM((dirs, m), F32),
            pltpu.SemaphoreType.DMA((3,)),
        ],
    )
    return scores, answer.T, last.T


def solution(mesh):
    return jax.shard_map(
        per_device,
        mesh=mesh,
        in_specs=(P("samp", "feat"), P("samp"), P("feat", None)),
        out_specs=(P(("samp", "feat"), None), P("feat", None), P("feat", None)),
        check_vma=False,
    )
```

time: 137 us -> 131 us (0.956)
  blocking collectives: 96.9 us -> 92.6 us
  local copies, waits for them, and re-layouts: 2.65 us -> 0.01 us
  starting transfers between devices: 25.2 us -> 22.9 us
  waiting for transfers between devices: 7.35 us -> 9.51 us
    all_to_all x8, blocking collectives: 96.9 us -> 92.6 us  [exchanged(): lax.all_to_all(pieces, axis, 0, 0, tiled=True, axis_index_groups=groups)]
    unnamed x11 -> x6, local copies, waits for them, and re-layouts: 2.65 us -> 0.01 us
    ppermute x2, starting transfers between devices: 25.2 us -> 22.9 us  [per_device(): other = lax.ppermute(mine, 'feat', SWAP)]
    ppermute x2, waiting for transfers between devices: 7.35 us -> 9.51 us  [per_device(): other = lax.ppermute(mine, 'feat', SWAP)]
where the time goes in v3:
time: 131 us; the launch traced here: 130 us
  blocking collectives  92.6 us (71%)
  starting transfers between devices  22.9 us (17%)
  waiting for transfers between devices  9.51 us (7%)
  Pallas kernels  4.37 us (3%)
    all_to_all x8, blocking collectives, exchanged(): lax.all_to_all(pieces, axis, 0, 0, tiled=True, axis_index_groups=groups)  92.6 us
    ppermute x2, starting transfers between devices, per_device(): other = lax.ppermute(mine, 'feat', SWAP)  22.9 us
    ppermute x2, waiting for transfers between devices, per_device(): other = lax.ppermute(mine, 'feat', SWAP)  9.51 us
    pallas_call x11, Pallas kernels, call(): pl.pallas_call(kernel, out_shape=[jax.ShapeDtypeStruct(s, t) for s, t in...  4.37 us
  transfers between devices with their start and end apart: 2, of which 2 were waited for; matrix products, arithmetic and copies ran while one was open for 0% of the time, Pallas kernels for 0%

profile of v3, /device:TPU:1, one launch (start us, length us, event | category | flops | bytes accessed | tf_op | source)
XLA Modules:
  0.0 130.1 jit_solution(18106348396336344600)
XLA Ops:
  0.6 1.8 %shard_map.58 = bf16[4,33,8,128]{3,2,1,0:T(8,128)(2,1)S(1)} custom-call(bf16[512,512]{1,0:T(8,128)(2,1)} %grads.7, f32[64,512]{1,0:T(8,128)} %bitcast.4), custom_call_target="tpu_custom_call" | custom-call | tf_op jit(solution)/shard_map/pallas_call | solution.py:250
  2.5 0.0 copy-start
  2.5 10.3 %all_to_all.40.arrived = bf16[4,33,8,128]{3,2,1,0:T(8,128)(2,1)S(1)} all-to-all(bf16[4,33,8,128]{3,2,1,0:T(8,128)(2,1)S(1)} %shard_map.58), channel_id=1, replica_groups={{0,1,2,3},{4,5,6,7},{8,9,10,11},{12,13,14,15},{16,17,18,19},{20,21,22,2..., dimensions={0} | all-to-all | bytes 540672 | tf_op jit(solution)/shard_map/all_to_all | solution.py:261
  12.8 0.0 copy-start.2
  12.8 0.1 shard_map.59.mine
  12.9 15.5 %collective-permute-start = (bf16[33,8,128]{2,1,0:T(8,128)(2,1)S(1)}, bf16[33,8,128]{2,1,0:T(8,128)(2,1)S(1)}, u32[]{:S(2)}, u32[]{:S(2)}) collective-permute-start(bf16[33,8,128]{2,1,0:T(8,128)(2,1)S(1)} %shard_map.59.mine), channel_id=1, source_target_pairs={{0,4},{1,5},{2,6},{3,7},{4,0},{5,1},{6,2},{7,3},{8,12},{9,13},{10,... | collective-permute-start | bytes 202760 | tf_op jit(solution)/shard_map/ppermute | solution.py:294
  28.4 0.0 copy-done.2
  28.4 1.6 %collective-permute-done.other = bf16[33,8,128]{2,1,0:T(8,128)(2,1)S(1)} collective-permute-done((bf16[33,8,128]{2,1,0:T(8,128)(2,1)S(1)}, bf16[33,8,128]{2,1,0:T(8,128)(2,1)S(1)}, u32[]{:S(2)}, u32[]{:S(2)}) %collective-permute-start) | collective-permute-done | bytes 67616 | tf_op jit(solution)/shard_map/ppermute | solution.py:294
  30.0 0.0 copy-done
  30.0 0.2 shard_map.60
  30.2 12.9 %all_to_all.41.arrived = bf16[8,5,8,128]{3,2,1,0:T(8,128)(2,1)S(1)} all-to-all(bf16[8,5,8,128]{3,2,1,0:T(8,128)(2,1)S(1)} %get-tuple-element.22), channel_id=1, replica_groups={{0,8,128,136,256,264,384,392},{16,24,144,152,272,280,400,408},{32,40,16..., dimensions={0} | all-to-all | bytes 163840 | tf_op jit(solution)/shard_map/all_to_all | solution.py:261
  43.2 0.0 copy-start.1
  43.2 19.6 %all_to_all.42.arrived = bf16[8,5,8,128]{3,2,1,0:T(8,128)(2,1)S(1)} all-to-all(bf16[8,5,8,128]{3,2,1,0:T(8,128)(2,1)S(1)} %shard_map.61), channel_id=1, replica_groups={{0,16,32,48,64,80,96,112},{8,24,40,56,72,88,104,120},{128,144,160,176,1..., dimensions={0} | all-to-all | bytes 163840 | tf_op jit(solution)/shard_map/all_to_all | solution.py:261
  62.9 0.0 copy-done.1
  62.9 0.1 shard_map.62
  63.0 9.4 %all_to_all.43.arrived = bf16[8,4,8,128]{3,2,1,0:T(8,128)(2,1)S(1)} all-to-all(bf16[8,4,8,128]{3,2,1,0:T(8,128)(2,1)S(1)} %get-tuple-element.23), channel_id=1, replica_groups={{0,8,128,136,256,264,384,392},{16,24,144,152,272,280,400,408},{32,40,16..., dimensions={0} | all-to-all | bytes 131072 | tf_op jit(solution)/shard_map/all_to_all | solution.py:261
  72.4 0.3 shard_map.63
  72.7 8.1 %all_to_all.44.arrived = bf16[4,33,8,128]{3,2,1,0:T(8,128)(2,1)S(1)} all-to-all(bf16[4,33,8,128]{3,2,1,0:T(8,128)(2,1)S(1)} %get-tuple-element.25), channel_id=1, replica_groups={{0,1,2,3},{4,5,6,7},{8,9,10,11},{12,13,14,15},{16,17,18,19},{20,21,22,2..., dimensions={0} | all-to-all | bytes 540672 | tf_op jit(solution)/shard_map/all_to_all | solution.py:261
  80.8 0.1 shard_map.64.mine
  80.9 7.4 %collective-permute-start.1 = (bf16[33,8,128]{2,1,0:T(8,128)(2,1)S(1)}, bf16[33,8,128]{2,1,0:T(8,128)(2,1)S(1)}, u32[]{:S(2)}, u32[]{:S(2)}) collective-permute-start(bf16[33,8,128]{2,1,0:T(8,128)(2,1)S(1)} %shard_map.64.mine), channel_id=1, source_target_pairs={{0,4},{1,5},{2,6},{3,7},{4,0},{5,1},{6,2},{7,3},{8,12},{9,13},{10,... | collective-permute-start | bytes 202760 | tf_op jit(solution)/shard_map/ppermute | solution.py:306
  88.3 7.9 %collective-permute-done.1.other = bf16[33,8,128]{2,1,0:T(8,128)(2,1)S(1)} collective-permute-done((bf16[33,8,128]{2,1,0:T(8,128)(2,1)S(1)}, bf16[33,8,128]{2,1,0:T(8,128)(2,1)S(1)}, u32[]{:S(2)}, u32[]{:S(2)}) %collective-permute-start.1) | collective-permute-done | bytes 67616 | tf_op jit(solution)/shard_map/ppermute | solution.py:306
  96.2 0.3 shard_map.65
  96.5 9.2 %all_to_all.45.arrived = bf16[8,5,8,128]{3,2,1,0:T(8,128)(2,1)S(1)} all-to-all(bf16[8,5,8,128]{3,2,1,0:T(8,128)(2,1)S(1)} %get-tuple-element.32), channel_id=1, replica_groups={{0,8,128,136,256,264,384,392},{16,24,144,152,272,280,400,408},{32,40,16..., dimensions={0} | all-to-all | bytes 163840 | tf_op jit(solution)/shard_map/all_to_all | solution.py:261
  105.7 13.5 %all_to_all.46.arrived = bf16[8,5,8,128]{3,2,1,0:T(8,128)(2,1)S(1)} all-to-all(bf16[8,5,8,128]{3,2,1,0:T(8,128)(2,1)S(1)} %shard_map.66), channel_id=1, replica_groups={{0,16,32,48,64,80,96,112},{8,24,40,56,72,88,104,120},{128,144,160,176,1..., dimensions={0} | all-to-all | bytes 163840 | tf_op jit(solution)/shard_map/all_to_all | solution.py:261
  119.1 0.1 shard_map.67
  119.3 9.4 %all_to_all.47.arrived = bf16[8,4,8,128]{3,2,1,0:T(8,128)(2,1)S(1)} all-to-all(bf16[8,4,8,128]{3,2,1,0:T(8,128)(2,1)S(1)} %get-tuple-element.35), channel_id=1, replica_groups={{0,8,128,136,256,264,384,392},{16,24,144,152,272,280,400,408},{32,40,16..., dimensions={0} | all-to-all | bytes 131072 | tf_op jit(solution)/shard_map/all_to_all | solution.py:261
  128.7 1.4 %shard_map.68 = (f32[64,64]{1,0:T(8,128)}, f32[64,512]{1,0:T(8,128)}, f32[64,512]{1,0:T(8,128)}) custom-call(f32[64,512]{1,0:T(8,128)S(1)} %bitcast.8, f32[64,512]{1,0:T(8,128)S(1)} %get-tuple-element.24.resid, f32[1,128]{1,0:T(1,128)S(1)} %get-tuple-element.27.beta, f32[1,128]{1,0:T(1,128)S(1)} %get-tuple-element.28.alpha0, ...), custom_call_target="tpu_custom_call" | custom-call | tf_op jit(solution)/shard_map/pallas_call | solution.py:250
  (3 shorter events, 0.1 us)
Async XLA Ops:
  2.5 27.5 %copy-start = (bf16[512,512]{1,0:T(8,128)(2,1)S(1)}, bf16[512,512]{1,0:T(8,128)(2,1)}, u32[]{:S(2)}) copy-start(bf16[512,512]{1,0:T(8,128)(2,1)} %grads.7) | copy-start | bytes 1572868
  12.8 15.5 %copy-start.2 = (f32[512]{0:T(512)S(1)}, f32[512]{0:T(512)}, u32[]{:S(2)}) copy-start(f32[512]{0:T(512)} %param.4) | copy-start | bytes 6148
  12.9 17.1 %collective-permute-start = (bf16[33,8,128]{2,1,0:T(8,128)(2,1)S(1)}, bf16[33,8,128]{2,1,0:T(8,128)(2,1)S(1)}, u32[]{:S(2)}, u32[]{:S(2)}) collective-permute-start(bf16[33,8,128]{2,1,0:T(8,128)(2,1)S(1)} %shard_map.59.mine), channel_id=1, source_target_pairs={{0,4},{1,5},{2,6},{3,7},{4,0},{5,1},{6,2},{7,3},{8,12},{9,13},{10,... | collective-permute-start | bytes 202760 | tf_op jit(solution)/shard_map/ppermute | solution.py:294
  43.2 19.7 %copy-start.1 = (f32[512,64]{0,1:T(8,128)S(1)}, f32[512,64]{0,1:T(8,128)}, u32[]{:S(2)}) copy-start(f32[512,64]{0,1:T(8,128)} %param.5) | copy-start | bytes 393220
  80.9 15.3 %collective-permute-start.1 = (bf16[33,8,128]{2,1,0:T(8,128)(2,1)S(1)}, bf16[33,8,128]{2,1,0:T(8,128)(2,1)S(1)}, u32[]{:S(2)}, u32[]{:S(2)}) collective-permute-start(bf16[33,8,128]{2,1,0:T(8,128)(2,1)S(1)} %shard_map.64.mine), channel_id=1, source_target_pairs={{0,4},{1,5},{2,6},{3,7},{4,0},{5,1},{6,2},{7,3},{8,12},{9,13},{10,... | collective-permute-start | bytes 202760 | tf_op jit(solution)/shard_map/ppermute | solution.py:306

commit v4 on v3

v4 whole, which is shorter than its diff:
```python
import functools
import math

import jax
import jax.numpy as jnp
from jax import lax
from jax.experimental import pallas as pl
from jax.experimental.pallas import tpu as pltpu
from jax.sharding import PartitionSpec as P

DAMPING = 0.1
PLANES, LAYERS, CORES = 4, 8, 2
HALVES, COLUMNS = 2, 4
NEAR = PLANES * CORES
LINES, LANES = 8, 128

X_GROUPS = [[h * COLUMNS + i for i in range(COLUMNS)] for h in range(HALVES)]
SWAP = [(i, (i + COLUMNS) % (HALVES * COLUMNS)) for i in range(HALVES * COLUMNS)]
NEAR_GROUPS = [
    [(y * LAYERS + z) * CORES + c for y in range(PLANES) for c in range(CORES)]
    for z in range(LAYERS)
]
FAR_GROUPS = [
    [(y * LAYERS + z) * CORES + c for z in range(LAYERS)]
    for y in range(PLANES)
    for c in range(CORES)
]
F32, BF16 = jnp.float32, jnp.bfloat16


def dot(a, b, dims):
    return lax.dot_general(a.astype(BF16), b, (dims, ((), ())), preferred_element_type=F32)


def col(x):
    return jnp.sum(x, axis=1, keepdims=True)


def iota(shape, axis):
    return lax.broadcasted_iota(jnp.int32, shape, axis)


def as_row(column):
    shape = (column.shape[0], LANES)
    eye = iota(shape, 0) == iota(shape, 1)
    return jnp.sum(jnp.where(eye, jnp.broadcast_to(column, shape), 0.0), axis=0, keepdims=True)


def as_column(row, n, first=0):
    shape = (n, LANES)
    eye = iota(shape, 0) + first == iota(shape, 1)
    return col(jnp.where(eye, jnp.broadcast_to(row, shape), 0.0))


def tail_of(*rows):
    shape = (LINES, LANES)
    tail = jnp.zeros(shape, F32)
    for i, x in enumerate(rows):
        x = jnp.broadcast_to(x, shape)
        for term in range(3):
            part = x.astype(BF16).astype(F32)
            tail = jnp.where(iota(shape, 0) == 3 * i + term, part, tail)
            x = x - part
    return tail


def row_in(tail, i):
    line = iota(tail.shape, 0)
    chosen = (line >= 3 * i) & (line < 3 * i + 3)
    return jnp.sum(jnp.where(chosen, tail, 0.0), axis=0, keepdims=True)


def column_tail(*columns):
    shape = (columns[0].shape[0], LANES)
    tail = jnp.zeros(shape, F32)
    for i, x in enumerate(columns):
        x = jnp.broadcast_to(x, shape)
        for term in range(3):
            part = x.astype(BF16).astype(F32)
            tail = jnp.where(iota(shape, 1) == 3 * i + term, part, tail)
            x = x - part
    return tail


def column_in(tail, i):
    lane = iota(tail.shape, 1)
    return col(jnp.where((lane >= 3 * i) & (lane < 3 * i + 3), tail, 0.0))


def tiles_of(body):
    return [
        body[i : i + LINES, j : j + LANES]
        for i in range(0, body.shape[0], LINES)
        for j in range(0, body.shape[1], LANES)
    ]


def body_of(tiles, width):
    across = width // LANES
    lines = [
        jnp.concatenate(tiles[i : i + across], axis=1) for i in range(0, len(tiles), across)
    ]
    return jnp.concatenate(lines, axis=0) if len(lines) > 1 else lines[0]


def put(ref, tiles):
    for i, tile in enumerate(tiles):
        ref[i] = tile.astype(BF16)


def put_copies(ref, tiles):
    for i in range(ref.shape[0]):
        put(ref.at[i], tiles)


def tiles_in(ref):
    return [ref[i].astype(F32) for i in range(ref.shape[0])]


def summed(ref):
    totals = tiles_in(ref.at[0])
    for i in range(1, ref.shape[0]):
        totals = [a + b for a, b in zip(totals, tiles_in(ref.at[i]))]
    return totals


def own_first():
    me = lax.axis_index("samp")
    near = me // (LAYERS * CORES) * CORES + lax.rem(me, CORES)
    return near * LINES


def own_lines(ref):
    return ref[pl.ds(pl.multiple_of(own_first(), LINES), LINES), :]


def chosen_part(x, width):
    feat = lax.axis_index("feat")
    mine = x[:, :width]
    for i in range(1, x.shape[1] // width):
        mine = jnp.where(feat == i, x[:, i * width : (i + 1) * width], mine)
    return mine


def first_rows(grads, base, out, held, line, sems):
    loads = [
        pltpu.make_async_copy(base, line, sems.at[0]),
        pltpu.make_async_copy(grads, held, sems.at[1]),
    ]
    for load in loads:
        load.start()
    loads[0].wait()
    b = line[...]
    tail = tail_of(as_row(col(b * b)))
    packed = b.astype(BF16)
    loads[1].wait()
    put_copies(out, tiles_of(dot(packed, held[...], ((1,), (1,)))) + [tail])


def x_total(count, arrived, out):
    tiles = summed(arrived)
    tail = tail_of(*[row_in(tiles[-1], i) for i in range(count)])
    put(out, tiles[:-1] + [tail])


def weight_tiles(weights, curve):
    blocks = [weights[:, i : i + LANES] for i in range(0, weights.shape[1], LANES)]
    shape, n = (LINES, LANES), len(blocks)
    low, high = tail_of(as_row(curve)), jnp.zeros(shape, F32)
    line = iota(shape, 0)
    for i, x in enumerate(blocks):
        x = jnp.broadcast_to(x, shape)
        first = x.astype(BF16).astype(F32)
        second = (x - first).astype(BF16).astype(F32)
        high = jnp.where(line == i, first, jnp.where(line == n + i, second, high))
        low = jnp.where(line == 3 + i, x - first - second, low)
    return [low, high]


def weights_in(low, high, n):
    return jnp.concatenate(
        [high[i : i + 1] + high[n + i : n + i + 1] + low[3 + i : 4 + i] for i in range(n)], axis=1
    )


def first_image(grads, weights, mine, other, rows, norm, out):
    tiles = [a + b for a, b in zip(tiles_in(mine), tiles_in(other))]
    r = body_of(tiles[:-1], rows.shape[1])
    rows[...] = r
    norm[...] = row_in(tiles[-1], 0)
    w = weights[...]
    weighted = r * w
    image = tiles_of(dot(weighted, grads[...], ((1,), (0,))))
    extra = weight_tiles(w, col(weighted * r))
    across = len(image) // out.shape[0]
    for i in range(out.shape[0]):
        put(out.at[i], image[i * across : (i + 1) * across] + extra)


def near_total(arrived, weights, out):
    tiles = summed(arrived)
    put_copies(out, tiles[:-2] + [tail_of(row_in(tiles[-2], 0))])
    low, high = arrived.shape[1] - 2, arrived.shape[1] - 1
    n = len(tiles) - 2
    width = n * LANES
    for i in range(arrived.shape[0]):
        weights[:, i * width : (i + 1) * width] = weights_in(
            arrived[i, low].astype(F32), arrived[i, high].astype(F32), n
        )


def turn(base, norm, arrived, near_grads, resid, image, alpha, curve, out, held, sems):
    high = held.shape[0] // NEAR
    loads = [
        pltpu.make_async_copy(
            near_grads.at[pl.ds(i * high, high), :], held.at[pl.ds(i * high, high), :], sems.at[i]
        )
        for i in range(NEAR)
    ]
    for load in loads:
        load.start()
    tiles = summed(arrived)
    n = norm[...]
    c = row_in(tiles[-1], 0) + DAMPING * n
    a = n / c
    alpha[...] = a
    curve[...] = c
    b = own_lines(base)
    q = body_of(tiles[:-1], base.shape[1]) + DAMPING * b
    r = b - as_column(a, LINES, own_first()) * q
    resid[...] = r
    image[...] = q
    tail = column_tail(col(r * r), col(r * q))
    packed = r.astype(BF16)
    parts = []
    for i in range(NEAR):
        loads[i].wait()
        parts += tiles_of(dot(packed, held[i * high : (i + 1) * high], ((1,), (1,))))
    put_copies(out, parts + [tail])


def x_total_columns(arrived, out):
    tiles = summed(arrived)
    put(out, tiles[:-1] + [column_tail(*[column_in(tiles[-1], i) for i in range(2)])])


def next_image(near_grads, weights, mine, other, rows, sums, out):
    tiles = [a + b for a, b in zip(tiles_in(mine), tiles_in(other))]
    u = body_of(tiles[:-1], rows.shape[1])
    rows[...] = u
    sums[...] = tiles[-1]
    weighted = u * weights[...]
    image = tiles_of(dot(weighted, near_grads[...], ((1,), (0,))))
    put_copies(out, image + [column_tail(col(weighted * u))])


def last_step(norm, curve, resid, image, rows, sums, arrived, out):
    first = own_first()
    tiles = summed(arrived)
    n0, c0 = as_column(norm[...], LINES, first), as_column(curve[...], LINES, first)
    n1, cross = column_in(sums[...], 0), column_in(sums[...], 1)
    beta = n1 / n0
    own = column_in(tiles[-1], 0) + DAMPING * n1
    alpha = n1 / (own + 2.0 * beta * cross + beta * beta * c0)
    r = resid[...]
    q = body_of(tiles[:-1], r.shape[1]) + DAMPING * r + beta * image[...]
    body = tiles_of(r - alpha * q) + tiles_of(r)
    tail = column_tail(alpha, alpha * beta)
    width = r.shape[1]
    share = width // lax.axis_size("feat")
    for i in range(out.shape[0]):
        part = chosen_part(rows[:, i * width : (i + 1) * width], share)
        tile = jnp.concatenate([part, tail[:, : LANES - share]], axis=1)
        put(out.at[i], body + [tile])


def outputs(scale, base, alpha0, rows0, arrived, scores, answer, last, *scratch):
    score_held, answer_held, last_held, sems = scratch
    width, share = base.shape[1], scores.shape[0]
    near, across = arrived.shape[0], width // LANES
    tiles = [tiles_in(arrived.at[i]) for i in range(near)]
    last_held[...] = body_of([t for of in tiles for t in of[:across]], width)
    stores = [
        pltpu.make_async_copy(held, out, sems.at[i])
        for i, (held, out) in enumerate(
            ((last_held, last), (answer_held, answer), (score_held, scores))
        )
    ]
    stores[0].start()
    ends = jnp.concatenate([of[-1] for of in tiles], axis=0)
    u, tail = ends[:, :share], ends[:, share:]
    gain = column_in(tail, 0)
    held = as_column(alpha0[...], base.shape[0]) + column_in(tail, 1)
    resid = body_of([t for of in tiles for t in of[across : 2 * across]], width)
    answer_held[...] = held * base[...] + gain * resid
    stores[1].start()
    mine = held * chosen_part(rows0[...], share) + gain * u
    score_held[...] = (mine * scale).T
    stores[2].start()
    for store in stores:
        store.wait()


VMEM = pl.BlockSpec(memory_space=pltpu.VMEM)
HBM = pl.BlockSpec(memory_space=pltpu.HBM)


def call(kernel, outs, *args, inputs=None, results=VMEM, scratch=()):
    return pl.pallas_call(
        kernel,
        out_shape=[jax.ShapeDtypeStruct(s, t) for s, t in outs],
        in_specs=inputs or [VMEM] * len(args),
        out_specs=[results] * len(outs),
        scratch_shapes=list(scratch),
        compiler_params=pltpu.CompilerParams(vmem_limit_bytes=16 * 2**20),
    )(*args)


def exchanged(pieces, axis, groups):
    return lax.all_to_all(pieces, axis, 0, 0, tiled=True, axis_index_groups=groups)


def per_device(grads, weights, targets):
    n_samp, n_feat = lax.axis_size("samp"), lax.axis_size("feat")
    samples = grads.shape[0]
    share = samples // n_feat
    near_grads = lax.all_gather(grads, "samp", axis_index_groups=NEAR_GROUPS, axis=0, tiled=True)
    scaled = (weights / (samples * n_samp))[None, :]
    base = targets.T
    dirs, m = base.shape
    across = m // LANES
    row_tiles = dirs // LINES * (samples // LANES) + 1
    block, row, part = ((dirs, m), F32), ((1, LANES), F32), ((LINES, m), F32)
    to_x = ((COLUMNS, row_tiles, LINES, LANES), BF16)
    to_half = ((row_tiles, LINES, LANES), BF16)
    to_near = ((NEAR, across + 2, LINES, LANES), BF16)
    to_far = ((LAYERS, across + 1, LINES, LANES), BF16)
    to_all = ((NEAR, 2 * across + 1, LINES, LANES), BF16)

    out, held, base = call(
        first_rows,
        [to_x, (grads.shape, grads.dtype), block],
        pltpu.with_memory_space_constraint(grads, pltpu.HBM),
        pltpu.with_memory_space_constraint(base, pltpu.HBM),
        inputs=[HBM, HBM],
        scratch=[pltpu.SemaphoreType.DMA((2,))],
    )
    (mine,) = call(functools.partial(x_total, 1), [to_half], exchanged(out, "feat", X_GROUPS))
    other = lax.ppermute(mine, "feat", SWAP)
    rows0, norm0, out = call(
        first_image, [((dirs, samples), F32), row, to_near], held, scaled, mine, other
    )
    near_weights, out = call(
        near_total,
        [((1, NEAR * samples), F32), to_far],
        exchanged(out, "samp", NEAR_GROUPS),
    )
    resid, image, alpha0, curve0, out, held = call(
        turn,
        [part, part, row, row, to_x, ((NEAR * samples, m), grads.dtype)],
        base,
        norm0,
        exchanged(out, "samp", FAR_GROUPS),
        pltpu.with_memory_space_constraint(near_grads, pltpu.HBM),
        inputs=[VMEM, VMEM, VMEM, HBM],
        scratch=[pltpu.SemaphoreType.DMA((NEAR,))],
    )
    (mine,) = call(x_total_columns, [to_half], exchanged(out, "feat", X_GROUPS))
    other = lax.ppermute(mine, "feat", SWAP)
    rows1, sums, out = call(
        next_image,
        [((LINES, NEAR * samples), F32), ((LINES, LANES), F32), to_far],
        held,
        near_weights,
        mine,
        other,
    )
    (out,) = call(
        last_step,
        [to_all],
        norm0,
        curve0,
        resid,
        image,
        rows1,
        sums,
        exchanged(out, "samp", FAR_GROUPS),
    )
    scores, answer, last = call(
        functools.partial(outputs, 1.0 / math.sqrt(m * n_feat)),
        [((share, dirs), F32), block, block],
        base,
        alpha0,
        rows0,
        exchanged(out, "samp", NEAR_GROUPS),
        results=HBM,
        scratch=[
            pltpu.VMEM((share, dirs), F32),
            pltpu.VMEM((dirs, m), F32),
            pltpu.VMEM((dirs, m), F32),
            pltpu.SemaphoreType.DMA((3,)),
        ],
    )
    return scores, answer.T, last.T


def solution(mesh):
    return jax.shard_map(
        per_device,
        mesh=mesh,
        in_specs=(P("samp", "feat"), P("samp"), P("feat", None)),
        out_specs=(P(("samp", "feat"), None), P("feat", None), P("feat", None)),
        check_vma=False,
    )
```

time: 131 us -> 134 us (1.023)
  blocking collectives: 92.6 us -> 79.1 us
  between operations: 0.7 us -> 14.1 us
  Pallas kernels: 4.37 us -> 7.43 us
    all_to_all x8 -> x6, blocking collectives: 92.6 us -> 79.1 us  [exchanged(): lax.all_to_all(pieces, axis, 0, 0, tiled=True, axis_index_groups=groups)]
    pallas_call x11 -> x9, Pallas kernels: 4.37 us -> 7.43 us  [call(): pl.pallas_call(kernel, out_shape=[jax.ShapeDtypeStruct(s, t) for s, t in...]
  transfers between devices with their start and end apart: 2 -> 3, of which waited for: 2 -> 2; matrix products, arithmetic and copies ran while one was open for 0% -> 1% of each run, Pallas kernels for 0% -> 1%
where the time goes in v4:
time: 134 us; the launch traced here: 133 us
  blocking collectives  79.1 us (59%)
  starting transfers between devices  22.9 us (17%)
  between operations  14.1 us (11%)
  waiting for transfers between devices  9.11 us (7%)
  Pallas kernels  7.43 us (6%)
    all_to_all x6, blocking collectives, exchanged(): lax.all_to_all(pieces, axis, 0, 0, tiled=True, axis_index_groups=groups)  79.1 us
    ppermute x2, starting transfers between devices, per_device(): other = lax.ppermute(mine, 'feat', SWAP)  22.9 us
    ppermute x2, waiting for transfers between devices, per_device(): other = lax.ppermute(mine, 'feat', SWAP)  8.43 us
    pallas_call x9, Pallas kernels, call(): pl.pallas_call(kernel, out_shape=[jax.ShapeDtypeStruct(s, t) for s, t in...  7.43 us
  transfers between devices with their start and end apart: 3, of which 2 were waited for; matrix products, arithmetic and copies ran while one was open for 1% of the time, Pallas kernels for 1%

profile of v4, /device:TPU:1, one launch (start us, length us, event | category | flops | bytes accessed | tf_op | source)
XLA Modules:
  0.0 133.3 jit_solution(1840594718032044780)
XLA Ops:
  7.2 0.0 all-gather.2.cloned.1.call-start
  7.2 0.7 all-gather.2.cloned.1.call-update
  7.9 1.4 %shard_map.58 = (bf16[4,33,8,128]{3,2,1,0:T(8,128)(2,1)S(1)}, bf16[512,512]{1,0:T(8,128)(2,1)S(1)}, f32[64,512]{1,0:T(8,128)S(1)}) custom-call(bf16[512,512]{1,0:T(8,128)(2,1)} %grads.1, f32[64,512]{1,0:T(8,128)} %bitcast.5), custom_call_target="tpu_custom_call" | custom-call | tf_op jit(solution)/shard_map/pallas_call | solution.py:309
  9.3 10.2 %all_to_all.30.arrived = bf16[4,33,8,128]{3,2,1,0:T(8,128)(2,1)S(1)} all-to-all(bf16[4,33,8,128]{3,2,1,0:T(8,128)(2,1)S(1)} %get-tuple-element.25), channel_id=1, replica_groups={{0,1,2,3},{4,5,6,7},{8,9,10,11},{12,13,14,15},{16,17,18,19},{20,21,22,2..., dimensions={0} | all-to-all | bytes 540672 | tf_op jit(solution)/shard_map/all_to_all | solution.py:320
  19.5 0.1 shard_map.59.mine
  19.6 15.5 %collective-permute-start = (bf16[33,8,128]{2,1,0:T(8,128)(2,1)S(1)}, bf16[33,8,128]{2,1,0:T(8,128)(2,1)S(1)}, u32[]{:S(2)}, u32[]{:S(2)}) collective-permute-start(bf16[33,8,128]{2,1,0:T(8,128)(2,1)S(1)} %shard_map.59.mine), channel_id=1, source_target_pairs={{0,4},{1,5},{2,6},{3,7},{4,0},{5,1},{6,2},{7,3},{8,12},{9,13},{10,... | collective-permute-start | bytes 202760 | tf_op jit(solution)/shard_map/ppermute | solution.py:349
  35.1 0.7 broadcast_multiply_fusion
  35.7 1.0 collective-permute-done.other
  36.7 0.2 shard_map.60
  36.9 14.2 %all_to_all.31.arrived = bf16[8,6,8,128]{3,2,1,0:T(8,128)(2,1)S(1)} all-to-all(bf16[8,6,8,128]{3,2,1,0:T(8,128)(2,1)S(1)} %get-tuple-element.27), channel_id=1, replica_groups={{0,8,128,136,256,264,384,392},{16,24,144,152,272,280,400,408},{32,40,16..., dimensions={0} | all-to-all | bytes 196608 | tf_op jit(solution)/shard_map/all_to_all | solution.py:320
  51.1 19.5 %all_to_all.32.arrived = bf16[8,5,8,128]{3,2,1,0:T(8,128)(2,1)S(1)} all-to-all(bf16[8,5,8,128]{3,2,1,0:T(8,128)(2,1)S(1)} %get-tuple-element.28), channel_id=1, replica_groups={{0,16,32,48,64,80,96,112},{8,24,40,56,72,88,104,120},{128,144,160,176,1..., dimensions={0} | all-to-all | bytes 163840 | tf_op jit(solution)/shard_map/all_to_all | solution.py:320
  70.6 0.0 all-gather.2.cloned.1.call-done.near_grads
  70.6 3.1 %shard_map.62 = (f32[8,512]{1,0:T(8,128)S(1)}, f32[8,512]{1,0:T(8,128)S(1)}, f32[1,128]{1,0:T(1,128)S(1)}, f32[1,128]{1,0:T(1,128)S(1)}, bf16[4,33,8,128]{3,2,1,...) custom-call(f32[64,512]{1,0:T(8,128)S(1)} %get-tuple-element.23.base, f32[1,128]{1,0:T(1,128)S(1)} %get-tuple-element.26.norm, ...), custom_call_target="tpu_custom_call" | custom-call | tf_op jit(solution)/shard_map/pallas_call | solution.py:309
  73.8 8.0 %all_to_all.33.arrived = bf16[4,33,8,128]{3,2,1,0:T(8,128)(2,1)S(1)} all-to-all(bf16[4,33,8,128]{3,2,1,0:T(8,128)(2,1)S(1)} %get-tuple-element.36), channel_id=1, replica_groups={{0,1,2,3},{4,5,6,7},{8,9,10,11},{12,13,14,15},{16,17,18,19},{20,21,22,2..., dimensions={0} | all-to-all | bytes 540672 | tf_op jit(solution)/shard_map/all_to_all | solution.py:320
  81.8 0.1 shard_map.63.mine
  81.8 7.4 %collective-permute-start.1 = (bf16[33,8,128]{2,1,0:T(8,128)(2,1)S(1)}, bf16[33,8,128]{2,1,0:T(8,128)(2,1)S(1)}, u32[]{:S(2)}, u32[]{:S(2)}) collective-permute-start(bf16[33,8,128]{2,1,0:T(8,128)(2,1)S(1)} %shard_map.63.mine), channel_id=1, source_target_pairs={{0,4},{1,5},{2,6},{3,7},{4,0},{5,1},{6,2},{7,3},{8,12},{9,13},{10,... | collective-permute-start | bytes 202760 | tf_op jit(solution)/shard_map/ppermute | solution.py:369
  89.3 7.5 %collective-permute-done.1.other = bf16[33,8,128]{2,1,0:T(8,128)(2,1)S(1)} collective-permute-done((bf16[33,8,128]{2,1,0:T(8,128)(2,1)S(1)}, bf16[33,8,128]{2,1,0:T(8,128)(2,1)S(1)}, u32[]{:S(2)}, u32[]{:S(2)}) %collective-permute-start.1) | collective-permute-done | bytes 67616 | tf_op jit(solution)/shard_map/ppermute | solution.py:369
  96.7 0.6 shard_map.64
  97.4 12.6 %all_to_all.34.arrived = bf16[8,5,8,128]{3,2,1,0:T(8,128)(2,1)S(1)} all-to-all(bf16[8,5,8,128]{3,2,1,0:T(8,128)(2,1)S(1)} %get-tuple-element.39), channel_id=1, replica_groups={{0,16,32,48,64,80,96,112},{8,24,40,56,72,88,104,120},{128,144,160,176,1..., dimensions={0} | all-to-all | bytes 163840 | tf_op jit(solution)/shard_map/all_to_all | solution.py:320
  110.0 0.6 shard_map.65
  110.6 14.6 %all_to_all.35.arrived = bf16[8,9,8,128]{3,2,1,0:T(8,128)(2,1)S(1)} all-to-all(bf16[8,9,8,128]{3,2,1,0:T(8,128)(2,1)S(1)} %shard_map.65), channel_id=1, replica_groups={{0,8,128,136,256,264,384,392},{16,24,144,152,272,280,400,408},{32,40,16..., dimensions={0} | all-to-all | bytes 294912 | tf_op jit(solution)/shard_map/all_to_all | solution.py:320
  125.1 1.3 shard_map.66
  (1 shorter events, 0.0 us)
Async XLA Ops:
  7.2 63.5 %all-gather.2.cloned.1.call-start = ((), (), s32[]{:S(2)}) async-start(), calls=%async_computation.6 | async-start | bytes 4718592 | tf_op jit(solution)/shard_map/all_gather | solution.py:327
  19.6 17.1 %collective-permute-start = (bf16[33,8,128]{2,1,0:T(8,128)(2,1)S(1)}, bf16[33,8,128]{2,1,0:T(8,128)(2,1)S(1)}, u32[]{:S(2)}, u32[]{:S(2)}) collective-permute-start(bf16[33,8,128]{2,1,0:T(8,128)(2,1)S(1)} %shard_map.59.mine), channel_id=1, source_target_pairs={{0,4},{1,5},{2,6},{3,7},{4,0},{5,1},{6,2},{7,3},{8,12},{9,13},{10,... | collective-permute-start | bytes 202760 | tf_op jit(solution)/shard_map/ppermute | solution.py:349
  81.8 14.9 %collective-permute-start.1 = (bf16[33,8,128]{2,1,0:T(8,128)(2,1)S(1)}, bf16[33,8,128]{2,1,0:T(8,128)(2,1)S(1)}, u32[]{:S(2)}, u32[]{:S(2)}) collective-permute-start(bf16[33,8,128]{2,1,0:T(8,128)(2,1)S(1)} %shard_map.63.mine), channel_id=1, source_target_pairs={{0,4},{1,5},{2,6},{3,7},{4,0},{5,1},{6,2},{7,3},{8,12},{9,13},{10,... | collective-permute-start | bytes 202760 | tf_op jit(solution)/shard_map/ppermute | solution.py:369
Sparse Core Ops, SparseCore 0:
  10.2 46.5 all-gather.1

commit v5 on v3

--- a/solution.py
+++ b/solution.py
@@ -13,7 +13,6 @@
 HALVES, COLUMNS = 2, 4
 NEAR = PLANES * CORES
 LINES, LANES = 8, 128
-CHUNKS = 4
 
 X_GROUPS = [[h * COLUMNS + i for i in range(COLUMNS)] for h in range(HALVES)]
 SWAP = [(i, (i + COLUMNS) % (HALVES * COLUMNS)) for i in range(HALVES * COLUMNS)]
@@ -126,10 +125,9 @@
 
 
 def first_rows(grads, base, out, held, line, sems):
-    high = held.shape[1]
-    loads = [pltpu.make_async_copy(base, line, sems.at[CHUNKS])] + [
-        pltpu.make_async_copy(grads.at[pl.ds(i * high, high), :], held.at[i], sems.at[i])
-        for i in range(CHUNKS)
+    loads = [
+        pltpu.make_async_copy(base, line, sems.at[0]),
+        pltpu.make_async_copy(grads, held, sems.at[1]),
     ]
     for load in loads:
         load.start()
@@ -137,11 +135,8 @@
     b = line[...]
     tail = tail_of(as_row(col(b * b)))
     packed = b.astype(BF16)
-    parts = []
-    for i in range(CHUNKS):
-        loads[i + 1].wait()
-        parts.append(dot(packed, held[i], ((1,), (1,))))
-    put_copies(out, tiles_of(jnp.concatenate(parts, axis=1)) + [tail])
+    loads[1].wait()
+    put_copies(out, tiles_of(dot(packed, held[...], ((1,), (1,)))) + [tail])
 
 
 def x_total(count, arrived, out):
@@ -278,17 +273,13 @@
     to_far = ((LAYERS, across + 1, LINES, LANES), BF16)
     to_all = ((NEAR, across, LINES, LANES), BF16)
 
-    (out,) = call(
+    out, grads, base = call(
         first_rows,
-        [to_x],
+        [to_x, (grads.shape, grads.dtype), block],
         pltpu.with_memory_space_constraint(grads, pltpu.HBM),
         pltpu.with_memory_space_constraint(base, pltpu.HBM),
         inputs=HBM,
-        scratch=[
-            pltpu.VMEM((CHUNKS, samples // CHUNKS, m), BF16),
-            pltpu.VMEM((dirs, m), F32),
-            pltpu.SemaphoreType.DMA((CHUNKS + 1,)),
-        ],
+        scratch=[pltpu.SemaphoreType.DMA((2,))],
     )
     (mine,) = call(functools.partial(x_total, 1), [to_half], exchanged(out, "feat", X_GROUPS))
     other = lax.ppermute(mine, "feat", SWAP)

time: 131 us -> 130 us (level)
  no operation moved by 1% of the time
where the time goes in v5:
time: 130 us; the launch traced here: 129 us
  blocking collectives  92.3 us (71%)
  starting transfers between devices  22.9 us (18%)
  waiting for transfers between devices  9.51 us (7%)
  Pallas kernels  3.93 us (3%)
    all_to_all x8, blocking collectives, exchanged(): lax.all_to_all(pieces, axis, 0, 0, tiled=True, axis_index_groups=groups)  92.3 us
    ppermute x2, starting transfers between devices, per_device(): other = lax.ppermute(mine, 'feat', SWAP)  22.9 us
    ppermute x2, waiting for transfers between devices, per_device(): other = lax.ppermute(mine, 'feat', SWAP)  9.51 us
    pallas_call x11, Pallas kernels, call(): pl.pallas_call(kernel, out_shape=[jax.ShapeDtypeStruct(s, t) for s, t in...  3.93 us
  transfers between devices with their start and end apart: 2, of which 2 were waited for; matrix products, arithmetic and copies ran while one was open for 0% of the time, Pallas kernels for 0%

profile of v5, /device:TPU:1, one launch (start us, length us, event | category | flops | bytes accessed | tf_op | source)
XLA Modules:
  0.0 129.4 jit_solution(616696197136388034)
XLA Ops:
  0.6 1.4 %shard_map.58 = (bf16[4,33,8,128]{3,2,1,0:T(8,128)(2,1)S(1)}, bf16[512,512]{1,0:T(8,128)(2,1)S(1)}, f32[64,512]{1,0:T(8,128)S(1)}) custom-call(bf16[512,512]{1,0:T(8,128)(2,1)} %grads.1, f32[64,512]{1,0:T(8,128)} %bitcast.6), custom_call_target="tpu_custom_call" | custom-call | tf_op jit(solution)/shard_map/pallas_call | solution.py:245
  2.1 10.2 %all_to_all.40.arrived = bf16[4,33,8,128]{3,2,1,0:T(8,128)(2,1)S(1)} all-to-all(bf16[4,33,8,128]{3,2,1,0:T(8,128)(2,1)S(1)} %get-tuple-element.26), channel_id=1, replica_groups={{0,1,2,3},{4,5,6,7},{8,9,10,11},{12,13,14,15},{16,17,18,19},{20,21,22,2..., dimensions={0} | all-to-all | bytes 540672 | tf_op jit(solution)/shard_map/all_to_all | solution.py:256
  12.3 0.0 copy-start
  12.3 0.1 shard_map.59.mine
  12.3 15.5 %collective-permute-start = (bf16[33,8,128]{2,1,0:T(8,128)(2,1)S(1)}, bf16[33,8,128]{2,1,0:T(8,128)(2,1)S(1)}, u32[]{:S(2)}, u32[]{:S(2)}) collective-permute-start(bf16[33,8,128]{2,1,0:T(8,128)(2,1)S(1)} %shard_map.59.mine), channel_id=1, source_target_pairs={{0,4},{1,5},{2,6},{3,7},{4,0},{5,1},{6,2},{7,3},{8,12},{9,13},{10,... | collective-permute-start | bytes 202760 | tf_op jit(solution)/shard_map/ppermute | solution.py:285
  27.8 0.0 copy-done
  27.8 1.6 %collective-permute-done.other = bf16[33,8,128]{2,1,0:T(8,128)(2,1)S(1)} collective-permute-done((bf16[33,8,128]{2,1,0:T(8,128)(2,1)S(1)}, bf16[33,8,128]{2,1,0:T(8,128)(2,1)S(1)}, u32[]{:S(2)}, u32[]{:S(2)}) %collective-permute-start) | collective-permute-done | bytes 67616 | tf_op jit(solution)/shard_map/ppermute | solution.py:285
  29.4 0.2 shard_map.60
  29.7 12.9 %all_to_all.41.arrived = bf16[8,5,8,128]{3,2,1,0:T(8,128)(2,1)S(1)} all-to-all(bf16[8,5,8,128]{3,2,1,0:T(8,128)(2,1)S(1)} %get-tuple-element.28), channel_id=1, replica_groups={{0,8,128,136,256,264,384,392},{16,24,144,152,272,280,400,408},{32,40,16..., dimensions={0} | all-to-all | bytes 163840 | tf_op jit(solution)/shard_map/all_to_all | solution.py:256
  42.6 19.5 %all_to_all.42.arrived = bf16[8,5,8,128]{3,2,1,0:T(8,128)(2,1)S(1)} all-to-all(bf16[8,5,8,128]{3,2,1,0:T(8,128)(2,1)S(1)} %shard_map.61), channel_id=1, replica_groups={{0,16,32,48,64,80,96,112},{8,24,40,56,72,88,104,120},{128,144,160,176,1..., dimensions={0} | all-to-all | bytes 163840 | tf_op jit(solution)/shard_map/all_to_all | solution.py:256
  62.2 0.1 shard_map.62
  62.3 9.4 %all_to_all.43.arrived = bf16[8,4,8,128]{3,2,1,0:T(8,128)(2,1)S(1)} all-to-all(bf16[8,4,8,128]{3,2,1,0:T(8,128)(2,1)S(1)} %get-tuple-element.29), channel_id=1, replica_groups={{0,8,128,136,256,264,384,392},{16,24,144,152,272,280,400,408},{32,40,16..., dimensions={0} | all-to-all | bytes 131072 | tf_op jit(solution)/shard_map/all_to_all | solution.py:256
  71.7 0.3 shard_map.63
  72.0 8.1 %all_to_all.44.arrived = bf16[4,33,8,128]{3,2,1,0:T(8,128)(2,1)S(1)} all-to-all(bf16[4,33,8,128]{3,2,1,0:T(8,128)(2,1)S(1)} %get-tuple-element.31), channel_id=1, replica_groups={{0,1,2,3},{4,5,6,7},{8,9,10,11},{12,13,14,15},{16,17,18,19},{20,21,22,2..., dimensions={0} | all-to-all | bytes 540672 | tf_op jit(solution)/shard_map/all_to_all | solution.py:256
  80.1 0.1 shard_map.64.mine
  80.2 7.4 %collective-permute-start.1 = (bf16[33,8,128]{2,1,0:T(8,128)(2,1)S(1)}, bf16[33,8,128]{2,1,0:T(8,128)(2,1)S(1)}, u32[]{:S(2)}, u32[]{:S(2)}) collective-permute-start(bf16[33,8,128]{2,1,0:T(8,128)(2,1)S(1)} %shard_map.64.mine), channel_id=1, source_target_pairs={{0,4},{1,5},{2,6},{3,7},{4,0},{5,1},{6,2},{7,3},{8,12},{9,13},{10,... | collective-permute-start | bytes 202760 | tf_op jit(solution)/shard_map/ppermute | solution.py:297
  87.6 7.9 %collective-permute-done.1.other = bf16[33,8,128]{2,1,0:T(8,128)(2,1)S(1)} collective-permute-done((bf16[33,8,128]{2,1,0:T(8,128)(2,1)S(1)}, bf16[33,8,128]{2,1,0:T(8,128)(2,1)S(1)}, u32[]{:S(2)}, u32[]{:S(2)}) %collective-permute-start.1) | collective-permute-done | bytes 67616 | tf_op jit(solution)/shard_map/ppermute | solution.py:297
  95.5 0.3 shard_map.65
  95.7 9.2 %all_to_all.45.arrived = bf16[8,5,8,128]{3,2,1,0:T(8,128)(2,1)S(1)} all-to-all(bf16[8,5,8,128]{3,2,1,0:T(8,128)(2,1)S(1)} %get-tuple-element.38), channel_id=1, replica_groups={{0,8,128,136,256,264,384,392},{16,24,144,152,272,280,400,408},{32,40,16..., dimensions={0} | all-to-all | bytes 163840 | tf_op jit(solution)/shard_map/all_to_all | solution.py:256
  105.0 13.5 %all_to_all.46.arrived = bf16[8,5,8,128]{3,2,1,0:T(8,128)(2,1)S(1)} all-to-all(bf16[8,5,8,128]{3,2,1,0:T(8,128)(2,1)S(1)} %shard_map.66), channel_id=1, replica_groups={{0,16,32,48,64,80,96,112},{8,24,40,56,72,88,104,120},{128,144,160,176,1..., dimensions={0} | all-to-all | bytes 163840 | tf_op jit(solution)/shard_map/all_to_all | solution.py:256
  118.4 0.1 shard_map.67
  118.5 9.4 %all_to_all.47.arrived = bf16[8,4,8,128]{3,2,1,0:T(8,128)(2,1)S(1)} all-to-all(bf16[8,4,8,128]{3,2,1,0:T(8,128)(2,1)S(1)} %get-tuple-element.41), channel_id=1, replica_groups={{0,8,128,136,256,264,384,392},{16,24,144,152,272,280,400,408},{32,40,16..., dimensions={0} | all-to-all | bytes 131072 | tf_op jit(solution)/shard_map/all_to_all | solution.py:256
  128.0 1.4 %shard_map.68 = (f32[64,64]{1,0:T(8,128)}, f32[64,512]{1,0:T(8,128)}, f32[64,512]{1,0:T(8,128)}) custom-call(f32[64,512]{1,0:T(8,128)S(1)} %get-tuple-element.24.base, f32[64,512]{1,0:T(8,128)S(1)} %get-tuple-element.30.resid, f32[1,128]{1,0:T(1,128)S(1)} %get-tuple-element.33.beta, f32[1,128]{1,0:T(1,128)S(1)} %get-tuple-element.34.alpha0, ...), custom_call_target="tpu_custom_call" | custom-call | tf_op jit(solution)/shard_map/pallas_call | solution.py:245
  (3 shorter events, 0.1 us)
Async XLA Ops:
  12.3 15.5 %copy-start = (f32[512]{0:T(512)S(1)}, f32[512]{0:T(512)}, u32[]{:S(2)}) copy-start(f32[512]{0:T(512)} %param.4) | copy-start | bytes 6148
  12.3 17.1 %collective-permute-start = (bf16[33,8,128]{2,1,0:T(8,128)(2,1)S(1)}, bf16[33,8,128]{2,1,0:T(8,128)(2,1)S(1)}, u32[]{:S(2)}, u32[]{:S(2)}) collective-permute-start(bf16[33,8,128]{2,1,0:T(8,128)(2,1)S(1)} %shard_map.59.mine), channel_id=1, source_target_pairs={{0,4},{1,5},{2,6},{3,7},{4,0},{5,1},{6,2},{7,3},{8,12},{9,13},{10,... | collective-permute-start | bytes 202760 | tf_op jit(solution)/shard_map/ppermute | solution.py:285
  80.2 15.3 %collective-permute-start.1 = (bf16[33,8,128]{2,1,0:T(8,128)(2,1)S(1)}, bf16[33,8,128]{2,1,0:T(8,128)(2,1)S(1)}, u32[]{:S(2)}, u32[]{:S(2)}) collective-permute-start(bf16[33,8,128]{2,1,0:T(8,128)(2,1)S(1)} %shard_map.64.mine), channel_id=1, source_target_pairs={{0,4},{1,5},{2,6},{3,7},{4,0},{5,1},{6,2},{7,3},{8,12},{9,13},{10,... | collective-permute-start | bytes 202760 | tf_op jit(solution)/shard_map/ppermute | solution.py:297

commit v6 on v5

--- a/solution.py
+++ b/solution.py
@@ -16,14 +16,11 @@
 
 X_GROUPS = [[h * COLUMNS + i for i in range(COLUMNS)] for h in range(HALVES)]
 SWAP = [(i, (i + COLUMNS) % (HALVES * COLUMNS)) for i in range(HALVES * COLUMNS)]
-NEAR_GROUPS = [
-    [(y * LAYERS + z) * CORES + c for y in range(PLANES) for c in range(CORES)]
-    for z in range(LAYERS)
-]
+FAR_ORDER = (3, 7, 0, 6, 1, 5, 2, 4)
+NEAR_ORDER = ((0, 1), (0, 0), (1, 0), (3, 1), (2, 1), (2, 0), (1, 1), (3, 0))
+NEAR_GROUPS = [[(y * LAYERS + z) * CORES + c for y, c in NEAR_ORDER] for z in range(LAYERS)]
 FAR_GROUPS = [
-    [(y * LAYERS + z) * CORES + c for z in range(LAYERS)]
-    for y in range(PLANES)
-    for c in range(CORES)
+    [(y * LAYERS + z) * CORES + c for z in FAR_ORDER] for y in range(PLANES) for c in range(CORES)
 ]
 F32, BF16 = jnp.float32, jnp.bfloat16
 
@@ -109,8 +106,11 @@
 
 def own_first():
     me = lax.axis_index("samp")
-    near = me // (LAYERS * CORES) * CORES + lax.rem(me, CORES)
-    return near * LINES
+    y, c = me // (LAYERS * CORES), lax.rem(me, CORES)
+    first = jnp.int32(0)
+    for place, (plane, core) in enumerate(NEAR_ORDER):
+        first = jnp.where((y == plane) & (c == core), place * LINES, first)
+    return first
 
 
 def own_lines(ref):

time: 130 us -> 126 us (0.969)
  blocking collectives: 92.3 us -> 90 us
  waiting for transfers between devices: 9.51 us -> 7.61 us
    all_to_all x8, blocking collectives: 92.3 us -> 90 us  [exchanged(): lax.all_to_all(pieces, axis, 0, 0, tiled=True, axis_index_groups=groups)]
    ppermute x2, waiting for transfers between devices: 9.51 us -> 7.61 us  [per_device(): other = lax.ppermute(mine, 'feat', SWAP)]
where the time goes in v6:
time: 126 us; the launch traced here: 125 us
  blocking collectives  90 us (71%)
  starting transfers between devices  23.2 us (18%)
  waiting for transfers between devices  7.61 us (6%)
  Pallas kernels  3.93 us (3%)
    all_to_all x8, blocking collectives, exchanged(): lax.all_to_all(pieces, axis, 0, 0, tiled=True, axis_index_groups=groups)  90 us
    ppermute x2, starting transfers between devices, per_device(): other = lax.ppermute(mine, 'feat', SWAP)  23.2 us
    ppermute x2, waiting for transfers between devices, per_device(): other = lax.ppermute(mine, 'feat', SWAP)  7.61 us
    pallas_call x11, Pallas kernels, call(): pl.pallas_call(kernel, out_shape=[jax.ShapeDtypeStruct(s, t) for s, t in...  3.93 us
  transfers between devices with their start and end apart: 2, of which 2 were waited for; matrix products, arithmetic and copies ran while one was open for 0% of the time, Pallas kernels for 0%

profile of v6, /device:TPU:1, one launch (start us, length us, event | category | flops | bytes accessed | tf_op | source)
XLA Modules:
  0.0 125.4 jit_solution(7123734419268122836)
XLA Ops:
  0.6 1.4 %shard_map.58 = (bf16[4,33,8,128]{3,2,1,0:T(8,128)(2,1)S(1)}, bf16[512,512]{1,0:T(8,128)(2,1)S(1)}, f32[64,512]{1,0:T(8,128)S(1)}) custom-call(bf16[512,512]{1,0:T(8,128)(2,1)} %grads.1, f32[64,512]{1,0:T(8,128)} %bitcast.6), custom_call_target="tpu_custom_call" | custom-call | tf_op jit(solution)/shard_map/pallas_call | solution.py:245
  2.1 10.2 %all_to_all.40.arrived = bf16[4,33,8,128]{3,2,1,0:T(8,128)(2,1)S(1)} all-to-all(bf16[4,33,8,128]{3,2,1,0:T(8,128)(2,1)S(1)} %get-tuple-element.26), channel_id=1, replica_groups={{0,1,2,3},{4,5,6,7},{8,9,10,11},{12,13,14,15},{16,17,18,19},{20,21,22,2..., dimensions={0} | all-to-all | bytes 540672 | tf_op jit(solution)/shard_map/all_to_all | solution.py:256
  12.3 0.0 copy-start
  12.3 0.1 shard_map.59.mine
  12.3 15.5 %collective-permute-start = (bf16[33,8,128]{2,1,0:T(8,128)(2,1)S(1)}, bf16[33,8,128]{2,1,0:T(8,128)(2,1)S(1)}, u32[]{:S(2)}, u32[]{:S(2)}) collective-permute-start(bf16[33,8,128]{2,1,0:T(8,128)(2,1)S(1)} %shard_map.59.mine), channel_id=1, source_target_pairs={{0,4},{1,5},{2,6},{3,7},{4,0},{5,1},{6,2},{7,3},{8,12},{9,13},{10,... | collective-permute-start | bytes 202760 | tf_op jit(solution)/shard_map/ppermute | solution.py:285
  27.8 0.0 copy-done
  27.8 1.6 %collective-permute-done.other = bf16[33,8,128]{2,1,0:T(8,128)(2,1)S(1)} collective-permute-done((bf16[33,8,128]{2,1,0:T(8,128)(2,1)S(1)}, bf16[33,8,128]{2,1,0:T(8,128)(2,1)S(1)}, u32[]{:S(2)}, u32[]{:S(2)}) %collective-permute-start) | collective-permute-done | bytes 67616 | tf_op jit(solution)/shard_map/ppermute | solution.py:285
  29.4 0.2 shard_map.60
  29.7 12.8 %all_to_all.41.arrived = bf16[8,5,8,128]{3,2,1,0:T(8,128)(2,1)S(1)} all-to-all(bf16[8,5,8,128]{3,2,1,0:T(8,128)(2,1)S(1)} %get-tuple-element.28), channel_id=1, replica_groups={{8,0,128,392,264,256,136,384},{24,16,144,408,280,272,152,400},{40,32,16..., dimensions={0} | all-to-all | bytes 163840 | tf_op jit(solution)/shard_map/all_to_all | solution.py:256
  42.5 16.8 %all_to_all.42.arrived = bf16[8,5,8,128]{3,2,1,0:T(8,128)(2,1)S(1)} all-to-all(bf16[8,5,8,128]{3,2,1,0:T(8,128)(2,1)S(1)} %shard_map.61), channel_id=1, replica_groups={{48,112,0,96,16,80,32,64},{56,120,8,104,24,88,40,72},{176,240,128,224,1..., dimensions={0} | all-to-all | bytes 163840 | tf_op jit(solution)/shard_map/all_to_all | solution.py:256
  59.3 0.1 shard_map.62
  59.4 8.8 %all_to_all.43.arrived = bf16[8,4,8,128]{3,2,1,0:T(8,128)(2,1)S(1)} all-to-all(bf16[8,4,8,128]{3,2,1,0:T(8,128)(2,1)S(1)} %get-tuple-element.29), channel_id=1, replica_groups={{8,0,128,392,264,256,136,384},{24,16,144,408,280,272,152,400},{40,32,16..., dimensions={0} | all-to-all | bytes 131072 | tf_op jit(solution)/shard_map/all_to_all | solution.py:256
  68.2 0.3 shard_map.63
  68.5 8.1 %all_to_all.44.arrived = bf16[4,33,8,128]{3,2,1,0:T(8,128)(2,1)S(1)} all-to-all(bf16[4,33,8,128]{3,2,1,0:T(8,128)(2,1)S(1)} %get-tuple-element.31), channel_id=1, replica_groups={{0,1,2,3},{4,5,6,7},{8,9,10,11},{12,13,14,15},{16,17,18,19},{20,21,22,2..., dimensions={0} | all-to-all | bytes 540672 | tf_op jit(solution)/shard_map/all_to_all | solution.py:256
  76.6 0.1 shard_map.64.mine
  76.6 7.8 %collective-permute-start.1 = (bf16[33,8,128]{2,1,0:T(8,128)(2,1)S(1)}, bf16[33,8,128]{2,1,0:T(8,128)(2,1)S(1)}, u32[]{:S(2)}, u32[]{:S(2)}) collective-permute-start(bf16[33,8,128]{2,1,0:T(8,128)(2,1)S(1)} %shard_map.64.mine), channel_id=1, source_target_pairs={{0,4},{1,5},{2,6},{3,7},{4,0},{5,1},{6,2},{7,3},{8,12},{9,13},{10,... | collective-permute-start | bytes 202760 | tf_op jit(solution)/shard_map/ppermute | solution.py:297
  84.4 6.0 %collective-permute-done.1.other = bf16[33,8,128]{2,1,0:T(8,128)(2,1)S(1)} collective-permute-done((bf16[33,8,128]{2,1,0:T(8,128)(2,1)S(1)}, bf16[33,8,128]{2,1,0:T(8,128)(2,1)S(1)}, u32[]{:S(2)}, u32[]{:S(2)}) %collective-permute-start.1) | collective-permute-done | bytes 67616 | tf_op jit(solution)/shard_map/ppermute | solution.py:297
  90.4 0.3 shard_map.65
  90.7 13.2 %all_to_all.45.arrived = bf16[8,5,8,128]{3,2,1,0:T(8,128)(2,1)S(1)} all-to-all(bf16[8,5,8,128]{3,2,1,0:T(8,128)(2,1)S(1)} %get-tuple-element.38), channel_id=1, replica_groups={{8,0,128,392,264,256,136,384},{24,16,144,408,280,272,152,400},{40,32,16..., dimensions={0} | all-to-all | bytes 163840 | tf_op jit(solution)/shard_map/all_to_all | solution.py:256
  103.9 11.2 %all_to_all.46.arrived = bf16[8,5,8,128]{3,2,1,0:T(8,128)(2,1)S(1)} all-to-all(bf16[8,5,8,128]{3,2,1,0:T(8,128)(2,1)S(1)} %shard_map.66), channel_id=1, replica_groups={{48,112,0,96,16,80,32,64},{56,120,8,104,24,88,40,72},{176,240,128,224,1..., dimensions={0} | all-to-all | bytes 163840 | tf_op jit(solution)/shard_map/all_to_all | solution.py:256
  115.2 0.1 shard_map.67
  115.3 8.8 %all_to_all.47.arrived = bf16[8,4,8,128]{3,2,1,0:T(8,128)(2,1)S(1)} all-to-all(bf16[8,4,8,128]{3,2,1,0:T(8,128)(2,1)S(1)} %get-tuple-element.41), channel_id=1, replica_groups={{8,0,128,392,264,256,136,384},{24,16,144,408,280,272,152,400},{40,32,16..., dimensions={0} | all-to-all | bytes 131072 | tf_op jit(solution)/shard_map/all_to_all | solution.py:256
  124.1 1.4 %shard_map.68 = (f32[64,64]{1,0:T(8,128)}, f32[64,512]{1,0:T(8,128)}, f32[64,512]{1,0:T(8,128)}) custom-call(f32[64,512]{1,0:T(8,128)S(1)} %get-tuple-element.24.base, f32[64,512]{1,0:T(8,128)S(1)} %get-tuple-element.30.resid, f32[1,128]{1,0:T(1,128)S(1)} %get-tuple-element.33.beta, f32[1,128]{1,0:T(1,128)S(1)} %get-tuple-element.34.alpha0, ...), custom_call_target="tpu_custom_call" | custom-call | tf_op jit(solution)/shard_map/pallas_call | solution.py:245
  (3 shorter events, 0.1 us)
Async XLA Ops:
  12.3 15.5 %copy-start = (f32[512]{0:T(512)S(1)}, f32[512]{0:T(512)}, u32[]{:S(2)}) copy-start(f32[512]{0:T(512)} %param.4) | copy-start | bytes 6148
  12.3 17.1 %collective-permute-start = (bf16[33,8,128]{2,1,0:T(8,128)(2,1)S(1)}, bf16[33,8,128]{2,1,0:T(8,128)(2,1)S(1)}, u32[]{:S(2)}, u32[]{:S(2)}) collective-permute-start(bf16[33,8,128]{2,1,0:T(8,128)(2,1)S(1)} %shard_map.59.mine), channel_id=1, source_target_pairs={{0,4},{1,5},{2,6},{3,7},{4,0},{5,1},{6,2},{7,3},{8,12},{9,13},{10,... | collective-permute-start | bytes 202760 | tf_op jit(solution)/shard_map/ppermute | solution.py:285
  76.6 13.8 %collective-permute-start.1 = (bf16[33,8,128]{2,1,0:T(8,128)(2,1)S(1)}, bf16[33,8,128]{2,1,0:T(8,128)(2,1)S(1)}, u32[]{:S(2)}, u32[]{:S(2)}) collective-permute-start(bf16[33,8,128]{2,1,0:T(8,128)(2,1)S(1)} %shard_map.64.mine), channel_id=1, source_target_pairs={{0,4},{1,5},{2,6},{3,7},{4,0},{5,1},{6,2},{7,3},{8,12},{9,13},{10,... | collective-permute-start | bytes 202760 | tf_op jit(solution)/shard_map/ppermute | solution.py:297

commit v7 on v6

--- a/solution.py
+++ b/solution.py
@@ -17,7 +17,7 @@
 X_GROUPS = [[h * COLUMNS + i for i in range(COLUMNS)] for h in range(HALVES)]
 SWAP = [(i, (i + COLUMNS) % (HALVES * COLUMNS)) for i in range(HALVES * COLUMNS)]
 FAR_ORDER = (3, 7, 0, 6, 1, 5, 2, 4)
-NEAR_ORDER = ((0, 1), (0, 0), (1, 0), (3, 1), (2, 1), (2, 0), (1, 1), (3, 0))
+NEAR_ORDER = ((0, 1), (1, 0), (2, 1), (3, 0), (0, 0), (1, 1), (2, 0), (3, 1))
 NEAR_GROUPS = [[(y * LAYERS + z) * CORES + c for y, c in NEAR_ORDER] for z in range(LAYERS)]
 FAR_GROUPS = [
     [(y * LAYERS + z) * CORES + c for z in FAR_ORDER] for y in range(PLANES) for c in range(CORES)

time: 126 us -> 126 us (level)
  waiting for transfers between devices: 7.61 us -> 10.1 us
  blocking collectives: 90 us -> 87.6 us
    ppermute x2, waiting for transfers between devices: 7.61 us -> 10.1 us  [per_device(): other = lax.ppermute(mine, 'feat', SWAP)]
    all_to_all x8, blocking collectives: 90 us -> 87.6 us  [exchanged(): lax.all_to_all(pieces, axis, 0, 0, tiled=True, axis_index_groups=groups)]
where the time goes in v7:
time: 126 us; the launch traced here: 125 us
  blocking collectives  87.6 us (70%)
  starting transfers between devices  22.7 us (18%)
  waiting for transfers between devices  10.1 us (8%)
  Pallas kernels  3.93 us (3%)
    all_to_all x8, blocking collectives, exchanged(): lax.all_to_all(pieces, axis, 0, 0, tiled=True, axis_index_groups=groups)  87.6 us
    ppermute x2, starting transfers between devices, per_device(): other = lax.ppermute(mine, 'feat', SWAP)  22.7 us
    ppermute x2, waiting for transfers between devices, per_device(): other = lax.ppermute(mine, 'feat', SWAP)  10.1 us
    pallas_call x11, Pallas kernels, call(): pl.pallas_call(kernel, out_shape=[jax.ShapeDtypeStruct(s, t) for s, t in...  3.93 us
  transfers between devices with their start and end apart: 2, of which 2 were waited for; matrix products, arithmetic and copies ran while one was open for 0% of the time, Pallas kernels for 0%

profile of v7, /device:TPU:1, one launch (start us, length us, event | category | flops | bytes accessed | tf_op | source)
XLA Modules:
  0.0 125.1 jit_solution(8553056766297044807)
XLA Ops:
  0.6 1.4 %shard_map.58 = (bf16[4,33,8,128]{3,2,1,0:T(8,128)(2,1)S(1)}, bf16[512,512]{1,0:T(8,128)(2,1)S(1)}, f32[64,512]{1,0:T(8,128)S(1)}) custom-call(bf16[512,512]{1,0:T(8,128)(2,1)} %grads.1, f32[64,512]{1,0:T(8,128)} %bitcast.6), custom_call_target="tpu_custom_call" | custom-call | tf_op jit(solution)/shard_map/pallas_call | solution.py:245
  2.1 10.2 %all_to_all.40.arrived = bf16[4,33,8,128]{3,2,1,0:T(8,128)(2,1)S(1)} all-to-all(bf16[4,33,8,128]{3,2,1,0:T(8,128)(2,1)S(1)} %get-tuple-element.26), channel_id=1, replica_groups={{0,1,2,3},{4,5,6,7},{8,9,10,11},{12,13,14,15},{16,17,18,19},{20,21,22,2..., dimensions={0} | all-to-all | bytes 540672 | tf_op jit(solution)/shard_map/all_to_all | solution.py:256
  12.3 0.0 copy-start
  12.3 0.1 shard_map.59.mine
  12.3 15.5 %collective-permute-start = (bf16[33,8,128]{2,1,0:T(8,128)(2,1)S(1)}, bf16[33,8,128]{2,1,0:T(8,128)(2,1)S(1)}, u32[]{:S(2)}, u32[]{:S(2)}) collective-permute-start(bf16[33,8,128]{2,1,0:T(8,128)(2,1)S(1)} %shard_map.59.mine), channel_id=1, source_target_pairs={{0,4},{1,5},{2,6},{3,7},{4,0},{5,1},{6,2},{7,3},{8,12},{9,13},{10,... | collective-permute-start | bytes 202760 | tf_op jit(solution)/shard_map/ppermute | solution.py:285
  27.8 0.0 copy-done
  27.8 1.6 %collective-permute-done.other = bf16[33,8,128]{2,1,0:T(8,128)(2,1)S(1)} collective-permute-done((bf16[33,8,128]{2,1,0:T(8,128)(2,1)S(1)}, bf16[33,8,128]{2,1,0:T(8,128)(2,1)S(1)}, u32[]{:S(2)}, u32[]{:S(2)}) %collective-permute-start) | collective-permute-done | bytes 67616 | tf_op jit(solution)/shard_map/ppermute | solution.py:285
  29.4 0.2 shard_map.60
  29.7 12.8 %all_to_all.41.arrived = bf16[8,5,8,128]{3,2,1,0:T(8,128)(2,1)S(1)} all-to-all(bf16[8,5,8,128]{3,2,1,0:T(8,128)(2,1)S(1)} %get-tuple-element.28), channel_id=1, replica_groups={{8,128,264,384,0,136,256,392},{24,144,280,400,16,152,272,408},{40,160,2..., dimensions={0} | all-to-all | bytes 163840 | tf_op jit(solution)/shard_map/all_to_all | solution.py:256
  42.5 16.8 %all_to_all.42.arrived = bf16[8,5,8,128]{3,2,1,0:T(8,128)(2,1)S(1)} all-to-all(bf16[8,5,8,128]{3,2,1,0:T(8,128)(2,1)S(1)} %shard_map.61), channel_id=1, replica_groups={{48,112,0,96,16,80,32,64},{56,120,8,104,24,88,40,72},{176,240,128,224,1..., dimensions={0} | all-to-all | bytes 163840 | tf_op jit(solution)/shard_map/all_to_all | solution.py:256
  59.3 0.1 shard_map.62
  59.4 9.1 %all_to_all.43.arrived = bf16[8,4,8,128]{3,2,1,0:T(8,128)(2,1)S(1)} all-to-all(bf16[8,4,8,128]{3,2,1,0:T(8,128)(2,1)S(1)} %get-tuple-element.29), channel_id=1, replica_groups={{8,128,264,384,0,136,256,392},{24,144,280,400,16,152,272,408},{40,160,2..., dimensions={0} | all-to-all | bytes 131072 | tf_op jit(solution)/shard_map/all_to_all | solution.py:256
  68.5 0.3 shard_map.63
  68.7 8.9 %all_to_all.44.arrived = bf16[4,33,8,128]{3,2,1,0:T(8,128)(2,1)S(1)} all-to-all(bf16[4,33,8,128]{3,2,1,0:T(8,128)(2,1)S(1)} %get-tuple-element.31), channel_id=1, replica_groups={{0,1,2,3},{4,5,6,7},{8,9,10,11},{12,13,14,15},{16,17,18,19},{20,21,22,2..., dimensions={0} | all-to-all | bytes 540672 | tf_op jit(solution)/shard_map/all_to_all | solution.py:256
  77.6 0.1 shard_map.64.mine
  77.7 7.3 %collective-permute-start.1 = (bf16[33,8,128]{2,1,0:T(8,128)(2,1)S(1)}, bf16[33,8,128]{2,1,0:T(8,128)(2,1)S(1)}, u32[]{:S(2)}, u32[]{:S(2)}) collective-permute-start(bf16[33,8,128]{2,1,0:T(8,128)(2,1)S(1)} %shard_map.64.mine), channel_id=1, source_target_pairs={{0,4},{1,5},{2,6},{3,7},{4,0},{5,1},{6,2},{7,3},{8,12},{9,13},{10,... | collective-permute-start | bytes 202760 | tf_op jit(solution)/shard_map/ppermute | solution.py:297
  85.0 8.4 %collective-permute-done.1.other = bf16[33,8,128]{2,1,0:T(8,128)(2,1)S(1)} collective-permute-done((bf16[33,8,128]{2,1,0:T(8,128)(2,1)S(1)}, bf16[33,8,128]{2,1,0:T(8,128)(2,1)S(1)}, u32[]{:S(2)}, u32[]{:S(2)}) %collective-permute-start.1) | collective-permute-done | bytes 67616 | tf_op jit(solution)/shard_map/ppermute | solution.py:297
  93.4 0.3 shard_map.65
  93.7 9.6 %all_to_all.45.arrived = bf16[8,5,8,128]{3,2,1,0:T(8,128)(2,1)S(1)} all-to-all(bf16[8,5,8,128]{3,2,1,0:T(8,128)(2,1)S(1)} %get-tuple-element.38), channel_id=1, replica_groups={{8,128,264,384,0,136,256,392},{24,144,280,400,16,152,272,408},{40,160,2..., dimensions={0} | all-to-all | bytes 163840 | tf_op jit(solution)/shard_map/all_to_all | solution.py:256
  103.3 11.2 %all_to_all.46.arrived = bf16[8,5,8,128]{3,2,1,0:T(8,128)(2,1)S(1)} all-to-all(bf16[8,5,8,128]{3,2,1,0:T(8,128)(2,1)S(1)} %shard_map.66), channel_id=1, replica_groups={{48,112,0,96,16,80,32,64},{56,120,8,104,24,88,40,72},{176,240,128,224,1..., dimensions={0} | all-to-all | bytes 163840 | tf_op jit(solution)/shard_map/all_to_all | solution.py:256
  114.6 0.1 shard_map.67
  114.7 9.1 %all_to_all.47.arrived = bf16[8,4,8,128]{3,2,1,0:T(8,128)(2,1)S(1)} all-to-all(bf16[8,4,8,128]{3,2,1,0:T(8,128)(2,1)S(1)} %get-tuple-element.41), channel_id=1, replica_groups={{8,128,264,384,0,136,256,392},{24,144,280,400,16,152,272,408},{40,160,2..., dimensions={0} | all-to-all | bytes 131072 | tf_op jit(solution)/shard_map/all_to_all | solution.py:256
  123.7 1.4 %shard_map.68 = (f32[64,64]{1,0:T(8,128)}, f32[64,512]{1,0:T(8,128)}, f32[64,512]{1,0:T(8,128)}) custom-call(f32[64,512]{1,0:T(8,128)S(1)} %get-tuple-element.24.base, f32[64,512]{1,0:T(8,128)S(1)} %get-tuple-element.30.resid, f32[1,128]{1,0:T(1,128)S(1)} %get-tuple-element.33.beta, f32[1,128]{1,0:T(1,128)S(1)} %get-tuple-element.34.alpha0, ...), custom_call_target="tpu_custom_call" | custom-call | tf_op jit(solution)/shard_map/pallas_call | solution.py:245
  (3 shorter events, 0.1 us)
Async XLA Ops:
  12.3 15.5 %copy-start = (f32[512]{0:T(512)S(1)}, f32[512]{0:T(512)}, u32[]{:S(2)}) copy-start(f32[512]{0:T(512)} %param.4) | copy-start | bytes 6148
  12.3 17.1 %collective-permute-start = (bf16[33,8,128]{2,1,0:T(8,128)(2,1)S(1)}, bf16[33,8,128]{2,1,0:T(8,128)(2,1)S(1)}, u32[]{:S(2)}, u32[]{:S(2)}) collective-permute-start(bf16[33,8,128]{2,1,0:T(8,128)(2,1)S(1)} %shard_map.59.mine), channel_id=1, source_target_pairs={{0,4},{1,5},{2,6},{3,7},{4,0},{5,1},{6,2},{7,3},{8,12},{9,13},{10,... | collective-permute-start | bytes 202760 | tf_op jit(solution)/shard_map/ppermute | solution.py:285
  77.7 15.8 %collective-permute-start.1 = (bf16[33,8,128]{2,1,0:T(8,128)(2,1)S(1)}, bf16[33,8,128]{2,1,0:T(8,128)(2,1)S(1)}, u32[]{:S(2)}, u32[]{:S(2)}) collective-permute-start(bf16[33,8,128]{2,1,0:T(8,128)(2,1)S(1)} %shard_map.64.mine), channel_id=1, source_target_pairs={{0,4},{1,5},{2,6},{3,7},{4,0},{5,1},{6,2},{7,3},{8,12},{9,13},{10,... | collective-permute-start | bytes 202760 | tf_op jit(solution)/shard_map/ppermute | solution.py:297

commit v8 on v7

--- a/solution.py
+++ b/solution.py
@@ -17,7 +17,7 @@
 X_GROUPS = [[h * COLUMNS + i for i in range(COLUMNS)] for h in range(HALVES)]
 SWAP = [(i, (i + COLUMNS) % (HALVES * COLUMNS)) for i in range(HALVES * COLUMNS)]
 FAR_ORDER = (3, 7, 0, 6, 1, 5, 2, 4)
-NEAR_ORDER = ((0, 1), (1, 0), (2, 1), (3, 0), (0, 0), (1, 1), (2, 0), (3, 1))
+NEAR_ORDER = ((0, 1), (0, 0), (1, 1), (1, 0), (2, 1), (2, 0), (3, 1), (3, 0))
 NEAR_GROUPS = [[(y * LAYERS + z) * CORES + c for y, c in NEAR_ORDER] for z in range(LAYERS)]
 FAR_GROUPS = [
     [(y * LAYERS + z) * CORES + c for z in FAR_ORDER] for y in range(PLANES) for c in range(CORES)

time: 126 us -> 126 us (level)
  blocking collectives: 87.6 us -> 90.1 us
  waiting for transfers between devices: 10.1 us -> 7.61 us
    ppermute x2, waiting for transfers between devices: 10.1 us -> 7.61 us  [per_device(): other = lax.ppermute(mine, 'feat', SWAP)]
    all_to_all x8, blocking collectives: 87.6 us -> 90.1 us  [exchanged(): lax.all_to_all(pieces, axis, 0, 0, tiled=True, axis_index_groups=groups)]
where the time goes in v8:
time: 126 us
  blocking collectives  90.1 us (72%)
  starting transfers between devices  23.2 us (18%)
  waiting for transfers between devices  7.61 us (6%)
  Pallas kernels  3.93 us (3%)
    all_to_all x8, blocking collectives, exchanged(): lax.all_to_all(pieces, axis, 0, 0, tiled=True, axis_index_groups=groups)  90.1 us
    ppermute x2, starting transfers between devices, per_device(): other = lax.ppermute(mine, 'feat', SWAP)  23.2 us
    ppermute x2, waiting for transfers between devices, per_device(): other = lax.ppermute(mine, 'feat', SWAP)  7.61 us
    pallas_call x11, Pallas kernels, call(): pl.pallas_call(kernel, out_shape=[jax.ShapeDtypeStruct(s, t) for s, t in...  3.93 us
  transfers between devices with their start and end apart: 2, of which 2 were waited for; matrix products, arithmetic and copies ran while one was open for 0% of the time, Pallas kernels for 0%

profile of v8, /device:TPU:1, one launch (start us, length us, event | category | flops | bytes accessed | tf_op | source)
XLA Modules:
  0.0 125.6 jit_solution(7040943460016501035)
XLA Ops:
  0.6 1.4 %shard_map.58 = (bf16[4,33,8,128]{3,2,1,0:T(8,128)(2,1)S(1)}, bf16[512,512]{1,0:T(8,128)(2,1)S(1)}, f32[64,512]{1,0:T(8,128)S(1)}) custom-call(bf16[512,512]{1,0:T(8,128)(2,1)} %grads.1, f32[64,512]{1,0:T(8,128)} %bitcast.6), custom_call_target="tpu_custom_call" | custom-call | tf_op jit(solution)/shard_map/pallas_call | solution.py:245
  2.1 10.2 %all_to_all.40.arrived = bf16[4,33,8,128]{3,2,1,0:T(8,128)(2,1)S(1)} all-to-all(bf16[4,33,8,128]{3,2,1,0:T(8,128)(2,1)S(1)} %get-tuple-element.26), channel_id=1, replica_groups={{0,1,2,3},{4,5,6,7},{8,9,10,11},{12,13,14,15},{16,17,18,19},{20,21,22,2..., dimensions={0} | all-to-all | bytes 540672 | tf_op jit(solution)/shard_map/all_to_all | solution.py:256
  12.3 0.0 copy-start
  12.3 0.1 shard_map.59.mine
  12.3 15.5 %collective-permute-start = (bf16[33,8,128]{2,1,0:T(8,128)(2,1)S(1)}, bf16[33,8,128]{2,1,0:T(8,128)(2,1)S(1)}, u32[]{:S(2)}, u32[]{:S(2)}) collective-permute-start(bf16[33,8,128]{2,1,0:T(8,128)(2,1)S(1)} %shard_map.59.mine), channel_id=1, source_target_pairs={{0,4},{1,5},{2,6},{3,7},{4,0},{5,1},{6,2},{7,3},{8,12},{9,13},{10,... | collective-permute-start | bytes 202760 | tf_op jit(solution)/shard_map/ppermute | solution.py:285
  27.8 0.0 copy-done
  27.8 1.6 %collective-permute-done.other = bf16[33,8,128]{2,1,0:T(8,128)(2,1)S(1)} collective-permute-done((bf16[33,8,128]{2,1,0:T(8,128)(2,1)S(1)}, bf16[33,8,128]{2,1,0:T(8,128)(2,1)S(1)}, u32[]{:S(2)}, u32[]{:S(2)}) %collective-permute-start) | collective-permute-done | bytes 67616 | tf_op jit(solution)/shard_map/ppermute | solution.py:285
  29.4 0.2 shard_map.60
  29.7 12.8 %all_to_all.41.arrived = bf16[8,5,8,128]{3,2,1,0:T(8,128)(2,1)S(1)} all-to-all(bf16[8,5,8,128]{3,2,1,0:T(8,128)(2,1)S(1)} %get-tuple-element.28), channel_id=1, replica_groups={{8,0,136,128,264,256,392,384},{24,16,152,144,280,272,408,400},{40,32,16..., dimensions={0} | all-to-all | bytes 163840 | tf_op jit(solution)/shard_map/all_to_all | solution.py:256
  42.5 16.8 %all_to_all.42.arrived = bf16[8,5,8,128]{3,2,1,0:T(8,128)(2,1)S(1)} all-to-all(bf16[8,5,8,128]{3,2,1,0:T(8,128)(2,1)S(1)} %shard_map.61), channel_id=1, replica_groups={{48,112,0,96,16,80,32,64},{56,120,8,104,24,88,40,72},{176,240,128,224,1..., dimensions={0} | all-to-all | bytes 163840 | tf_op jit(solution)/shard_map/all_to_all | solution.py:256
  59.3 0.1 shard_map.62
  59.4 8.9 %all_to_all.43.arrived = bf16[8,4,8,128]{3,2,1,0:T(8,128)(2,1)S(1)} all-to-all(bf16[8,4,8,128]{3,2,1,0:T(8,128)(2,1)S(1)} %get-tuple-element.29), channel_id=1, replica_groups={{8,0,136,128,264,256,392,384},{24,16,152,144,280,272,408,400},{40,32,16..., dimensions={0} | all-to-all | bytes 131072 | tf_op jit(solution)/shard_map/all_to_all | solution.py:256
  68.3 0.3 shard_map.63
  68.6 8.1 %all_to_all.44.arrived = bf16[4,33,8,128]{3,2,1,0:T(8,128)(2,1)S(1)} all-to-all(bf16[4,33,8,128]{3,2,1,0:T(8,128)(2,1)S(1)} %get-tuple-element.31), channel_id=1, replica_groups={{0,1,2,3},{4,5,6,7},{8,9,10,11},{12,13,14,15},{16,17,18,19},{20,21,22,2..., dimensions={0} | all-to-all | bytes 540672 | tf_op jit(solution)/shard_map/all_to_all | solution.py:256
  76.7 0.1 shard_map.64.mine
  76.7 7.8 %collective-permute-start.1 = (bf16[33,8,128]{2,1,0:T(8,128)(2,1)S(1)}, bf16[33,8,128]{2,1,0:T(8,128)(2,1)S(1)}, u32[]{:S(2)}, u32[]{:S(2)}) collective-permute-start(bf16[33,8,128]{2,1,0:T(8,128)(2,1)S(1)} %shard_map.64.mine), channel_id=1, source_target_pairs={{0,4},{1,5},{2,6},{3,7},{4,0},{5,1},{6,2},{7,3},{8,12},{9,13},{10,... | collective-permute-start | bytes 202760 | tf_op jit(solution)/shard_map/ppermute | solution.py:297
  84.5 6.0 %collective-permute-done.1.other = bf16[33,8,128]{2,1,0:T(8,128)(2,1)S(1)} collective-permute-done((bf16[33,8,128]{2,1,0:T(8,128)(2,1)S(1)}, bf16[33,8,128]{2,1,0:T(8,128)(2,1)S(1)}, u32[]{:S(2)}, u32[]{:S(2)}) %collective-permute-start.1) | collective-permute-done | bytes 67616 | tf_op jit(solution)/shard_map/ppermute | solution.py:297
  90.5 0.3 shard_map.65
  90.8 13.1 %all_to_all.45.arrived = bf16[8,5,8,128]{3,2,1,0:T(8,128)(2,1)S(1)} all-to-all(bf16[8,5,8,128]{3,2,1,0:T(8,128)(2,1)S(1)} %get-tuple-element.38), channel_id=1, replica_groups={{8,0,136,128,264,256,392,384},{24,16,152,144,280,272,408,400},{40,32,16..., dimensions={0} | all-to-all | bytes 163840 | tf_op jit(solution)/shard_map/all_to_all | solution.py:256
  104.0 11.2 %all_to_all.46.arrived = bf16[8,5,8,128]{3,2,1,0:T(8,128)(2,1)S(1)} all-to-all(bf16[8,5,8,128]{3,2,1,0:T(8,128)(2,1)S(1)} %shard_map.66), channel_id=1, replica_groups={{48,112,0,96,16,80,32,64},{56,120,8,104,24,88,40,72},{176,240,128,224,1..., dimensions={0} | all-to-all | bytes 163840 | tf_op jit(solution)/shard_map/all_to_all | solution.py:256
  115.2 0.1 shard_map.67
  115.3 8.9 %all_to_all.47.arrived = bf16[8,4,8,128]{3,2,1,0:T(8,128)(2,1)S(1)} all-to-all(bf16[8,4,8,128]{3,2,1,0:T(8,128)(2,1)S(1)} %get-tuple-element.41), channel_id=1, replica_groups={{8,0,136,128,264,256,392,384},{24,16,152,144,280,272,408,400},{40,32,16..., dimensions={0} | all-to-all | bytes 131072 | tf_op jit(solution)/shard_map/all_to_all | solution.py:256
  124.2 1.4 %shard_map.68 = (f32[64,64]{1,0:T(8,128)}, f32[64,512]{1,0:T(8,128)}, f32[64,512]{1,0:T(8,128)}) custom-call(f32[64,512]{1,0:T(8,128)S(1)} %get-tuple-element.24.base, f32[64,512]{1,0:T(8,128)S(1)} %get-tuple-element.30.resid, f32[1,128]{1,0:T(1,128)S(1)} %get-tuple-element.33.beta, f32[1,128]{1,0:T(1,128)S(1)} %get-tuple-element.34.alpha0, ...), custom_call_target="tpu_custom_call" | custom-call | tf_op jit(solution)/shard_map/pallas_call | solution.py:245
  (3 shorter events, 0.1 us)
Async XLA Ops:
  12.3 15.5 %copy-start = (f32[512]{0:T(512)S(1)}, f32[512]{0:T(512)}, u32[]{:S(2)}) copy-start(f32[512]{0:T(512)} %param.4) | copy-start | bytes 6148
  12.3 17.1 %collective-permute-start = (bf16[33,8,128]{2,1,0:T(8,128)(2,1)S(1)}, bf16[33,8,128]{2,1,0:T(8,128)(2,1)S(1)}, u32[]{:S(2)}, u32[]{:S(2)}) collective-permute-start(bf16[33,8,128]{2,1,0:T(8,128)(2,1)S(1)} %shard_map.59.mine), channel_id=1, source_target_pairs={{0,4},{1,5},{2,6},{3,7},{4,0},{5,1},{6,2},{7,3},{8,12},{9,13},{10,... | collective-permute-start | bytes 202760 | tf_op jit(solution)/shard_map/ppermute | solution.py:285
  76.7 13.8 %collective-permute-start.1 = (bf16[33,8,128]{2,1,0:T(8,128)(2,1)S(1)}, bf16[33,8,128]{2,1,0:T(8,128)(2,1)S(1)}, u32[]{:S(2)}, u32[]{:S(2)}) collective-permute-start(bf16[33,8,128]{2,1,0:T(8,128)(2,1)S(1)} %shard_map.64.mine), channel_id=1, source_target_pairs={{0,4},{1,5},{2,6},{3,7},{4,0},{5,1},{6,2},{7,3},{8,12},{9,13},{10,... | collective-permute-start | bytes 202760 | tf_op jit(solution)/shard_map/ppermute | solution.py:297

commit v9 on v7

--- a/solution.py
+++ b/solution.py
@@ -124,10 +124,11 @@
         put(out.at[i], tiles[i * across : (i + 1) * across] + [tail])
 
 
-def first_rows(grads, base, out, held, line, sems):
+def first_rows(total, grads, base, weights, out, held, line, scaled, sems):
     loads = [
         pltpu.make_async_copy(base, line, sems.at[0]),
         pltpu.make_async_copy(grads, held, sems.at[1]),
+        pltpu.make_async_copy(weights, scaled, sems.at[2]),
     ]
     for load in loads:
         load.start()
@@ -135,18 +136,20 @@
     b = line[...]
     tail = tail_of(as_row(col(b * b)))
     packed = b.astype(BF16)
+    loads[2].wait()
+    scaled[...] = scaled[...] / total
     loads[1].wait()
-    put_copies(out, tiles_of(dot(packed, held[...], ((1,), (1,)))) + [tail])
-
-
-def x_total(count, arrived, out):
-    tiles = summed(arrived)
+    put(out, tiles_of(dot(packed, held[...], ((1,), (1,)))) + [tail])
+
+
+def half_total(count, mine, other, out):
+    tiles = [a + b for a, b in zip(tiles_in(mine), tiles_in(other))]
     tail = tail_of(*[row_in(tiles[-1], i) for i in range(count)])
-    put(out, tiles[:-1] + [tail])
-
-
-def first_image(grads, weights, mine, other, rows, norm, out):
-    tiles = [a + b for a, b in zip(tiles_in(mine), tiles_in(other))]
+    put_copies(out, tiles[:-1] + [tail])
+
+
+def first_image(grads, weights, arrived, rows, norm, out):
+    tiles = summed(arrived)
     r = body_of(tiles[:-1], rows.shape[1])
     rows[...] = r
     norm[...] = row_in(tiles[-1], 0)
@@ -180,11 +183,11 @@
     r = laid_out(arrived, b.shape[1])
     resid[...] = r
     tail = tail_of(as_row(col(r * r)), as_row(col(r * b)))
-    put_copies(out, tiles_of(dot(r, grads[...], ((1,), (1,)))) + [tail])
-
-
-def next_image(grads, weights, mine, other, rows0, norm0, rows, norm, square, beta, out):
-    tiles = [a + b for a, b in zip(tiles_in(mine), tiles_in(other))]
+    put(out, tiles_of(dot(r, grads[...], ((1,), (1,)))) + [tail])
+
+
+def next_image(grads, weights, arrived, rows0, norm0, rows, norm, square, beta, out):
+    tiles = summed(arrived)
     n0, n1, cross = norm0[...], row_in(tiles[-1], 0), row_in(tiles[-1], 1)
     bt = n1 / n0
     norm[...] = n1
@@ -260,7 +263,6 @@
     n_samp, n_feat = lax.axis_size("samp"), lax.axis_size("feat")
     samples = grads.shape[0]
     share = samples // n_feat
-    scaled = (weights / (samples * n_samp))[None, :]
     base = targets.T
     dirs, m = base.shape
     across = m // LANES
@@ -273,35 +275,35 @@
     to_far = ((LAYERS, across + 1, LINES, LANES), BF16)
     to_all = ((NEAR, across, LINES, LANES), BF16)
 
-    out, grads, base = call(
-        first_rows,
-        [to_x, (grads.shape, grads.dtype), block],
+    out, grads, base, scaled = call(
+        functools.partial(first_rows, samples * n_samp),
+        [to_half, (grads.shape, grads.dtype), block, ((1, samples), F32)],
         pltpu.with_memory_space_constraint(grads, pltpu.HBM),
         pltpu.with_memory_space_constraint(base, pltpu.HBM),
+        pltpu.with_memory_space_constraint(weights[None, :], pltpu.HBM),
         inputs=HBM,
-        scratch=[pltpu.SemaphoreType.DMA((2,))],
-    )
-    (mine,) = call(functools.partial(x_total, 1), [to_half], exchanged(out, "feat", X_GROUPS))
-    other = lax.ppermute(mine, "feat", SWAP)
+        scratch=[pltpu.SemaphoreType.DMA((3,))],
+    )
+    other = lax.ppermute(out, "feat", SWAP)
+    (out,) = call(functools.partial(half_total, 1), [to_x], out, other)
     rows0, norm0, out = call(
-        first_image, [block_rows, row, to_near], grads, scaled, mine, other
+        first_image, [block_rows, row, to_near], grads, scaled, exchanged(out, "feat", X_GROUPS)
     )
     (out,) = call(near_total, [to_far], exchanged(out, "samp", NEAR_GROUPS))
     resid_own, alpha0, out = call(
         first_step, [part, row, to_all], base, norm0, exchanged(out, "samp", FAR_GROUPS)
     )
     resid, out = call(
-        next_rows, [block, to_x], grads, base, exchanged(out, "samp", NEAR_GROUPS)
-    )
-    (mine,) = call(functools.partial(x_total, 2), [to_half], exchanged(out, "feat", X_GROUPS))
-    other = lax.ppermute(mine, "feat", SWAP)
+        next_rows, [block, to_half], grads, base, exchanged(out, "samp", NEAR_GROUPS)
+    )
+    other = lax.ppermute(out, "feat", SWAP)
+    (out,) = call(functools.partial(half_total, 2), [to_x], out, other)
     rows1, norm1, square, beta, out = call(
         next_image,
         [block_rows, row, row, row, to_near],
         grads,
         scaled,
-        mine,
-        other,
+        exchanged(out, "feat", X_GROUPS),
         rows0,
         norm0,
     )

time: 126 us -> 127 us (level)
  waiting for transfers between devices: 10.1 us -> 7.22 us
  blocking collectives: 87.6 us -> 89.7 us
  starting transfers between devices: 22.7 us -> 24.7 us
    ppermute x2, waiting for transfers between devices: 10.1 us -> 7.22 us  [per_device(): other = lax.ppermute(out, 'feat', SWAP)]
    all_to_all x8, blocking collectives: 87.6 us -> 89.7 us  [exchanged(): lax.all_to_all(pieces, axis, 0, 0, tiled=True, axis_index_groups=groups)]
    ppermute x2, starting transfers between devices: 22.7 us -> 24.7 us  [per_device(): other = lax.ppermute(out, 'feat', SWAP)]
where the time goes in v9:
time: 127 us; the launch traced here: 126 us
  blocking collectives  89.7 us (71%)
  starting transfers between devices  24.7 us (19%)
  waiting for transfers between devices  7.22 us (6%)
  Pallas kernels  3.89 us (3%)
    all_to_all x8, blocking collectives, exchanged(): lax.all_to_all(pieces, axis, 0, 0, tiled=True, axis_index_groups=groups)  89.7 us
    ppermute x2, starting transfers between devices, per_device(): other = lax.ppermute(out, 'feat', SWAP)  24.7 us
    ppermute x2, waiting for transfers between devices, per_device(): other = lax.ppermute(out, 'feat', SWAP)  7.22 us
    pallas_call x11, Pallas kernels, call(): pl.pallas_call(kernel, out_shape=[jax.ShapeDtypeStruct(s, t) for s, t in...  3.89 us
  transfers between devices with their start and end apart: 2, of which 2 were waited for; matrix products, arithmetic and copies ran while one was open for 0% of the time, Pallas kernels for 0%

profile of v9, /device:TPU:1, one launch (start us, length us, event | category | flops | bytes accessed | tf_op | source)
XLA Modules:
  0.0 126.1 jit_solution(16971562294076888526)
XLA Ops:
  0.6 1.4 %shard_map.58 = (bf16[33,8,128]{2,1,0:T(8,128)(2,1)S(1)}, bf16[512,512]{1,0:T(8,128)(2,1)S(1)}, f32[64,512]{1,0:T(8,128)S(1)}, f32[1,512]{1,0:T(1,128)S(1)}) custom-call(bf16[512,512]{1,0:T(8,128)(2,1)} %grads.1, f32[64,512]{1,0:T(8,128)} %bitcast.4, f32[1,512]{1,0:T(1,128)} %bitcast.5), custom_call_target="tpu_custom_call" | custom-call | tf_op jit(solution)/shard_map/pallas_call | solution.py:248
  2.1 16.3 %collective-permute-start = (bf16[33,8,128]{2,1,0:T(8,128)(2,1)S(1)}, bf16[33,8,128]{2,1,0:T(8,128)(2,1)S(1)}, u32[]{:S(2)}, u32[]{:S(2)}) collective-permute-start(bf16[33,8,128]{2,1,0:T(8,128)(2,1)S(1)} %get-tuple-element.28.mine), channel_id=1, source_target_pairs={{0,4},{1,5},{2,6},{3,7},{4,0},{5,1},{6,2},{7,3},{8,12},{9,13},{10,... | collective-permute-start | bytes 202760 | tf_op jit(solution)/shard_map/ppermute | solution.py:287
  18.3 1.9 %collective-permute-done.other = bf16[33,8,128]{2,1,0:T(8,128)(2,1)S(1)} collective-permute-done((bf16[33,8,128]{2,1,0:T(8,128)(2,1)S(1)}, bf16[33,8,128]{2,1,0:T(8,128)(2,1)S(1)}, u32[]{:S(2)}, u32[]{:S(2)}) %collective-permute-start) | collective-permute-done | bytes 67616 | tf_op jit(solution)/shard_map/ppermute | solution.py:287
  20.2 9.4 %all_to_all.40.arrived = bf16[4,33,8,128]{3,2,1,0:T(8,128)(2,1)S(1)} all-to-all(bf16[4,33,8,128]{3,2,1,0:T(8,128)(2,1)S(1)} %shard_map.59), channel_id=1, replica_groups={{0,1,2,3},{4,5,6,7},{8,9,10,11},{12,13,14,15},{16,17,18,19},{20,21,22,2..., dimensions={0} | all-to-all | bytes 540672 | tf_op jit(solution)/shard_map/all_to_all | solution.py:259
  29.6 0.2 shard_map.60
  29.8 13.9 %all_to_all.41.arrived = bf16[8,5,8,128]{3,2,1,0:T(8,128)(2,1)S(1)} all-to-all(bf16[8,5,8,128]{3,2,1,0:T(8,128)(2,1)S(1)} %get-tuple-element.30), channel_id=1, replica_groups={{8,128,264,384,0,136,256,392},{24,144,280,400,16,152,272,408},{40,160,2..., dimensions={0} | all-to-all | bytes 163840 | tf_op jit(solution)/shard_map/all_to_all | solution.py:259
  43.8 15.9 %all_to_all.42.arrived = bf16[8,5,8,128]{3,2,1,0:T(8,128)(2,1)S(1)} all-to-all(bf16[8,5,8,128]{3,2,1,0:T(8,128)(2,1)S(1)} %shard_map.61), channel_id=1, replica_groups={{48,112,0,96,16,80,32,64},{56,120,8,104,24,88,40,72},{176,240,128,224,1..., dimensions={0} | all-to-all | bytes 163840 | tf_op jit(solution)/shard_map/all_to_all | solution.py:259
  59.7 0.1 shard_map.62
  59.8 9.1 %all_to_all.43.arrived = bf16[8,4,8,128]{3,2,1,0:T(8,128)(2,1)S(1)} all-to-all(bf16[8,4,8,128]{3,2,1,0:T(8,128)(2,1)S(1)} %get-tuple-element.31), channel_id=1, replica_groups={{8,128,264,384,0,136,256,392},{24,144,280,400,16,152,272,408},{40,160,2..., dimensions={0} | all-to-all | bytes 131072 | tf_op jit(solution)/shard_map/all_to_all | solution.py:259
  68.8 0.3 shard_map.63
  69.1 8.4 %collective-permute-start.1 = (bf16[33,8,128]{2,1,0:T(8,128)(2,1)S(1)}, bf16[33,8,128]{2,1,0:T(8,128)(2,1)S(1)}, u32[]{:S(2)}, u32[]{:S(2)}) collective-permute-start(bf16[33,8,128]{2,1,0:T(8,128)(2,1)S(1)} %get-tuple-element.33.mine), channel_id=1, source_target_pairs={{0,4},{1,5},{2,6},{3,7},{4,0},{5,1},{6,2},{7,3},{8,12},{9,13},{10,... | collective-permute-start | bytes 202760 | tf_op jit(solution)/shard_map/ppermute | solution.py:299
  77.5 5.3 %collective-permute-done.1.other = bf16[33,8,128]{2,1,0:T(8,128)(2,1)S(1)} collective-permute-done((bf16[33,8,128]{2,1,0:T(8,128)(2,1)S(1)}, bf16[33,8,128]{2,1,0:T(8,128)(2,1)S(1)}, u32[]{:S(2)}, u32[]{:S(2)}) %collective-permute-start.1) | collective-permute-done | bytes 67616 | tf_op jit(solution)/shard_map/ppermute | solution.py:299
  82.9 8.0 %all_to_all.44.arrived = bf16[4,33,8,128]{3,2,1,0:T(8,128)(2,1)S(1)} all-to-all(bf16[4,33,8,128]{3,2,1,0:T(8,128)(2,1)S(1)} %shard_map.64), channel_id=1, replica_groups={{0,1,2,3},{4,5,6,7},{8,9,10,11},{12,13,14,15},{16,17,18,19},{20,21,22,2..., dimensions={0} | all-to-all | bytes 540672 | tf_op jit(solution)/shard_map/all_to_all | solution.py:259
  90.9 0.3 shard_map.65
  91.2 13.2 %all_to_all.45.arrived = bf16[8,5,8,128]{3,2,1,0:T(8,128)(2,1)S(1)} all-to-all(bf16[8,5,8,128]{3,2,1,0:T(8,128)(2,1)S(1)} %get-tuple-element.40), channel_id=1, replica_groups={{8,128,264,384,0,136,256,392},{24,144,280,400,16,152,272,408},{40,160,2..., dimensions={0} | all-to-all | bytes 163840 | tf_op jit(solution)/shard_map/all_to_all | solution.py:259
  104.3 11.2 %all_to_all.46.arrived = bf16[8,5,8,128]{3,2,1,0:T(8,128)(2,1)S(1)} all-to-all(bf16[8,5,8,128]{3,2,1,0:T(8,128)(2,1)S(1)} %shard_map.66), channel_id=1, replica_groups={{48,112,0,96,16,80,32,64},{56,120,8,104,24,88,40,72},{176,240,128,224,1..., dimensions={0} | all-to-all | bytes 163840 | tf_op jit(solution)/shard_map/all_to_all | solution.py:259
  115.6 0.1 shard_map.67
  115.7 9.1 %all_to_all.47.arrived = bf16[8,4,8,128]{3,2,1,0:T(8,128)(2,1)S(1)} all-to-all(bf16[8,4,8,128]{3,2,1,0:T(8,128)(2,1)S(1)} %get-tuple-element.43), channel_id=1, replica_groups={{8,128,264,384,0,136,256,392},{24,144,280,400,16,152,272,408},{40,160,2..., dimensions={0} | all-to-all | bytes 131072 | tf_op jit(solution)/shard_map/all_to_all | solution.py:259
  124.8 1.4 %shard_map.68 = (f32[64,64]{1,0:T(8,128)}, f32[64,512]{1,0:T(8,128)}, f32[64,512]{1,0:T(8,128)}) custom-call(f32[64,512]{1,0:T(8,128)S(1)} %get-tuple-element.25.base, f32[64,512]{1,0:T(8,128)S(1)} %get-tuple-element.32.resid, f32[1,128]{1,0:T(1,128)S(1)} %get-tuple-element.35.beta, f32[1,128]{1,0:T(1,128)S(1)} %get-tuple-element.36.alpha0, ...), custom_call_target="tpu_custom_call" | custom-call | tf_op jit(solution)/shard_map/pallas_call | solution.py:248
  (4 shorter events, 0.1 us)
Async XLA Ops:
  2.1 18.1 %collective-permute-start = (bf16[33,8,128]{2,1,0:T(8,128)(2,1)S(1)}, bf16[33,8,128]{2,1,0:T(8,128)(2,1)S(1)}, u32[]{:S(2)}, u32[]{:S(2)}) collective-permute-start(bf16[33,8,128]{2,1,0:T(8,128)(2,1)S(1)} %get-tuple-element.28.mine), channel_id=1, source_target_pairs={{0,4},{1,5},{2,6},{3,7},{4,0},{5,1},{6,2},{7,3},{8,12},{9,13},{10,... | collective-permute-start | bytes 202760 | tf_op jit(solution)/shard_map/ppermute | solution.py:287
  69.1 13.7 %collective-permute-start.1 = (bf16[33,8,128]{2,1,0:T(8,128)(2,1)S(1)}, bf16[33,8,128]{2,1,0:T(8,128)(2,1)S(1)}, u32[]{:S(2)}, u32[]{:S(2)}) collective-permute-start(bf16[33,8,128]{2,1,0:T(8,128)(2,1)S(1)} %get-tuple-element.33.mine), channel_id=1, source_target_pairs={{0,4},{1,5},{2,6},{3,7},{4,0},{5,1},{6,2},{7,3},{8,12},{9,13},{10,... | collective-permute-start | bytes 202760 | tf_op jit(solution)/shard_map/ppermute | solution.py:299

commit v10 on v9

--- a/solution.py
+++ b/solution.py
@@ -15,7 +15,7 @@
 LINES, LANES = 8, 128
 
 X_GROUPS = [[h * COLUMNS + i for i in range(COLUMNS)] for h in range(HALVES)]
-SWAP = [(i, (i + COLUMNS) % (HALVES * COLUMNS)) for i in range(HALVES * COLUMNS)]
+FEAT_ORDER = (0, 6, 1, 4, 2, 5, 3, 7)
 FAR_ORDER = (3, 7, 0, 6, 1, 5, 2, 4)
 NEAR_ORDER = ((0, 1), (1, 0), (2, 1), (3, 0), (0, 0), (1, 1), (2, 0), (3, 1))
 NEAR_GROUPS = [[(y * LAYERS + z) * CORES + c for y, c in NEAR_ORDER] for z in range(LAYERS)]
@@ -122,6 +122,12 @@
     across = len(tiles) // out.shape[0]
     for i in range(out.shape[0]):
         put(out.at[i], tiles[i * across : (i + 1) * across] + [tail])
+
+
+def put_quarters(out, tiles, tail):
+    each = len(tiles) // out.shape[0]
+    for i in range(out.shape[0]):
+        put(out.at[i], tiles[i * each : (i + 1) * each] + [tail])
 
 
 def first_rows(total, grads, base, weights, out, held, line, scaled, sems):
@@ -139,17 +145,27 @@
     loads[2].wait()
     scaled[...] = scaled[...] / total
     loads[1].wait()
-    put(out, tiles_of(dot(packed, held[...], ((1,), (1,)))) + [tail])
-
-
-def half_total(count, mine, other, out):
-    tiles = [a + b for a, b in zip(tiles_in(mine), tiles_in(other))]
+    put_quarters(out, tiles_of(dot(packed, held[...], ((1,), (1,)))), tail)
+
+
+def x_total(count, arrived, out):
+    tiles = summed(arrived)
     tail = tail_of(*[row_in(tiles[-1], i) for i in range(count)])
     put_copies(out, tiles[:-1] + [tail])
 
 
+def feat_total(arrived):
+    tiles, tail = [], None
+    for x in range(COLUMNS):
+        low, high = (arrived.at[FEAT_ORDER.index(half * COLUMNS + x)] for half in range(HALVES))
+        both = [a + b for a, b in zip(tiles_in(low), tiles_in(high))]
+        tiles += both[:-1]
+        tail = both[-1] if x == 0 else tail
+    return tiles + [tail]
+
+
 def first_image(grads, weights, arrived, rows, norm, out):
-    tiles = summed(arrived)
+    tiles = feat_total(arrived)
     r = body_of(tiles[:-1], rows.shape[1])
     rows[...] = r
     norm[...] = row_in(tiles[-1], 0)
@@ -183,11 +199,11 @@
     r = laid_out(arrived, b.shape[1])
     resid[...] = r
     tail = tail_of(as_row(col(r * r)), as_row(col(r * b)))
-    put(out, tiles_of(dot(r, grads[...], ((1,), (1,)))) + [tail])
+    put_quarters(out, tiles_of(dot(r, grads[...], ((1,), (1,)))), tail)
 
 
 def next_image(grads, weights, arrived, rows0, norm0, rows, norm, square, beta, out):
-    tiles = summed(arrived)
+    tiles = feat_total(arrived)
     n0, n1, cross = norm0[...], row_in(tiles[-1], 0), row_in(tiles[-1], 1)
     bt = n1 / n0
     norm[...] = n1
@@ -266,44 +282,42 @@
     base = targets.T
     dirs, m = base.shape
     across = m // LANES
-    row_tiles = dirs // LINES * (samples // LANES) + 1
+    quarter = dirs // COLUMNS // LINES * (samples // LANES) + 1
     block, row, part = ((dirs, m), F32), ((1, LANES), F32), ((LINES, m), F32)
     block_rows = ((dirs, samples), F32)
-    to_x = ((COLUMNS, row_tiles, LINES, LANES), BF16)
-    to_half = ((row_tiles, LINES, LANES), BF16)
+    to_x = ((COLUMNS, quarter, LINES, LANES), BF16)
+    to_feat = ((HALVES * COLUMNS, quarter, LINES, LANES), BF16)
     to_near = ((NEAR, across + 1, LINES, LANES), BF16)
     to_far = ((LAYERS, across + 1, LINES, LANES), BF16)
     to_all = ((NEAR, across, LINES, LANES), BF16)
 
     out, grads, base, scaled = call(
         functools.partial(first_rows, samples * n_samp),
-        [to_half, (grads.shape, grads.dtype), block, ((1, samples), F32)],
+        [to_x, (grads.shape, grads.dtype), block, ((1, samples), F32)],
         pltpu.with_memory_space_constraint(grads, pltpu.HBM),
         pltpu.with_memory_space_constraint(base, pltpu.HBM),
         pltpu.with_memory_space_constraint(weights[None, :], pltpu.HBM),
         inputs=HBM,
         scratch=[pltpu.SemaphoreType.DMA((3,))],
     )
-    other = lax.ppermute(out, "feat", SWAP)
-    (out,) = call(functools.partial(half_total, 1), [to_x], out, other)
+    (out,) = call(functools.partial(x_total, 1), [to_feat], exchanged(out, "feat", X_GROUPS))
     rows0, norm0, out = call(
-        first_image, [block_rows, row, to_near], grads, scaled, exchanged(out, "feat", X_GROUPS)
+        first_image, [block_rows, row, to_near], grads, scaled, exchanged(out, "feat", [FEAT_ORDER])
     )
     (out,) = call(near_total, [to_far], exchanged(out, "samp", NEAR_GROUPS))
     resid_own, alpha0, out = call(
         first_step, [part, row, to_all], base, norm0, exchanged(out, "samp", FAR_GROUPS)
     )
     resid, out = call(
-        next_rows, [block, to_half], grads, base, exchanged(out, "samp", NEAR_GROUPS)
-    )
-    other = lax.ppermute(out, "feat", SWAP)
-    (out,) = call(functools.partial(half_total, 2), [to_x], out, other)
+        next_rows, [block, to_x], grads, base, exchanged(out, "samp", NEAR_GROUPS)
+    )
+    (out,) = call(functools.partial(x_total, 2), [to_feat], exchanged(out, "feat", X_GROUPS))
     rows1, norm1, square, beta, out = call(
         next_image,
         [block_rows, row, row, row, to_near],
         grads,
         scaled,
-        exchanged(out, "feat", X_GROUPS),
+        exchanged(out, "feat", [FEAT_ORDER]),
         rows0,
         norm0,
     )

time: 127 us -> 136 us (1.071)
  blocking collectives: 89.7 us -> 131 us
  starting transfers between devices: 24.7 us -> 0 us
  waiting for transfers between devices: 7.22 us -> 0 us
    all_to_all x8 -> x10, blocking collectives: 89.7 us -> 131 us  [exchanged(): lax.all_to_all(pieces, axis, 0, 0, tiled=True, axis_index_groups=groups)]
    ppermute x2 -> x0, starting transfers between devices: 24.7 us -> none  [per_device(): other = lax.ppermute(out, 'feat', SWAP)]
    ppermute x2 -> x0, waiting for transfers between devices: 7.22 us -> none  [per_device(): other = lax.ppermute(out, 'feat', SWAP)]
  transfers between devices with their start and end apart: 2 -> 0, of which waited for: 2 -> 0; matrix products, arithmetic and copies ran while one was open for 0% -> 0% of each run, Pallas kernels for 0% -> 0%
where the time goes in v10:
time: 136 us
  blocking collectives  131 us (96%)
  Pallas kernels  3.89 us (3%)
    all_to_all x10, blocking collectives, exchanged(): lax.all_to_all(pieces, axis, 0, 0, tiled=True, axis_index_groups=groups)  131 us
    pallas_call x11, Pallas kernels, call(): pl.pallas_call(kernel, out_shape=[jax.ShapeDtypeStruct(s, t) for s, t in...  3.89 us

profile of v10, /device:TPU:1, one launch (start us, length us, event | category | flops | bytes accessed | tf_op | source)
XLA Modules:
  0.0 135.6 jit_solution(4415584183375524530)
XLA Ops:
  0.6 1.4 %shard_map.58 = (bf16[4,9,8,128]{3,2,1,0:T(8,128)(2,1)S(1)}, bf16[512,512]{1,0:T(8,128)(2,1)S(1)}, f32[64,512]{1,0:T(8,128)S(1)}, f32[1,512]{1,0:T(1,128)S(1)}) custom-call(bf16[512,512]{1,0:T(8,128)(2,1)} %grads.1, f32[64,512]{1,0:T(8,128)} %bitcast.4, f32[1,512]{1,0:T(1,128)} %bitcast.5), custom_call_target="tpu_custom_call" | custom-call | tf_op jit(solution)/shard_map/pallas_call | solution.py:264
  2.1 9.2 %all_to_all.50.arrived = bf16[4,9,8,128]{3,2,1,0:T(8,128)(2,1)S(1)} all-to-all(bf16[4,9,8,128]{3,2,1,0:T(8,128)(2,1)S(1)} %get-tuple-element.28), channel_id=1, replica_groups={{0,1,2,3},{4,5,6,7},{8,9,10,11},{12,13,14,15},{16,17,18,19},{20,21,22,2..., dimensions={0} | all-to-all | bytes 147456 | tf_op jit(solution)/shard_map/all_to_all | solution.py:275
  11.3 29.6 %all_to_all.51.arrived = bf16[8,9,8,128]{3,2,1,0:T(8,128)(2,1)S(1)} all-to-all(bf16[8,9,8,128]{3,2,1,0:T(8,128)(2,1)S(1)} %shard_map.59), channel_id=1, replica_groups={{0,6,1,4,2,5,3,7},{8,14,9,12,10,13,11,15},{16,22,17,20,18,21,19,23},{24..., dimensions={0} | all-to-all | bytes 294912 | tf_op jit(solution)/shard_map/all_to_all | solution.py:275
  40.9 0.2 shard_map.60
  41.1 12.3 %all_to_all.52.arrived = bf16[8,5,8,128]{3,2,1,0:T(8,128)(2,1)S(1)} all-to-all(bf16[8,5,8,128]{3,2,1,0:T(8,128)(2,1)S(1)} %get-tuple-element.30), channel_id=1, replica_groups={{8,128,264,384,0,136,256,392},{24,144,280,400,16,152,272,408},{40,160,2..., dimensions={0} | all-to-all | bytes 163840 | tf_op jit(solution)/shard_map/all_to_all | solution.py:275
  53.5 15.2 %all_to_all.53.arrived = bf16[8,5,8,128]{3,2,1,0:T(8,128)(2,1)S(1)} all-to-all(bf16[8,5,8,128]{3,2,1,0:T(8,128)(2,1)S(1)} %shard_map.61), channel_id=1, replica_groups={{48,112,0,96,16,80,32,64},{56,120,8,104,24,88,40,72},{176,240,128,224,1..., dimensions={0} | all-to-all | bytes 163840 | tf_op jit(solution)/shard_map/all_to_all | solution.py:275
  68.7 0.1 shard_map.62
  68.8 9.1 %all_to_all.54.arrived = bf16[8,4,8,128]{3,2,1,0:T(8,128)(2,1)S(1)} all-to-all(bf16[8,4,8,128]{3,2,1,0:T(8,128)(2,1)S(1)} %get-tuple-element.31), channel_id=1, replica_groups={{8,128,264,384,0,136,256,392},{24,144,280,400,16,152,272,408},{40,160,2..., dimensions={0} | all-to-all | bytes 131072 | tf_op jit(solution)/shard_map/all_to_all | solution.py:275
  77.9 0.3 shard_map.63
  78.2 6.9 %all_to_all.55.arrived = bf16[4,9,8,128]{3,2,1,0:T(8,128)(2,1)S(1)} all-to-all(bf16[4,9,8,128]{3,2,1,0:T(8,128)(2,1)S(1)} %get-tuple-element.33), channel_id=1, replica_groups={{0,1,2,3},{4,5,6,7},{8,9,10,11},{12,13,14,15},{16,17,18,19},{20,21,22,2..., dimensions={0} | all-to-all | bytes 147456 | tf_op jit(solution)/shard_map/all_to_all | solution.py:275
  85.1 16.7 %all_to_all.56.arrived = bf16[8,9,8,128]{3,2,1,0:T(8,128)(2,1)S(1)} all-to-all(bf16[8,9,8,128]{3,2,1,0:T(8,128)(2,1)S(1)} %shard_map.64), channel_id=1, replica_groups={{0,6,1,4,2,5,3,7},{8,14,9,12,10,13,11,15},{16,22,17,20,18,21,19,23},{24..., dimensions={0} | all-to-all | bytes 294912 | tf_op jit(solution)/shard_map/all_to_all | solution.py:275
  101.8 0.3 shard_map.65
  102.0 10.0 %all_to_all.57.arrived = bf16[8,5,8,128]{3,2,1,0:T(8,128)(2,1)S(1)} all-to-all(bf16[8,5,8,128]{3,2,1,0:T(8,128)(2,1)S(1)} %get-tuple-element.40), channel_id=1, replica_groups={{8,128,264,384,0,136,256,392},{24,144,280,400,16,152,272,408},{40,160,2..., dimensions={0} | all-to-all | bytes 163840 | tf_op jit(solution)/shard_map/all_to_all | solution.py:275
  112.1 12.9 %all_to_all.58.arrived = bf16[8,5,8,128]{3,2,1,0:T(8,128)(2,1)S(1)} all-to-all(bf16[8,5,8,128]{3,2,1,0:T(8,128)(2,1)S(1)} %shard_map.66), channel_id=1, replica_groups={{48,112,0,96,16,80,32,64},{56,120,8,104,24,88,40,72},{176,240,128,224,1..., dimensions={0} | all-to-all | bytes 163840 | tf_op jit(solution)/shard_map/all_to_all | solution.py:275
  125.0 0.1 shard_map.67
  125.1 9.1 %all_to_all.59.arrived = bf16[8,4,8,128]{3,2,1,0:T(8,128)(2,1)S(1)} all-to-all(bf16[8,4,8,128]{3,2,1,0:T(8,128)(2,1)S(1)} %get-tuple-element.43), channel_id=1, replica_groups={{8,128,264,384,0,136,256,392},{24,144,280,400,16,152,272,408},{40,160,2..., dimensions={0} | all-to-all | bytes 131072 | tf_op jit(solution)/shard_map/all_to_all | solution.py:275
  134.2 1.4 %shard_map.68 = (f32[64,64]{1,0:T(8,128)}, f32[64,512]{1,0:T(8,128)}, f32[64,512]{1,0:T(8,128)}) custom-call(f32[64,512]{1,0:T(8,128)S(1)} %get-tuple-element.25.base, f32[64,512]{1,0:T(8,128)S(1)} %get-tuple-element.32.resid, f32[1,128]{1,0:T(1,128)S(1)} %get-tuple-element.35.beta, f32[1,128]{1,0:T(1,128)S(1)} %get-tuple-element.36.alpha0, ...), custom_call_target="tpu_custom_call" | custom-call | tf_op jit(solution)/shard_map/pallas_call | solution.py:264
  (4 shorter events, 0.1 us)

commit v11 on v8

--- a/solution.py
+++ b/solution.py
@@ -17,7 +17,7 @@
 X_GROUPS = [[h * COLUMNS + i for i in range(COLUMNS)] for h in range(HALVES)]
 SWAP = [(i, (i + COLUMNS) % (HALVES * COLUMNS)) for i in range(HALVES * COLUMNS)]
 FAR_ORDER = (3, 7, 0, 6, 1, 5, 2, 4)
-NEAR_ORDER = ((0, 1), (0, 0), (1, 1), (1, 0), (2, 1), (2, 0), (3, 1), (3, 0))
+NEAR_ORDER = ((1, 1), (2, 0), (0, 1), (3, 0), (1, 0), (2, 1), (0, 0), (3, 1))
 NEAR_GROUPS = [[(y * LAYERS + z) * CORES + c for y, c in NEAR_ORDER] for z in range(LAYERS)]
 FAR_GROUPS = [
     [(y * LAYERS + z) * CORES + c for z in FAR_ORDER] for y in range(PLANES) for c in range(CORES)

time: 126 us -> 124 us (0.984)
  blocking collectives: 90.1 us -> 88.5 us
    all_to_all x8, blocking collectives: 90.1 us -> 88.5 us  [exchanged(): lax.all_to_all(pieces, axis, 0, 0, tiled=True, axis_index_groups=groups)]
where the time goes in v11:
time: 124 us
  blocking collectives  88.5 us (71%)
  starting transfers between devices  23.2 us (19%)
  waiting for transfers between devices  7.7 us (6%)
  Pallas kernels  3.93 us (3%)
    all_to_all x8, blocking collectives, exchanged(): lax.all_to_all(pieces, axis, 0, 0, tiled=True, axis_index_groups=groups)  88.5 us
    ppermute x2, starting transfers between devices, per_device(): other = lax.ppermute(mine, 'feat', SWAP)  23.2 us
    ppermute x2, waiting for transfers between devices, per_device(): other = lax.ppermute(mine, 'feat', SWAP)  7.7 us
    pallas_call x11, Pallas kernels, call(): pl.pallas_call(kernel, out_shape=[jax.ShapeDtypeStruct(s, t) for s, t in...  3.93 us
  transfers between devices with their start and end apart: 2, of which 2 were waited for; matrix products, arithmetic and copies ran while one was open for 0% of the time, Pallas kernels for 0%

profile of v11, /device:TPU:1, one launch (start us, length us, event | category | flops | bytes accessed | tf_op | source)
XLA Modules:
  0.0 124.0 jit_solution(8772798539200541712)
XLA Ops:
  0.6 1.4 %shard_map.58 = (bf16[4,33,8,128]{3,2,1,0:T(8,128)(2,1)S(1)}, bf16[512,512]{1,0:T(8,128)(2,1)S(1)}, f32[64,512]{1,0:T(8,128)S(1)}) custom-call(bf16[512,512]{1,0:T(8,128)(2,1)} %grads.1, f32[64,512]{1,0:T(8,128)} %bitcast.6), custom_call_target="tpu_custom_call" | custom-call | tf_op jit(solution)/shard_map/pallas_call | solution.py:245
  2.1 10.2 %all_to_all.40.arrived = bf16[4,33,8,128]{3,2,1,0:T(8,128)(2,1)S(1)} all-to-all(bf16[4,33,8,128]{3,2,1,0:T(8,128)(2,1)S(1)} %get-tuple-element.26), channel_id=1, replica_groups={{0,1,2,3},{4,5,6,7},{8,9,10,11},{12,13,14,15},{16,17,18,19},{20,21,22,2..., dimensions={0} | all-to-all | bytes 540672 | tf_op jit(solution)/shard_map/all_to_all | solution.py:256
  12.3 0.0 copy-start
  12.3 0.1 shard_map.59.mine
  12.3 15.5 %collective-permute-start = (bf16[33,8,128]{2,1,0:T(8,128)(2,1)S(1)}, bf16[33,8,128]{2,1,0:T(8,128)(2,1)S(1)}, u32[]{:S(2)}, u32[]{:S(2)}) collective-permute-start(bf16[33,8,128]{2,1,0:T(8,128)(2,1)S(1)} %shard_map.59.mine), channel_id=1, source_target_pairs={{0,4},{1,5},{2,6},{3,7},{4,0},{5,1},{6,2},{7,3},{8,12},{9,13},{10,... | collective-permute-start | bytes 202760 | tf_op jit(solution)/shard_map/ppermute | solution.py:285
  27.8 0.0 copy-done
  27.8 1.6 %collective-permute-done.other = bf16[33,8,128]{2,1,0:T(8,128)(2,1)S(1)} collective-permute-done((bf16[33,8,128]{2,1,0:T(8,128)(2,1)S(1)}, bf16[33,8,128]{2,1,0:T(8,128)(2,1)S(1)}, u32[]{:S(2)}, u32[]{:S(2)}) %collective-permute-start) | collective-permute-done | bytes 67616 | tf_op jit(solution)/shard_map/ppermute | solution.py:285
  29.4 0.2 shard_map.60
  29.7 12.3 %all_to_all.41.arrived = bf16[8,5,8,128]{3,2,1,0:T(8,128)(2,1)S(1)} all-to-all(bf16[8,5,8,128]{3,2,1,0:T(8,128)(2,1)S(1)} %get-tuple-element.28), channel_id=1, replica_groups={{136,256,8,384,128,264,0,392},{152,272,24,400,144,280,16,408},{168,288,..., dimensions={0} | all-to-all | bytes 163840 | tf_op jit(solution)/shard_map/all_to_all | solution.py:256
  42.0 16.8 %all_to_all.42.arrived = bf16[8,5,8,128]{3,2,1,0:T(8,128)(2,1)S(1)} all-to-all(bf16[8,5,8,128]{3,2,1,0:T(8,128)(2,1)S(1)} %shard_map.61), channel_id=1, replica_groups={{48,112,0,96,16,80,32,64},{56,120,8,104,24,88,40,72},{176,240,128,224,1..., dimensions={0} | all-to-all | bytes 163840 | tf_op jit(solution)/shard_map/all_to_all | solution.py:256
  58.8 0.1 shard_map.62
  58.9 8.8 %all_to_all.43.arrived = bf16[8,4,8,128]{3,2,1,0:T(8,128)(2,1)S(1)} all-to-all(bf16[8,4,8,128]{3,2,1,0:T(8,128)(2,1)S(1)} %get-tuple-element.29), channel_id=1, replica_groups={{136,256,8,384,128,264,0,392},{152,272,24,400,144,280,16,408},{168,288,..., dimensions={0} | all-to-all | bytes 131072 | tf_op jit(solution)/shard_map/all_to_all | solution.py:256
  67.7 0.3 shard_map.63
  68.0 8.1 %all_to_all.44.arrived = bf16[4,33,8,128]{3,2,1,0:T(8,128)(2,1)S(1)} all-to-all(bf16[4,33,8,128]{3,2,1,0:T(8,128)(2,1)S(1)} %get-tuple-element.31), channel_id=1, replica_groups={{0,1,2,3},{4,5,6,7},{8,9,10,11},{12,13,14,15},{16,17,18,19},{20,21,22,2..., dimensions={0} | all-to-all | bytes 540672 | tf_op jit(solution)/shard_map/all_to_all | solution.py:256
  76.2 0.1 shard_map.64.mine
  76.2 7.7 %collective-permute-start.1 = (bf16[33,8,128]{2,1,0:T(8,128)(2,1)S(1)}, bf16[33,8,128]{2,1,0:T(8,128)(2,1)S(1)}, u32[]{:S(2)}, u32[]{:S(2)}) collective-permute-start(bf16[33,8,128]{2,1,0:T(8,128)(2,1)S(1)} %shard_map.64.mine), channel_id=1, source_target_pairs={{0,4},{1,5},{2,6},{3,7},{4,0},{5,1},{6,2},{7,3},{8,12},{9,13},{10,... | collective-permute-start | bytes 202760 | tf_op jit(solution)/shard_map/ppermute | solution.py:297
  83.9 6.1 %collective-permute-done.1.other = bf16[33,8,128]{2,1,0:T(8,128)(2,1)S(1)} collective-permute-done((bf16[33,8,128]{2,1,0:T(8,128)(2,1)S(1)}, bf16[33,8,128]{2,1,0:T(8,128)(2,1)S(1)}, u32[]{:S(2)}, u32[]{:S(2)}) %collective-permute-start.1) | collective-permute-done | bytes 67616 | tf_op jit(solution)/shard_map/ppermute | solution.py:297
  90.0 0.3 shard_map.65
  90.3 12.1 %all_to_all.45.arrived = bf16[8,5,8,128]{3,2,1,0:T(8,128)(2,1)S(1)} all-to-all(bf16[8,5,8,128]{3,2,1,0:T(8,128)(2,1)S(1)} %get-tuple-element.38), channel_id=1, replica_groups={{136,256,8,384,128,264,0,392},{152,272,24,400,144,280,16,408},{168,288,..., dimensions={0} | all-to-all | bytes 163840 | tf_op jit(solution)/shard_map/all_to_all | solution.py:256
  102.4 11.2 %all_to_all.46.arrived = bf16[8,5,8,128]{3,2,1,0:T(8,128)(2,1)S(1)} all-to-all(bf16[8,5,8,128]{3,2,1,0:T(8,128)(2,1)S(1)} %shard_map.66), channel_id=1, replica_groups={{48,112,0,96,16,80,32,64},{56,120,8,104,24,88,40,72},{176,240,128,224,1..., dimensions={0} | all-to-all | bytes 163840 | tf_op jit(solution)/shard_map/all_to_all | solution.py:256
  113.7 0.1 shard_map.67
  113.8 8.9 %all_to_all.47.arrived = bf16[8,4,8,128]{3,2,1,0:T(8,128)(2,1)S(1)} all-to-all(bf16[8,4,8,128]{3,2,1,0:T(8,128)(2,1)S(1)} %get-tuple-element.41), channel_id=1, replica_groups={{136,256,8,384,128,264,0,392},{152,272,24,400,144,280,16,408},{168,288,..., dimensions={0} | all-to-all | bytes 131072 | tf_op jit(solution)/shard_map/all_to_all | solution.py:256
  122.6 1.4 %shard_map.68 = (f32[64,64]{1,0:T(8,128)}, f32[64,512]{1,0:T(8,128)}, f32[64,512]{1,0:T(8,128)}) custom-call(f32[64,512]{1,0:T(8,128)S(1)} %get-tuple-element.24.base, f32[64,512]{1,0:T(8,128)S(1)} %get-tuple-element.30.resid, f32[1,128]{1,0:T(1,128)S(1)} %get-tuple-element.33.beta, f32[1,128]{1,0:T(1,128)S(1)} %get-tuple-element.34.alpha0, ...), custom_call_target="tpu_custom_call" | custom-call | tf_op jit(solution)/shard_map/pallas_call | solution.py:245
  (3 shorter events, 0.1 us)
Async XLA Ops:
  12.3 15.5 %copy-start = (f32[512]{0:T(512)S(1)}, f32[512]{0:T(512)}, u32[]{:S(2)}) copy-start(f32[512]{0:T(512)} %param.4) | copy-start | bytes 6148
  12.3 17.1 %collective-permute-start = (bf16[33,8,128]{2,1,0:T(8,128)(2,1)S(1)}, bf16[33,8,128]{2,1,0:T(8,128)(2,1)S(1)}, u32[]{:S(2)}, u32[]{:S(2)}) collective-permute-start(bf16[33,8,128]{2,1,0:T(8,128)(2,1)S(1)} %shard_map.59.mine), channel_id=1, source_target_pairs={{0,4},{1,5},{2,6},{3,7},{4,0},{5,1},{6,2},{7,3},{8,12},{9,13},{10,... | collective-permute-start | bytes 202760 | tf_op jit(solution)/shard_map/ppermute | solution.py:285
  76.2 13.8 %collective-permute-start.1 = (bf16[33,8,128]{2,1,0:T(8,128)(2,1)S(1)}, bf16[33,8,128]{2,1,0:T(8,128)(2,1)S(1)}, u32[]{:S(2)}, u32[]{:S(2)}) collective-permute-start(bf16[33,8,128]{2,1,0:T(8,128)(2,1)S(1)} %shard_map.64.mine), channel_id=1, source_target_pairs={{0,4},{1,5},{2,6},{3,7},{4,0},{5,1},{6,2},{7,3},{8,12},{9,13},{10,... | collective-permute-start | bytes 202760 | tf_op jit(solution)/shard_map/ppermute | solution.py:297

commit v12 on v11

--- a/solution.py
+++ b/solution.py
@@ -17,7 +17,7 @@
 X_GROUPS = [[h * COLUMNS + i for i in range(COLUMNS)] for h in range(HALVES)]
 SWAP = [(i, (i + COLUMNS) % (HALVES * COLUMNS)) for i in range(HALVES * COLUMNS)]
 FAR_ORDER = (3, 7, 0, 6, 1, 5, 2, 4)
-NEAR_ORDER = ((1, 1), (2, 0), (0, 1), (3, 0), (1, 0), (2, 1), (0, 0), (3, 1))
+NEAR_ORDER = ((2, 0), (1, 1), (3, 0), (0, 1), (2, 1), (1, 0), (3, 1), (0, 0))
 NEAR_GROUPS = [[(y * LAYERS + z) * CORES + c for y, c in NEAR_ORDER] for z in range(LAYERS)]
 FAR_GROUPS = [
     [(y * LAYERS + z) * CORES + c for z in FAR_ORDER] for y in range(PLANES) for c in range(CORES)

time: 124 us -> 125 us (level)
  waiting for transfers between devices: 7.7 us -> 10.1 us
  blocking collectives: 88.5 us -> 87.2 us
    ppermute x2, waiting for transfers between devices: 7.7 us -> 10.1 us  [per_device(): other = lax.ppermute(mine, 'feat', SWAP)]
where the time goes in v12:
time: 125 us
  blocking collectives  87.2 us (70%)
  starting transfers between devices  22.7 us (18%)
  waiting for transfers between devices  10.1 us (8%)
  Pallas kernels  3.93 us (3%)
    all_to_all x8, blocking collectives, exchanged(): lax.all_to_all(pieces, axis, 0, 0, tiled=True, axis_index_groups=groups)  87.2 us
    ppermute x2, starting transfers between devices, per_device(): other = lax.ppermute(mine, 'feat', SWAP)  22.7 us
    ppermute x2, waiting for transfers between devices, per_device(): other = lax.ppermute(mine, 'feat', SWAP)  10.1 us
    pallas_call x11, Pallas kernels, call(): pl.pallas_call(kernel, out_shape=[jax.ShapeDtypeStruct(s, t) for s, t in...  3.93 us
  transfers between devices with their start and end apart: 2, of which 2 were waited for; matrix products, arithmetic and copies ran while one was open for 0% of the time, Pallas kernels for 0%

profile of v12, /device:TPU:1, one launch (start us, length us, event | category | flops | bytes accessed | tf_op | source)
XLA Modules:
  0.0 124.7 jit_solution(11191437498944455397)
XLA Ops:
  0.6 1.4 %shard_map.58 = (bf16[4,33,8,128]{3,2,1,0:T(8,128)(2,1)S(1)}, bf16[512,512]{1,0:T(8,128)(2,1)S(1)}, f32[64,512]{1,0:T(8,128)S(1)}) custom-call(bf16[512,512]{1,0:T(8,128)(2,1)} %grads.1, f32[64,512]{1,0:T(8,128)} %bitcast.6), custom_call_target="tpu_custom_call" | custom-call | tf_op jit(solution)/shard_map/pallas_call | solution.py:245
  2.1 10.2 %all_to_all.40.arrived = bf16[4,33,8,128]{3,2,1,0:T(8,128)(2,1)S(1)} all-to-all(bf16[4,33,8,128]{3,2,1,0:T(8,128)(2,1)S(1)} %get-tuple-element.26), channel_id=1, replica_groups={{0,1,2,3},{4,5,6,7},{8,9,10,11},{12,13,14,15},{16,17,18,19},{20,21,22,2..., dimensions={0} | all-to-all | bytes 540672 | tf_op jit(solution)/shard_map/all_to_all | solution.py:256
  12.3 0.0 copy-start
  12.3 0.1 shard_map.59.mine
  12.3 15.5 %collective-permute-start = (bf16[33,8,128]{2,1,0:T(8,128)(2,1)S(1)}, bf16[33,8,128]{2,1,0:T(8,128)(2,1)S(1)}, u32[]{:S(2)}, u32[]{:S(2)}) collective-permute-start(bf16[33,8,128]{2,1,0:T(8,128)(2,1)S(1)} %shard_map.59.mine), channel_id=1, source_target_pairs={{0,4},{1,5},{2,6},{3,7},{4,0},{5,1},{6,2},{7,3},{8,12},{9,13},{10,... | collective-permute-start | bytes 202760 | tf_op jit(solution)/shard_map/ppermute | solution.py:285
  27.8 0.0 copy-done
  27.8 1.6 %collective-permute-done.other = bf16[33,8,128]{2,1,0:T(8,128)(2,1)S(1)} collective-permute-done((bf16[33,8,128]{2,1,0:T(8,128)(2,1)S(1)}, bf16[33,8,128]{2,1,0:T(8,128)(2,1)S(1)}, u32[]{:S(2)}, u32[]{:S(2)}) %collective-permute-start) | collective-permute-done | bytes 67616 | tf_op jit(solution)/shard_map/ppermute | solution.py:285
  29.4 0.2 shard_map.60
  29.7 11.4 %all_to_all.41.arrived = bf16[8,5,8,128]{3,2,1,0:T(8,128)(2,1)S(1)} all-to-all(bf16[8,5,8,128]{3,2,1,0:T(8,128)(2,1)S(1)} %get-tuple-element.28), channel_id=1, replica_groups={{256,136,384,8,264,128,392,0},{272,152,400,24,280,144,408,16},{288,168,..., dimensions={0} | all-to-all | bytes 163840 | tf_op jit(solution)/shard_map/all_to_all | solution.py:256
  41.0 16.8 %all_to_all.42.arrived = bf16[8,5,8,128]{3,2,1,0:T(8,128)(2,1)S(1)} all-to-all(bf16[8,5,8,128]{3,2,1,0:T(8,128)(2,1)S(1)} %shard_map.61), channel_id=1, replica_groups={{48,112,0,96,16,80,32,64},{56,120,8,104,24,88,40,72},{176,240,128,224,1..., dimensions={0} | all-to-all | bytes 163840 | tf_op jit(solution)/shard_map/all_to_all | solution.py:256
  57.9 0.1 shard_map.62
  58.0 9.5 %all_to_all.43.arrived = bf16[8,4,8,128]{3,2,1,0:T(8,128)(2,1)S(1)} all-to-all(bf16[8,4,8,128]{3,2,1,0:T(8,128)(2,1)S(1)} %get-tuple-element.29), channel_id=1, replica_groups={{256,136,384,8,264,128,392,0},{272,152,400,24,280,144,408,16},{288,168,..., dimensions={0} | all-to-all | bytes 131072 | tf_op jit(solution)/shard_map/all_to_all | solution.py:256
  67.5 0.3 shard_map.63
  67.8 8.9 %all_to_all.44.arrived = bf16[4,33,8,128]{3,2,1,0:T(8,128)(2,1)S(1)} all-to-all(bf16[4,33,8,128]{3,2,1,0:T(8,128)(2,1)S(1)} %get-tuple-element.31), channel_id=1, replica_groups={{0,1,2,3},{4,5,6,7},{8,9,10,11},{12,13,14,15},{16,17,18,19},{20,21,22,2..., dimensions={0} | all-to-all | bytes 540672 | tf_op jit(solution)/shard_map/all_to_all | solution.py:256
  76.6 0.1 shard_map.64.mine
  76.7 7.3 %collective-permute-start.1 = (bf16[33,8,128]{2,1,0:T(8,128)(2,1)S(1)}, bf16[33,8,128]{2,1,0:T(8,128)(2,1)S(1)}, u32[]{:S(2)}, u32[]{:S(2)}) collective-permute-start(bf16[33,8,128]{2,1,0:T(8,128)(2,1)S(1)} %shard_map.64.mine), channel_id=1, source_target_pairs={{0,4},{1,5},{2,6},{3,7},{4,0},{5,1},{6,2},{7,3},{8,12},{9,13},{10,... | collective-permute-start | bytes 202760 | tf_op jit(solution)/shard_map/ppermute | solution.py:297
  84.0 8.4 %collective-permute-done.1.other = bf16[33,8,128]{2,1,0:T(8,128)(2,1)S(1)} collective-permute-done((bf16[33,8,128]{2,1,0:T(8,128)(2,1)S(1)}, bf16[33,8,128]{2,1,0:T(8,128)(2,1)S(1)}, u32[]{:S(2)}, u32[]{:S(2)}) %collective-permute-start.1) | collective-permute-done | bytes 67616 | tf_op jit(solution)/shard_map/ppermute | solution.py:297
  92.4 0.3 shard_map.65
  92.7 9.7 %all_to_all.45.arrived = bf16[8,5,8,128]{3,2,1,0:T(8,128)(2,1)S(1)} all-to-all(bf16[8,5,8,128]{3,2,1,0:T(8,128)(2,1)S(1)} %get-tuple-element.38), channel_id=1, replica_groups={{256,136,384,8,264,128,392,0},{272,152,400,24,280,144,408,16},{288,168,..., dimensions={0} | all-to-all | bytes 163840 | tf_op jit(solution)/shard_map/all_to_all | solution.py:256
  102.5 11.2 %all_to_all.46.arrived = bf16[8,5,8,128]{3,2,1,0:T(8,128)(2,1)S(1)} all-to-all(bf16[8,5,8,128]{3,2,1,0:T(8,128)(2,1)S(1)} %shard_map.66), channel_id=1, replica_groups={{48,112,0,96,16,80,32,64},{56,120,8,104,24,88,40,72},{176,240,128,224,1..., dimensions={0} | all-to-all | bytes 163840 | tf_op jit(solution)/shard_map/all_to_all | solution.py:256
  113.7 0.1 shard_map.67
  113.8 9.5 %all_to_all.47.arrived = bf16[8,4,8,128]{3,2,1,0:T(8,128)(2,1)S(1)} all-to-all(bf16[8,4,8,128]{3,2,1,0:T(8,128)(2,1)S(1)} %get-tuple-element.41), channel_id=1, replica_groups={{256,136,384,8,264,128,392,0},{272,152,400,24,280,144,408,16},{288,168,..., dimensions={0} | all-to-all | bytes 131072 | tf_op jit(solution)/shard_map/all_to_all | solution.py:256
  123.4 1.4 %shard_map.68 = (f32[64,64]{1,0:T(8,128)}, f32[64,512]{1,0:T(8,128)}, f32[64,512]{1,0:T(8,128)}) custom-call(f32[64,512]{1,0:T(8,128)S(1)} %get-tuple-element.24.base, f32[64,512]{1,0:T(8,128)S(1)} %get-tuple-element.30.resid, f32[1,128]{1,0:T(1,128)S(1)} %get-tuple-element.33.beta, f32[1,128]{1,0:T(1,128)S(1)} %get-tuple-element.34.alpha0, ...), custom_call_target="tpu_custom_call" | custom-call | tf_op jit(solution)/shard_map/pallas_call | solution.py:245
  (3 shorter events, 0.1 us)
Async XLA Ops:
  12.3 15.5 %copy-start = (f32[512]{0:T(512)S(1)}, f32[512]{0:T(512)}, u32[]{:S(2)}) copy-start(f32[512]{0:T(512)} %param.4) | copy-start | bytes 6148
  12.3 17.1 %collective-permute-start = (bf16[33,8,128]{2,1,0:T(8,128)(2,1)S(1)}, bf16[33,8,128]{2,1,0:T(8,128)(2,1)S(1)}, u32[]{:S(2)}, u32[]{:S(2)}) collective-permute-start(bf16[33,8,128]{2,1,0:T(8,128)(2,1)S(1)} %shard_map.59.mine), channel_id=1, source_target_pairs={{0,4},{1,5},{2,6},{3,7},{4,0},{5,1},{6,2},{7,3},{8,12},{9,13},{10,... | collective-permute-start | bytes 202760 | tf_op jit(solution)/shard_map/ppermute | solution.py:285
  76.7 15.8 %collective-permute-start.1 = (bf16[33,8,128]{2,1,0:T(8,128)(2,1)S(1)}, bf16[33,8,128]{2,1,0:T(8,128)(2,1)S(1)}, u32[]{:S(2)}, u32[]{:S(2)}) collective-permute-start(bf16[33,8,128]{2,1,0:T(8,128)(2,1)S(1)} %shard_map.64.mine), channel_id=1, source_target_pairs={{0,4},{1,5},{2,6},{3,7},{4,0},{5,1},{6,2},{7,3},{8,12},{9,13},{10,... | collective-permute-start | bytes 202760 | tf_op jit(solution)/shard_map/ppermute | solution.py:297

commit v13 on v12

--- a/solution.py
+++ b/solution.py
@@ -17,7 +17,7 @@
 X_GROUPS = [[h * COLUMNS + i for i in range(COLUMNS)] for h in range(HALVES)]
 SWAP = [(i, (i + COLUMNS) % (HALVES * COLUMNS)) for i in range(HALVES * COLUMNS)]
 FAR_ORDER = (3, 7, 0, 6, 1, 5, 2, 4)
-NEAR_ORDER = ((2, 0), (1, 1), (3, 0), (0, 1), (2, 1), (1, 0), (3, 1), (0, 0))
+NEAR_ORDER = ((1, 1), (2, 0), (1, 0), (2, 1), (0, 1), (3, 0), (0, 0), (3, 1))
 NEAR_GROUPS = [[(y * LAYERS + z) * CORES + c for y, c in NEAR_ORDER] for z in range(LAYERS)]
 FAR_GROUPS = [
     [(y * LAYERS + z) * CORES + c for z in FAR_ORDER] for y in range(PLANES) for c in range(CORES)

time: 125 us -> 125 us (level)
  waiting for transfers between devices: 10.1 us -> 7.7 us
  blocking collectives: 87.2 us -> 88.5 us
    ppermute x2, waiting for transfers between devices: 10.1 us -> 7.7 us  [per_device(): other = lax.ppermute(mine, 'feat', SWAP)]
    all_to_all x8, blocking collectives: 87.2 us -> 88.5 us  [exchanged(): lax.all_to_all(pieces, axis, 0, 0, tiled=True, axis_index_groups=groups)]
where the time goes in v13:
time: 125 us; the launch traced here: 124 us
  blocking collectives  88.5 us (71%)
  starting transfers between devices  23.2 us (19%)
  waiting for transfers between devices  7.7 us (6%)
  Pallas kernels  3.93 us (3%)
    all_to_all x8, blocking collectives, exchanged(): lax.all_to_all(pieces, axis, 0, 0, tiled=True, axis_index_groups=groups)  88.5 us
    ppermute x2, starting transfers between devices, per_device(): other = lax.ppermute(mine, 'feat', SWAP)  23.2 us
    ppermute x2, waiting for transfers between devices, per_device(): other = lax.ppermute(mine, 'feat', SWAP)  7.7 us
    pallas_call x11, Pallas kernels, call(): pl.pallas_call(kernel, out_shape=[jax.ShapeDtypeStruct(s, t) for s, t in...  3.93 us
  transfers between devices with their start and end apart: 2, of which 2 were waited for; matrix products, arithmetic and copies ran while one was open for 0% of the time, Pallas kernels for 0%

profile of v13, /device:TPU:1, one launch (start us, length us, event | category | flops | bytes accessed | tf_op | source)
XLA Modules:
  0.0 124.1 jit_solution(1662769054110954018)
XLA Ops:
  0.6 1.4 %shard_map.58 = (bf16[4,33,8,128]{3,2,1,0:T(8,128)(2,1)S(1)}, bf16[512,512]{1,0:T(8,128)(2,1)S(1)}, f32[64,512]{1,0:T(8,128)S(1)}) custom-call(bf16[512,512]{1,0:T(8,128)(2,1)} %grads.1, f32[64,512]{1,0:T(8,128)} %bitcast.6), custom_call_target="tpu_custom_call" | custom-call | tf_op jit(solution)/shard_map/pallas_call | solution.py:245
  2.1 10.2 %all_to_all.40.arrived = bf16[4,33,8,128]{3,2,1,0:T(8,128)(2,1)S(1)} all-to-all(bf16[4,33,8,128]{3,2,1,0:T(8,128)(2,1)S(1)} %get-tuple-element.26), channel_id=1, replica_groups={{0,1,2,3},{4,5,6,7},{8,9,10,11},{12,13,14,15},{16,17,18,19},{20,21,22,2..., dimensions={0} | all-to-all | bytes 540672 | tf_op jit(solution)/shard_map/all_to_all | solution.py:256
  12.3 0.0 copy-start
  12.3 0.1 shard_map.59.mine
  12.3 15.5 %collective-permute-start = (bf16[33,8,128]{2,1,0:T(8,128)(2,1)S(1)}, bf16[33,8,128]{2,1,0:T(8,128)(2,1)S(1)}, u32[]{:S(2)}, u32[]{:S(2)}) collective-permute-start(bf16[33,8,128]{2,1,0:T(8,128)(2,1)S(1)} %shard_map.59.mine), channel_id=1, source_target_pairs={{0,4},{1,5},{2,6},{3,7},{4,0},{5,1},{6,2},{7,3},{8,12},{9,13},{10,... | collective-permute-start | bytes 202760 | tf_op jit(solution)/shard_map/ppermute | solution.py:285
  27.8 0.0 copy-done
  27.8 1.6 %collective-permute-done.other = bf16[33,8,128]{2,1,0:T(8,128)(2,1)S(1)} collective-permute-done((bf16[33,8,128]{2,1,0:T(8,128)(2,1)S(1)}, bf16[33,8,128]{2,1,0:T(8,128)(2,1)S(1)}, u32[]{:S(2)}, u32[]{:S(2)}) %collective-permute-start) | collective-permute-done | bytes 67616 | tf_op jit(solution)/shard_map/ppermute | solution.py:285
  29.4 0.2 shard_map.60
  29.7 12.3 %all_to_all.41.arrived = bf16[8,5,8,128]{3,2,1,0:T(8,128)(2,1)S(1)} all-to-all(bf16[8,5,8,128]{3,2,1,0:T(8,128)(2,1)S(1)} %get-tuple-element.28), channel_id=1, replica_groups={{136,256,128,264,8,384,0,392},{152,272,144,280,24,400,16,408},{168,288,..., dimensions={0} | all-to-all | bytes 163840 | tf_op jit(solution)/shard_map/all_to_all | solution.py:256
  42.0 16.8 %all_to_all.42.arrived = bf16[8,5,8,128]{3,2,1,0:T(8,128)(2,1)S(1)} all-to-all(bf16[8,5,8,128]{3,2,1,0:T(8,128)(2,1)S(1)} %shard_map.61), channel_id=1, replica_groups={{48,112,0,96,16,80,32,64},{56,120,8,104,24,88,40,72},{176,240,128,224,1..., dimensions={0} | all-to-all | bytes 163840 | tf_op jit(solution)/shard_map/all_to_all | solution.py:256
  58.8 0.1 shard_map.62
  58.9 8.8 %all_to_all.43.arrived = bf16[8,4,8,128]{3,2,1,0:T(8,128)(2,1)S(1)} all-to-all(bf16[8,4,8,128]{3,2,1,0:T(8,128)(2,1)S(1)} %get-tuple-element.29), channel_id=1, replica_groups={{136,256,128,264,8,384,0,392},{152,272,144,280,24,400,16,408},{168,288,..., dimensions={0} | all-to-all | bytes 131072 | tf_op jit(solution)/shard_map/all_to_all | solution.py:256
  67.7 0.3 shard_map.63
  68.0 8.1 %all_to_all.44.arrived = bf16[4,33,8,128]{3,2,1,0:T(8,128)(2,1)S(1)} all-to-all(bf16[4,33,8,128]{3,2,1,0:T(8,128)(2,1)S(1)} %get-tuple-element.31), channel_id=1, replica_groups={{0,1,2,3},{4,5,6,7},{8,9,10,11},{12,13,14,15},{16,17,18,19},{20,21,22,2..., dimensions={0} | all-to-all | bytes 540672 | tf_op jit(solution)/shard_map/all_to_all | solution.py:256
  76.2 0.1 shard_map.64.mine
  76.2 7.7 %collective-permute-start.1 = (bf16[33,8,128]{2,1,0:T(8,128)(2,1)S(1)}, bf16[33,8,128]{2,1,0:T(8,128)(2,1)S(1)}, u32[]{:S(2)}, u32[]{:S(2)}) collective-permute-start(bf16[33,8,128]{2,1,0:T(8,128)(2,1)S(1)} %shard_map.64.mine), channel_id=1, source_target_pairs={{0,4},{1,5},{2,6},{3,7},{4,0},{5,1},{6,2},{7,3},{8,12},{9,13},{10,... | collective-permute-start | bytes 202760 | tf_op jit(solution)/shard_map/ppermute | solution.py:297
  83.9 6.1 %collective-permute-done.1.other = bf16[33,8,128]{2,1,0:T(8,128)(2,1)S(1)} collective-permute-done((bf16[33,8,128]{2,1,0:T(8,128)(2,1)S(1)}, bf16[33,8,128]{2,1,0:T(8,128)(2,1)S(1)}, u32[]{:S(2)}, u32[]{:S(2)}) %collective-permute-start.1) | collective-permute-done | bytes 67616 | tf_op jit(solution)/shard_map/ppermute | solution.py:297
  90.0 0.3 shard_map.65
  90.3 12.2 %all_to_all.45.arrived = bf16[8,5,8,128]{3,2,1,0:T(8,128)(2,1)S(1)} all-to-all(bf16[8,5,8,128]{3,2,1,0:T(8,128)(2,1)S(1)} %get-tuple-element.38), channel_id=1, replica_groups={{136,256,128,264,8,384,0,392},{152,272,144,280,24,400,16,408},{168,288,..., dimensions={0} | all-to-all | bytes 163840 | tf_op jit(solution)/shard_map/all_to_all | solution.py:256
  102.5 11.2 %all_to_all.46.arrived = bf16[8,5,8,128]{3,2,1,0:T(8,128)(2,1)S(1)} all-to-all(bf16[8,5,8,128]{3,2,1,0:T(8,128)(2,1)S(1)} %shard_map.66), channel_id=1, replica_groups={{48,112,0,96,16,80,32,64},{56,120,8,104,24,88,40,72},{176,240,128,224,1..., dimensions={0} | all-to-all | bytes 163840 | tf_op jit(solution)/shard_map/all_to_all | solution.py:256
  113.7 0.1 shard_map.67
  113.8 8.9 %all_to_all.47.arrived = bf16[8,4,8,128]{3,2,1,0:T(8,128)(2,1)S(1)} all-to-all(bf16[8,4,8,128]{3,2,1,0:T(8,128)(2,1)S(1)} %get-tuple-element.41), channel_id=1, replica_groups={{136,256,128,264,8,384,0,392},{152,272,144,280,24,400,16,408},{168,288,..., dimensions={0} | all-to-all | bytes 131072 | tf_op jit(solution)/shard_map/all_to_all | solution.py:256
  122.7 1.4 %shard_map.68 = (f32[64,64]{1,0:T(8,128)}, f32[64,512]{1,0:T(8,128)}, f32[64,512]{1,0:T(8,128)}) custom-call(f32[64,512]{1,0:T(8,128)S(1)} %get-tuple-element.24.base, f32[64,512]{1,0:T(8,128)S(1)} %get-tuple-element.30.resid, f32[1,128]{1,0:T(1,128)S(1)} %get-tuple-element.33.beta, f32[1,128]{1,0:T(1,128)S(1)} %get-tuple-element.34.alpha0, ...), custom_call_target="tpu_custom_call" | custom-call | tf_op jit(solution)/shard_map/pallas_call | solution.py:245
  (3 shorter events, 0.1 us)
Async XLA Ops:
  12.3 15.5 %copy-start = (f32[512]{0:T(512)S(1)}, f32[512]{0:T(512)}, u32[]{:S(2)}) copy-start(f32[512]{0:T(512)} %param.4) | copy-start | bytes 6148
  12.3 17.1 %collective-permute-start = (bf16[33,8,128]{2,1,0:T(8,128)(2,1)S(1)}, bf16[33,8,128]{2,1,0:T(8,128)(2,1)S(1)}, u32[]{:S(2)}, u32[]{:S(2)}) collective-permute-start(bf16[33,8,128]{2,1,0:T(8,128)(2,1)S(1)} %shard_map.59.mine), channel_id=1, source_target_pairs={{0,4},{1,5},{2,6},{3,7},{4,0},{5,1},{6,2},{7,3},{8,12},{9,13},{10,... | collective-permute-start | bytes 202760 | tf_op jit(solution)/shard_map/ppermute | solution.py:285
  76.2 13.8 %collective-permute-start.1 = (bf16[33,8,128]{2,1,0:T(8,128)(2,1)S(1)}, bf16[33,8,128]{2,1,0:T(8,128)(2,1)S(1)}, u32[]{:S(2)}, u32[]{:S(2)}) collective-permute-start(bf16[33,8,128]{2,1,0:T(8,128)(2,1)S(1)} %shard_map.64.mine), channel_id=1, source_target_pairs={{0,4},{1,5},{2,6},{3,7},{4,0},{5,1},{6,2},{7,3},{8,12},{9,13},{10,... | collective-permute-start | bytes 202760 | tf_op jit(solution)/shard_map/ppermute | solution.py:297
